TPU v7x, 32 devices: a whole 2x2x4 slice. The times are simulated.
32 devices in a mesh: ctx: 8 (over z, x), fsdp: 4 (over y, core).
Axes of the slice: x: 2, y: 2, z: 4, core: 2. Of those that a mesh axis runs over, the one named last changes fastest.
Arguments:
- layer_in: bfloat16 [4, 1024, 4096], P('fsdp', 'ctx'), may hold values from -6 to 6
- w_bc: bfloat16 [4096, 256], P('fsdp'), may hold values from -0.09375 to 0.09375
- conv_w: float32 [4, 256], replicated, may hold values from -3 to 3
- conv_b: float32 [256], replicated, may hold values from -0.5 to 0.5
- ssm_in: bfloat16 [4, 1024, 4096], P('fsdp', 'ctx'), may hold values from -6 to 6
- dt_raw: float32 [4, 1024, 32], P('fsdp', 'ctx'), may hold values from -4 to 4
- dt_bias: float32 [32], replicated, as said below
- a_log: float32 [32], replicated, as said below
- skip_scale: float32 [32], replicated, may hold values from 0.5 to 1.5
- grad_out: bfloat16 [4, 1024, 4096], P('fsdp', 'ctx'), may hold values from -6 to 6
Outputs:
- ssm_out: bfloat16 [4, 1024, 4096], P('fsdp', 'ctx')
- grad_ssm_in: bfloat16 [4, 1024, 4096], P('fsdp', 'ctx')
- grad_layer_in: bfloat16 [4, 1024, 4096], P('fsdp', 'ctx')
- grad_dt_raw: float32 [4, 1024, 32], P('fsdp', 'ctx')
- grad_w_bc: float32 [4096, 256], P('fsdp')
- grad_conv_w: float32 [4, 256], replicated
- grad_conv_b: float32 [256], replicated
- grad_dt_bias: float32 [32], replicated
- grad_a_log: float32 [32], replicated
- grad_skip: float32 [32], replicated
Inputs may be any that keep to these rules, and one draw needn't show every extreme that they name: `dt_bias`: drawn together with a_log. `a_log`: drawn together with dt_bias.
All inputs are finite; a program needn't handle non-finite values.
Results may differ from a plain program's by a relative error of at most 0.039.
Values may be sent and summed in bfloat16 or wider, within the bound.
No kernel may reach another device: no remote copies, remote signals or barrier semaphores. Data moves between devices by JAX's collectives and lax.ppermute only.
A program may use at most 320 MiB of HBM per device.

v0:
```python
import functools

import jax
import jax.numpy as jnp
from jax import lax
from jax.experimental import pallas as pl
from jax.experimental.pallas import tpu as pltpu
from jax.sharding import PartitionSpec as P

F32 = jnp.float32
BF16 = jnp.bfloat16
LANES = 128
HALO = 16
PARTS = (2, 2)
GROUPS = len(PARTS)
LIMIT = 16 * 1024 * 1024
HIGHEST = lax.Precision.HIGHEST
TN = ((0,), (0,))
NT = ((1,), (1,))


def dot(a, b, dims=((1,), (0,)), precision=None):
    return lax.dot_general(
        a, b, (dims, ((), ())), precision=precision, preferred_element_type=F32
    )


def shape(dims, dtype):
    return jax.ShapeDtypeStruct(dims, dtype)


def call(kernel, name, out_shape, smem, *operands, hbm=(), hbm_outs=0, scratch=(), aliases=None):
    single = not isinstance(out_shape, list)
    outs = [out_shape] if single else out_shape
    spaces = [pltpu.SMEM] * len(smem) + [pl.ANY] * len(hbm) + [pltpu.VMEM] * len(operands)
    out_spaces = [pltpu.HBM] * hbm_outs + [pltpu.VMEM] * (len(outs) - hbm_outs)
    result = pl.pallas_call(
        kernel,
        out_shape=outs,
        in_specs=[pl.BlockSpec(memory_space=a) for a in spaces],
        out_specs=[pl.BlockSpec(memory_space=a) for a in out_spaces],
        scratch_shapes=list(scratch),
        compiler_params=pltpu.CompilerParams(vmem_limit_bytes=LIMIT),
        input_output_aliases=aliases or {},
        name=name,
    )(*smem, *hbm, *operands)
    return result[0] if single else result


def copy_all(pairs, sems):
    copies = [pltpu.make_async_copy(a, b, sems.at[i]) for i, (a, b) in enumerate(pairs)]
    for copy in copies:
        copy.start()
    return copies


def side():
    return lax.rem(lax.axis_index("ctx"), 2)


def place():
    return lax.div(lax.axis_index("ctx"), 2)


def peer_columns(k, rows):
    return aligned((lax.axis_index("fsdp") ^ k) * rows, rows)


def aligned(at, size):
    return pl.ds(pl.multiple_of(at, LANES), size)


def triangle(n):
    rows = lax.broadcasted_iota(jnp.int32, (n, n), 0)
    cols = lax.broadcasted_iota(jnp.int32, (n, n), 1)
    return rows >= cols


def split(value):
    high = value.astype(BF16).astype(F32)
    return jnp.concatenate([high, value - high], 0).astype(BF16)


def tail_kernel(layer_ref, out_ref, sems):
    tokens = layer_ref.shape[0]
    for copy in copy_all([(layer_ref.at[tokens - HALO : tokens, :], out_ref)], sems):
        copy.wait()


def swap_kernel(x_ref, g_ref, out_ref, sems):
    width = out_ref.shape[1] // 2
    other = aligned((1 - side()) * width, width)
    pairs = [
        (x_ref.at[:, other], out_ref.at[:, :width]),
        (g_ref.at[:, other], out_ref.at[:, width:]),
    ]
    for copy in copy_all(pairs, sems):
        copy.wait()


def vectors_kernel(
    dt_ref, back_ref, bias_ref, alog_ref, step_ref, cum_ref, cumt_ref, grow_ref, endw_ref, sig_ref,
    rate_ref, turned, rows,
):
    n = back_ref.shape[1]
    heads = back_ref.shape[0] // 2
    r = side()
    mine = pl.ds(pl.multiple_of(r * heads, 8), heads)
    turned[...] = jnp.zeros_like(turned)
    turned[0:heads, :] = dt_ref[mine, :]
    turned[heads : 2 * heads, :] = back_ref[mine, :]
    rows[...] = jnp.zeros_like(rows)
    for i, ref in enumerate((bias_ref, alog_ref)):
        half = jnp.where(r == 0, ref[:, :heads], ref[:, heads:])
        rows[i : i + 1, 0:heads] = half
        rows[i : i + 1, heads : 2 * heads] = half
    raw = turned[...].T + rows[0:1, :]
    step = jnp.maximum(raw, 0.0) + jnp.log1p(jnp.exp(-jnp.abs(raw)))
    rate = jnp.exp(rows[1:2, :])
    log_decay = -step * rate
    lower = jnp.where(triangle(n), 1.0, 0.0).astype(F32)
    cum = dot(lower, log_decay, precision=HIGHEST)
    step_ref[...] = step
    cum_ref[...] = cum
    cumt_ref[...] = cum.T
    grow_ref[...] = jnp.exp(cum)
    endw_ref[...] = jnp.exp(cum[n - 1 : n, :] - cum)
    sig_ref[...] = jax.nn.sigmoid(raw)
    rate_ref[...] = jnp.broadcast_to(rate, rate_ref.shape)


def early_kernel(count, layer_ref, *refs):
    pieces = refs[:count]
    out_ref, layer_scr, w_scr, sems = refs[count:]
    copies = copy_all(
        [(layer_ref, layer_scr)] + [(pieces[k], w_scr.at[k]) for k in range(count)], sems
    )
    copies[0].wait()
    total = 0.0
    for k in range(count):
        copies[k + 1].wait()
        total += dot(layer_scr[:, peer_columns(k, w_scr.shape[1])], w_scr[k])
    out_ref[...] = total


def project_kernel(done, count, layer_ref, *refs):
    pieces = refs[:count]
    halo_ref, early_ref, cw_ref, cb_ref, kept_ref, bc_ref, layer_scr, w_scr, ext_scr, sems = refs[count:]
    copies = copy_all(
        [(layer_ref, layer_scr)] + [(pieces[k], w_scr.at[k]) for k in range(count)], sems
    )
    taps = cw_ref.shape[0]
    tokens = layer_ref.shape[0]
    copies[0].wait()
    total, rim = early_ref[...], 0.0
    for k in range(count):
        copies[k + 1].wait()
        at = peer_columns(k, w_scr.shape[1])
        rim += dot(halo_ref[:, at], w_scr[k])
        if k >= done:
            total += dot(layer_scr[:, at], w_scr[k])
    ext_scr[0:HALO, :] = rim
    ext_scr[HALO:, :] = total
    kept_ref[0 : HALO + tokens, :] = ext_scr[...]
    first = HALO - taps + 1
    pre = cb_ref[...] + cw_ref[0:1, :] * ext_scr[first : first + tokens, :]
    for k in range(1, taps):
        pre = pre + cw_ref[k : k + 1, :] * ext_scr[first + k : first + k + tokens, :]
    kept_ref[HALO + tokens :, :] = pre
    bc_ref[...] = (pre * jax.nn.sigmoid(pre)).astype(BF16)


def head_columns(at, h):
    first, more = at
    return aligned(first + side() * more + h * LANES, LANES)


def scale_kernel(heads, lane, x_at, g_at, x_ref, g_ref, step_ref, grow_ref, endw_ref, xe_ref, ge_ref):
    for h in range(heads):
        at = slice(h * LANES, (h + 1) * LANES)
        one = slice(lane + h, lane + h + 1)
        x = x_ref[:, head_columns(x_at, h)].astype(F32)
        g = g_ref[:, head_columns(g_at, h)].astype(F32)
        xe_ref[:, at] = (x * (step_ref[:, one] * endw_ref[:, one])).astype(BF16)
        ge_ref[:, at] = (g * grow_ref[:, one]).astype(BF16)


def widen(row, lane, heads):
    return jnp.concatenate(
        [jnp.broadcast_to(row[:, lane + h : lane + h + 1], (1, LANES)) for h in range(heads)], 1
    )


def states_kernel(
    heads, lanes, bc0_ref, bc1_ref, xe0_ref, ge0_ref, xe1_ref, ge1_ref, grow_ref,
    first_ref, p_ref, q_ref, sf_ref, ds_ref, dec_ref, s_scr, d_scr, dec_scr,
):
    n = grow_ref.shape[0]
    r = side()
    for slot, (bc_ref, xe_ref, ge_ref) in enumerate(
        ((bc0_ref, xe0_ref, ge0_ref), (bc1_ref, xe1_ref, ge1_ref))
    ):
        s_scr[slot] = dot(bc_ref[:, :LANES], xe_ref[...], TN)
        d_scr[slot] = dot(bc_ref[:, LANES:], ge_ref[...], TN)
        dec_scr[slot] = widen(grow_ref[n - 1 : n, :], lanes[slot], heads)
    dec_first, dec_second = dec_scr[r], dec_scr[1 - r]
    s_first, d_second = s_scr[r], d_scr[1 - r]
    sf_ref[...] = s_first.astype(BF16)
    ds_ref[...] = d_second.astype(BF16)
    p = (dec_second * s_first + s_scr[1 - r]).astype(BF16)
    q = (dec_first * d_second + d_scr[r]).astype(BF16)
    p_ref[...] = p
    q_ref[...] = q

    @pl.when(place() == 0)
    def _():
        first_ref[...] = p

    @pl.when(place() != 0)
    def _():
        first_ref[...] = q

    dec_ref[0:1, :] = dec_first * dec_second
    dec_ref[1:2, :] = dec_first
    dec_ref[2:3, :] = dec_second
    dec_ref[3:8, :] = jnp.zeros((5, dec_first.shape[1]), F32)


def hop_kernel(hop, received_ref, p_ref, q_ref, dec_ref, out_ref):
    carried = dec_ref[0:1, :] * received_ref[...].astype(F32)

    @pl.when(place() == hop)
    def _():
        out_ref[...] = (carried + p_ref[...].astype(F32)).astype(BF16)

    @pl.when(place() != hop)
    def _():
        out_ref[...] = (carried + q_ref[...].astype(F32)).astype(BF16)


def inside_kernel(
    heads, lane, skip_at, all_heads, x_at, g_at, skip_ref, x_ref, g_ref, bc_ref, step_ref, cum_ref,
    cumt_ref, y_ref, dx_ref, dscores_ref, gy_ref, ds_ref, gx_ref,
):
    n = step_ref.shape[0]
    mask = triangle(n)
    scores = jnp.where(mask, dot(bc_ref[:, LANES:], bc_ref[:, :LANES], NT), 0.0)
    gy_ref[...] = jnp.zeros_like(gy_ref)
    ds_ref[...] = jnp.zeros_like(ds_ref)
    gx_ref[...] = jnp.zeros_like(gx_ref)
    dscores = jnp.zeros((n, n), F32)
    for h in range(heads):
        at = slice(h * LANES, (h + 1) * LANES)
        one = slice(lane + h, lane + h + 1)
        step = step_ref[:, one]
        gap = cum_ref[:, one] - cumt_ref[one, :]
        decay = jnp.exp(jnp.where(mask, gap, 0.0))
        mixing = (scores * decay).astype(BF16)
        x = x_ref[:, head_columns(x_at, h)].astype(F32)
        g = g_ref[:, head_columns(g_at, h)]
        gf = g.astype(F32)
        xs = (x * step).astype(BF16)
        skip = skip_ref[side() * all_heads + skip_at + h]
        y = dot(mixing, xs)
        dxs = dot(mixing, g, TN)
        dscores += dot(g, xs, NT) * decay
        y_ref[:, at] = y + skip * x
        dx_ref[:, at] = dxs * step + skip * gf
        gy_ref[:, one] = jnp.sum(gf * y, axis=1, keepdims=True)
        ds_ref[:, one] = jnp.sum(x * dxs, axis=1, keepdims=True)
        gx_ref[0:1, one] = jnp.sum(jnp.sum(gf * x, axis=0, keepdims=True), axis=1, keepdims=True)
    dscores_ref[...] = jnp.where(mask, dscores, 0.0)


def inside_bc_kernel(bc0_ref, bc1_ref, *refs):
    parts, outs = refs[: 2 * GROUPS], refs[2 * GROUPS :]
    for slot, bc_ref in enumerate((bc0_ref, bc1_ref)):
        total = parts[slot * GROUPS][...]
        for i in range(1, GROUPS):
            total = total + parts[slot * GROUPS + i][...]
        ds = total.astype(BF16)
        outs[slot][:, :LANES] = dot(ds, bc_ref[:, LANES:], TN)
        outs[slot][:, LANES:] = dot(ds, bc_ref[:, :LANES])


def across_kernel(heads, lanes, hops, filled, own_at, columns, *refs):
    refs = refs[2 * filled :]
    across_block(heads, lanes, hops, own_at, columns, *refs)


def across_block(
    heads, lanes, hops, own_at, columns, x0_ref, g0_ref, x1_ref, g1_ref, bc0_ref, bc1_ref, xe0_ref,
    ge0_ref, xe1_ref, ge1_ref, step_ref, grow_ref, endw_ref, dec_ref, p_ref, sf_ref, ds_ref,
    y0_ref, dx0_ref, y1_ref, dx1_ref, dbc0_ref, dbc1_ref, *refs
):
    received = refs[:hops]
    (
        yf_ref, dxf_ref, ys_ref, dxs_ref, dbco0_ref, dbco1_ref, u_ref, t_ref, re_ref,
        e_in, r_in, e_scr, r_scr, n_scr, yo_ref, dxo_ref, sems,
    ) = refs[hops:]
    r, pos = side(), place()
    width = yo_ref.shape[1]
    e_in[...] = jnp.zeros_like(e_in)
    r_in[...] = jnp.zeros_like(r_in)
    for k in range(hops):

        @pl.when(pos - 1 == k)
        def _(k=k):
            e_in[...] = received[k][...]

        @pl.when(hops - 1 - pos == k)
        def _(k=k):
            r_in[...] = received[k][...]

    dec_pair, dec_first, dec_second = dec_ref[0:1, :], dec_ref[1:2, :], dec_ref[2:3, :]
    entering = e_in[...].astype(F32)
    later = r_in[...].astype(F32)
    middle = dec_first * entering + sf_ref[...].astype(F32)
    leaving = dec_pair * entering + p_ref[...].astype(F32)
    earlier = dec_second * later + ds_ref[...].astype(F32)
    e_scr[r] = e_in[...]
    e_scr[1 - r] = middle.astype(BF16)
    r_scr[1 - r] = r_in[...]
    r_scr[r] = earlier.astype(BF16)
    n_scr[1 - r] = jnp.sum(later * leaving, axis=0, keepdims=True)
    n_scr[r] = jnp.sum(earlier * middle, axis=0, keepdims=True)

    u_ref[...] = jnp.zeros_like(u_ref)
    t_ref[...] = jnp.zeros_like(t_ref)
    re_ref[...] = jnp.zeros_like(re_ref)
    for slot, (bc_ref, xe_ref, ge_ref, y_ref, dx_ref, dbc_ref, dbco_ref) in enumerate(
        (
            (bc0_ref, xe0_ref, ge0_ref, y0_ref, dx0_ref, dbc0_ref, dbco0_ref),
            (bc1_ref, xe1_ref, ge1_ref, y1_ref, dx1_ref, dbc1_ref, dbco1_ref),
        )
    ):
        e_all = e_scr[slot]
        r_all = r_scr[slot]
        db = dbc_ref[:, :LANES] + dot(xe_ref[...], r_all, NT)
        dc = dbc_ref[:, LANES:] + dot(ge_ref[...], e_all, NT)
        dbco_ref[:, :LANES] = db.astype(dbco_ref.dtype)
        dbco_ref[:, LANES:] = dc.astype(dbco_ref.dtype)
        ce_all = dot(bc_ref[:, LANES:], e_all)
        br_all = dot(bc_ref[:, :LANES], r_all)
        for h in range(heads):
            at = slice(h * LANES, (h + 1) * LANES)
            lane = lanes[slot] + h
            one = slice(lane, lane + 1)
            ce, br = ce_all[:, at], br_all[:, at]
            y = (y_ref[:, at] + grow_ref[:, one] * ce).astype(BF16)
            dx = (dx_ref[:, at] + (step_ref[:, one] * endw_ref[:, one]) * br).astype(BF16)
            if slot == 0:
                yo_ref[:, at] = y
                dxo_ref[:, at] = dx
                x = x0_ref[:, head_columns(own_at, h)].astype(F32)
                g = g0_ref[:, head_columns(own_at, h)].astype(F32)
            else:
                ys_ref[:, at] = y
                dxs_ref[:, at] = dx
                x = x1_ref[:, head_columns(columns[0], h)].astype(F32)
                g = g1_ref[:, head_columns(columns[1], h)].astype(F32)
            u_ref[:, one] = jnp.sum(g * ce, axis=1, keepdims=True)
            t_ref[:, one] = jnp.sum(x * br, axis=1, keepdims=True)
            re_ref[0:1, one] = jnp.sum(n_scr[slot][:, at], axis=1, keepdims=True)
        if slot == 0:
            final = aligned(own_at[0] + r * own_at[1], width)
            pairs = [(yo_ref, yf_ref.at[:, final]), (dxo_ref, dxf_ref.at[:, final])]
            copies = copy_all(pairs, sems)
    for copy in copies:
        copy.wait()


def steps_kernel(sig_ref, rate_ref, step_ref, grow_ref, endw_ref, *refs):
    count = 2 * GROUPS
    gys, dss, gxs = refs[:count], refs[count : 2 * count], refs[2 * count : 3 * count]
    refs = refs[3 * count :]
    us, ts, res = refs[:GROUPS], refs[GROUPS : 2 * GROUPS], refs[2 * GROUPS : 3 * GROUPS]
    dbc_ref, own_ref, send_ref, sums_ref = refs[3 * GROUPS :]

    def total(parts):
        value = parts[0][...]
        for a in parts[1:]:
            value = value + a[...]
        return value

    n = step_ref.shape[0]
    step = step_ref[...]
    ds = total(dss) + endw_ref[...] * total(ts)
    gy = total(gys) + grow_ref[...] * total(us)
    rate = rate_ref[0:1, :]
    last = lax.broadcasted_iota(jnp.int32, (n, LANES), 0) == n - 1
    dcum = gy - step * ds + jnp.where(last, total(res)[0:1, :], 0.0)
    lower = jnp.where(triangle(n), 1.0, 0.0).astype(F32)
    dlog = dot(lower, dcum, TN, precision=HIGHEST)
    draw = (ds - rate * dlog) * sig_ref[...]
    turned = draw.T
    heads = own_ref.shape[0]
    own_ref[...] = turned[:heads, :]
    both = split(turned[heads : 2 * heads, :])
    send_ref[0:n, :] = dbc_ref[...]
    send_ref[n:, :LANES] = both[:heads]
    send_ref[n:, LANES:] = both[heads:]
    sums_ref[0:1, :] = jnp.sum(draw, axis=0, keepdims=True)
    sums_ref[1:2, :] = jnp.sum(dlog * (-step * rate), axis=0, keepdims=True)
    sums_ref[2:3, :] = total(gxs)[0:1, :]
    sums_ref[3:8, :] = jnp.zeros((5, LANES), F32)


def conv_back_kernel(
    own_ref, ret_ref, kept_ref, cw_ref, heads_ref, grad_ref, raw_ref, rim_ref, message_ref, z_scr,
    sum_scr, grad_scr, raw_scr, sems,
):
    tokens = own_ref.shape[0]
    taps = cw_ref.shape[0]
    pre = kept_ref[HALO + tokens :, :]
    sig = jax.nn.sigmoid(pre)
    dconv = (own_ref[...] + ret_ref[0:tokens, :].astype(F32)) * sig * (1.0 + pre * (1.0 - sig))
    z_scr[...] = jnp.zeros_like(z_scr)
    z_scr[HALO : HALO + tokens, :] = dconv
    grad = cw_ref[0:1, :] * z_scr[taps - 1 : taps - 1 + tokens + HALO, :]
    for k in range(1, taps):
        grad = grad + cw_ref[k : k + 1, :] * z_scr[taps - 1 - k : taps - 1 - k + tokens + HALO, :]
    grad_scr[...] = grad[HALO:, :]
    raw = ret_ref[tokens:, :].astype(F32)
    raw_scr[...] = raw[:, :LANES] + raw[:, LANES:]
    copies = copy_all([(grad_scr, grad_ref), (raw_scr, raw_ref)], sems)
    rim_ref[...] = grad[HALO - 8 : HALO, :]
    first = HALO - taps + 1
    sum_scr[...] = jnp.zeros_like(sum_scr)
    for k in range(taps):
        sum_scr[k : k + 1, :] = jnp.sum(
            dconv * kept_ref[first + k : first + k + tokens, :], axis=0, keepdims=True
        )
    sum_scr[taps : taps + 1, :] = jnp.sum(dconv, axis=0, keepdims=True)
    sum_scr[5:8, aligned(side() * LANES, LANES)] = heads_ref[0:3, :]
    small = split(sum_scr[...])
    message_ref[0 : tokens + HALO, :] = grad.astype(BF16)
    message_ref[tokens + HALO :, :] = small
    for copy in copies:
        copy.wait()


def pack_kernel(layer_ref, halo_ref, keep_ref, send_ref, sems):
    half, _, rows = keep_ref.shape
    pairs = []
    for k in range(2 * half):
        out = keep_ref.at[k] if k < half else send_ref.at[k - half]
        at = peer_columns(k, rows)
        pairs.append((halo_ref.at[:, at], out.at[0:HALO, :]))
        pairs.append((layer_ref.at[:, at], out.at[HALO:, :]))
    for copy in copy_all(pairs, sems):
        copy.wait()


def relay_kernel(picks, *refs):
    out_ref = refs[-1]
    for j, (ref, at) in enumerate(picks):
        out_ref[j] = refs[ref][at]


def turn_kernel(picks, *refs):
    out_ref = refs[-1]
    parts = [refs[ref].at[at] for ref, at in picks]
    tokens = parts[0].shape[0] - HALO
    for k, part in enumerate(parts):
        out_ref[:, k * tokens : (k + 1) * tokens] = part[HALO:, :].T
    halos = jnp.concatenate([part[0:HALO, :] for part in parts], 0)
    out_ref[:, len(parts) * tokens :] = halos.T


def weight_kernel(count, left_ref, *refs):
    rights, out_ref = refs[:count], refs[count]
    tokens = (left_ref.shape[1] // count) - HALO
    right = jnp.concatenate(
        [a[HALO : HALO + tokens, :] for a in rights] + [a[0:HALO, :] for a in rights], 0
    )
    at = tokens + HALO
    both = jnp.zeros((16, right.shape[1]), F32)
    for a in rights:
        both += a[at : at + 16, :].astype(F32)
    small = split(both[0:8, :] + both[8:16, :])
    chunk = out_ref.shape[1] - 16
    for k in range(out_ref.shape[0]):
        term = dot(left_ref[k * chunk : (k + 1) * chunk, :], right)
        out_ref[k, 0:chunk, :] = term.astype(BF16)
        out_ref[k, chunk:, :] = small


def reduce_kernel(heads, terms_ref, total_ref, cw_ref, cb_ref, *head_refs):
    chunk = total_ref.shape[1]
    total = terms_ref[0].astype(F32)
    for k in range(1, terms_ref.shape[0]):
        total = total + terms_ref[k].astype(F32)
    for k in range(total_ref.shape[0]):
        total_ref[k] = total[0:chunk].astype(BF16)
    small = total[chunk : chunk + 8] + total[chunk + 8 :]
    taps = cw_ref.shape[0]
    cw_ref[...] = small[0:taps, :]
    cb_ref[...] = small[taps : taps + 1, :]
    for i, ref in enumerate(head_refs):
        row = small[5 + i : 6 + i, :]
        ref[:, :heads] = row[:, :heads] + row[:, heads : 2 * heads]
        row = row[:, LANES:]
        ref[:, heads:] = row[:, :heads] + row[:, heads : 2 * heads]


def place_rows_kernel(parts_ref, out_ref):
    chunk = parts_ref.shape[1]
    for k in range(parts_ref.shape[0]):
        out_ref[k * chunk : (k + 1) * chunk, :] = parts_ref[k].astype(F32)


def tokens_kernel(count, *refs):
    pieces = refs[:count]
    grad_ref, rim_ref, out_ref, w_scr, sems = refs[count:]
    copies = copy_all([(pieces[k], w_scr.at[k]) for k in range(count)], sems)
    tail = rim_ref.shape[0]
    own = grad_ref[...]
    g = jnp.concatenate([own[:-tail], own[-tail:] + rim_ref[...]], 0).astype(BF16)
    rows = pieces[0].shape[0]
    for k in range(count):
        copies[k].wait()
        out_ref[:, peer_columns(k, rows)] = dot(g, w_scr[k], NT).astype(BF16)


def join_kernel(*refs):
    own_ref, back_ref = refs[2:4]
    backs = refs[4 : 4 + 2 * GROUPS]
    y_ref, dx_ref, raw_ref, sems = refs[4 + 2 * GROUPS :]
    r = side()
    at = (1 - r) * (y_ref.shape[1] // 2)
    pairs = []
    for i in range(GROUPS):
        y, dx = backs[2 * i : 2 * i + 2]
        columns = aligned(at, y.shape[1])
        at += y.shape[1]
        pairs.append((y, y_ref.at[:, columns]))
        pairs.append((dx, dx_ref.at[:, columns]))
    copies = copy_all(pairs, sems)
    heads = own_ref.shape[0]
    raw_ref[pl.ds(pl.multiple_of(r * heads, 8), heads), :] = own_ref[...]
    raw_ref[pl.ds(pl.multiple_of((1 - r) * heads, 8), heads), :] = back_ref[...]
    for copy in copies:
        copy.wait()


def pinned(x):
    return pltpu.with_memory_space_constraint(x, pltpu.HBM)


def toggled(x, axis, bits):
    size = lax.axis_size(axis)
    return lax.ppermute(x, axis, [(i, i ^ bits) for i in range(size)])


def exchanged(x, axis):
    return lax.all_to_all(x, axis, 0, 0)


def after(x, *others):
    return lax.optimization_barrier((x, *others))[0]


def body(layer_in, w_bc, conv_w, conv_b, ssm_in, dt_raw, dt_bias, a_log, skip_scale, grad_out):
    ctx, fsdp = lax.axis_size("ctx"), lax.axis_size("fsdp")
    layer, x, g, dt = layer_in[0], ssm_in[0], grad_out[0], dt_raw[0].T
    tokens, width = x.shape
    total_heads = dt_bias.shape[0]
    heads = total_heads // 2
    half = width // 2
    counts = [heads // part for part in PARTS]
    starts = [sum(counts[:i]) for i in range(GROUPS)]
    widths = [half // part for part in PARTS]
    ats = [sum(widths[:i]) for i in range(GROUPS)]
    state = w_bc.shape[1] // 2
    taps = conv_w.shape[0]
    rows = w_bc.shape[0]
    chunk_rows = rows // ctx
    pairs = ctx // 2
    hops = pairs - 1
    square = shape((tokens, LANES), F32)
    flats = [shape((tokens, a), BF16) for a in widths]
    turned = shape((heads, tokens), F32)
    both_bc = [shape((tokens, 2 * state), F32)] * 2

    tail = call(
        tail_kernel, "tail", shape((HALO, layer.shape[1]), BF16), (), hbm=(pinned(layer),),
        scratch=[pltpu.SemaphoreType.DMA((1,))],
    )
    halo = lax.ppermute(tail, "ctx", [(i, i + 1) for i in range(ctx - 1)])
    dt_back = toggled(dt, "ctx", 1)
    swap = call(
        swap_kernel, "swap", shape((tokens, width), BF16), (), hbm=(pinned(x), pinned(g)),
        scratch=[pltpu.SemaphoreType.DMA((2,))],
    )
    swapped = toggled(after(swap, halo, dt_back), "ctx", 1)

    step, cum, cumt, grow, endw, sig, rate = call(
        vectors_kernel, "vectors", [square] * 6 + [shape((8, LANES), F32)], (), dt, dt_back,
        dt_bias[None, :], a_log[None, :],
        scratch=[pltpu.VMEM((tokens, tokens), F32), pltpu.VMEM((8, LANES), F32)],
    )

    def source(slot, i):
        if slot == 0:
            return (ats[i], half), (ats[i], half), x, g
        return (ats[i], 0), (half + ats[i], 0), swapped, swapped

    def scale(slot, i):
        x_at, g_at, xa, ga = source(slot, i)
        return call(
            functools.partial(scale_kernel, counts[i], slot * heads + starts[i], x_at, g_at), "scale",
            [flats[i]] * 2, (), xa, ga, step, grow, endw,
        )

    scaled = {(0, i): scale(0, i) for i in range(GROUPS)}
    def landing(count):
        return [
            pltpu.VMEM(layer.shape, BF16),
            pltpu.VMEM((count, *w_bc.shape), BF16),
            pltpu.SemaphoreType.DMA((1 + count,)),
        ]

    parts = shape((fsdp // 2, tokens + HALO, rows), BF16)
    packs = call(
        pack_kernel, "pack", [parts, parts], (), hbm=(pinned(layer), halo),
        scratch=[pltpu.SemaphoreType.DMA((2 * fsdp,))],
    )
    far_bit = fsdp // 2
    own = after(w_bc, swap)
    far = [toggled(own, "fsdp", far_bit)]
    near = [own]
    while len(near) < far_bit:
        near += [toggled(a, "fsdp", len(near)) for a in near]
    early = call(
        functools.partial(early_kernel, len(near)), "project_early",
        shape((tokens, 2 * state), F32), (), hbm=(pinned(layer), after(near[0], packs[0]), *near[1:]),
        scratch=landing(len(near)),
    )
    far[0] = after(far[0], early, *[scaled[0, i][0] for i in range(GROUPS)])
    while len(far) < far_bit:
        far += [toggled(a, "fsdp", len(far)) for a in far]
    pieces = near + far
    layer_scr, w_scr, sems = landing(fsdp)
    kept, bc = call(
        functools.partial(project_kernel, len(near), fsdp), "project",
        [
            shape((2 * tokens + HALO, 2 * state), F32),
            shape((tokens, 2 * state), BF16),
        ],
        (), halo, early, conv_w, conv_b[None, :], hbm=(pinned(layer), *pieces),
        scratch=[layer_scr, w_scr, pltpu.VMEM((tokens + HALO, 2 * state), F32), sems],
    )
    bcs = [bc, toggled(bc, "ctx", 1)]
    def within(slot, i, *earlier):
        x_at, g_at, xa, ga = source(slot, i)
        return call(
            functools.partial(
                inside_kernel, counts[i], slot * heads + starts[i], starts[i], heads, x_at, g_at
            ),
            "inside",
            [shape((tokens, widths[i]), F32)] * 2 + [shape((tokens, tokens), F32), square, square]
            + [shape((8, LANES), F32)],
            (skip_scale,), xa, ga, after(bcs[slot], *earlier), step, cum, cumt,
        )

    order = [(slot, i) for slot in range(2) for i in range(GROUPS)]
    inside, states, received, earlier = {}, [], [], []
    for key in order[:GROUPS]:
        inside[key] = within(*key, *earlier)
        earlier = [inside[key][2]]
    for i in range(GROUPS):
        lanes = (starts[i], heads + starts[i])
        scaled[1, i] = scale(1, i)
        wide = shape((state, widths[i]), BF16)
        first, p, q, s_first, d_second, decays = call(
            functools.partial(states_kernel, counts[i], lanes), "states",
            [wide] * 5 + [shape((8, widths[i]), F32)],
            (), *bcs, *scaled[0, i], *scaled[1, i], after(grow, *earlier),
            scratch=[pltpu.VMEM((2, state, widths[i]), F32)] * 2
            + [pltpu.VMEM((2, 1, widths[i]), F32)],
        )
        states.append((decays, p, s_first, d_second, q))
        received.append([first])
        earlier = [first]
    for slot, i in order[GROUPS:]:
        inside[slot, i] = within(slot, i, *earlier)
        earlier = [inside[slot, i][2]]
    for hop in range(hops):
        moves = [(hop, hop + 1), (pairs - 1 - hop, pairs - 2 - hop)]
        moves = [(2 * a + i, 2 * b + i) for a, b in moves for i in range(2)]
        for i in range(GROUPS):
            value = received[i][-1]
            if hop:
                decays, p, _, _, q = states[i]
                value = call(
                    functools.partial(hop_kernel, hop), "hop", shape(value.shape, BF16), (),
                    after(value, *earlier), p, q, decays,
                )
                earlier = [value]
            received[i].append(lax.ppermute(value, "ctx", moves))
    arrays = [packs[0]]
    at = {(0, k): (0, k) for k in range(fsdp // 2)}
    message, bit = packs[1], fsdp // 2
    sent = [(0, k) for k in range(bit, fsdp)]
    while bit:
        arrays.append(toggled(message, "fsdp", bit))
        for j, (source_bits, owner_bits) in enumerate(sent):
            at[source_bits ^ bit, owner_bits ^ bit] = (len(arrays) - 1, j)
        bit //= 2
        if bit:
            sent = [key for key in sorted(at) if key[1] & bit and key[1] < 2 * bit]
            message = call(
                functools.partial(relay_kernel, [at[key] for key in sent]), "relay",
                shape((len(sent), tokens + HALO, rows), BF16), (), after(arrays[0], received[-1][0]),
                *arrays[1:],
            )
    picks = [at[k, 0] for k in range(fsdp)]
    dbcs = call(inside_bc_kernel, "inside_bc", both_bc, (), *bcs, *[inside[key][2] for key in order])

    full = shape((tokens, width), BF16)
    finals, sends, us, ts, res = (), [], [], [], []
    for i in range(GROUPS):
        last = i == GROUPS - 1
        own_at, _, xa, ga = source(0, i)
        x_at, g_at, xb, gb = source(1, i)
        if i == 1:
            left = call(
                functools.partial(turn_kernel, picks), "turn",
                shape((rows, fsdp * (tokens + HALO)), BF16), (), after(arrays[0], *sends), *arrays[1:],
            )
        lanes = (starts[i], heads + starts[i])
        y, dx, y_send, dx_send, dbc_own, dbc_other, u, t, re = call(
            functools.partial(
                across_kernel, counts[i], lanes, hops, len(finals) // 2, own_at, (x_at, g_at)
            ),
            "across",
            [full, full, flats[i], flats[i]]
            + [both_bc[0], shape((tokens, 2 * state), BF16 if last else F32)]
            + [square, square, shape((8, LANES), F32)],
            (), xa, ga, xb, gb, after(bcs[0], left) if i == 1 else bcs[0], bcs[1], *scaled[0, i],
            *scaled[1, i], step, grow, endw,
            *states[i][:4], *inside[0, i][:2], *inside[1, i][:2], *dbcs, *received[i][1:],
            hbm=finals, hbm_outs=2, aliases={0: 0, 1: 1} if finals else None,
            scratch=[pltpu.VMEM((state, widths[i]), BF16)] * 2
            + [pltpu.VMEM((2, state, widths[i]), BF16)] * 2
            + [pltpu.VMEM((2, 1, widths[i]), F32)] + [pltpu.VMEM((tokens, widths[i]), BF16)] * 2
            + [pltpu.SemaphoreType.DMA((2,))],
        )
        finals, dbcs = (y, dx), (dbc_own, dbc_other)
        sends += [y_send, dx_send]
        us.append(u)
        ts.append(t)
        res.append(re)

    raw_own, dbc_send, head_sums = call(
        steps_kernel, "steps",
        [turned, shape((tokens + heads, 2 * state), BF16), shape((8, LANES), F32)], (),
        sig, rate, step, grow, endw, *[inside[key][j] for j in (3, 4, 5) for key in order],
        *us, *ts, *res, dbcs[1],
    )
    dbc_ret = toggled(dbc_send, "ctx", 1)
    backs = [toggled(sends[0], "ctx", 1)]
    grad, raw_back, rim_send, message = call(
        conv_back_kernel, "conv_back",
        [
            shape((tokens, 2 * state), F32),
            turned,
            shape((8, 2 * state), F32),
            shape((tokens + HALO + 16, 2 * state), BF16),
        ],
        (), after(dbcs[0], *backs), dbc_ret, kept, conv_w, head_sums, hbm_outs=2,
        scratch=[
            pltpu.VMEM((tokens + 2 * HALO, 2 * state), F32),
            pltpu.VMEM((8, 2 * state), F32),
            pltpu.VMEM((tokens, 2 * state), F32),
            pltpu.VMEM(turned.shape, F32),
            pltpu.SemaphoreType.DMA((2,)),
        ],
    )
    rim = lax.ppermute(rim_send, "ctx", [(i + 1, i) for i in range(ctx - 1)])
    backs.append(toggled(after(sends[1], dbc_ret), "ctx", 1))

    rights = [message] + [toggled(message, "fsdp", k) for k in range(fsdp - 1, 0, -1)][::-1]
    terms = call(
        functools.partial(weight_kernel, fsdp), "weight",
        shape((ctx, chunk_rows + 16, 2 * state), BF16), (), left, after(message, rim, *backs), *rights[1:],
    )
    backs += [toggled(after(a, terms), "ctx", 1) for a in sends[2:]]
    total, grad_cw, grad_cb, *per_head = call(
        functools.partial(reduce_kernel, heads), "reduce",
        [
            shape((ctx, chunk_rows, 2 * state), BF16),
            shape((taps, 2 * state), F32),
            shape((1, 2 * state), F32),
        ]
        + [shape((1, total_heads), F32)] * 3,
        (), after(exchanged(terms, "ctx"), *backs[:-1]),
    )
    grad_weight = call(
        place_rows_kernel, "place_rows", shape((rows, 2 * state), F32), (), exchanged(total, "ctx")
    )
    grad_tokens = call(
        functools.partial(tokens_kernel, fsdp), "grad_tokens", shape((tokens, fsdp * rows), BF16),
        (), after(grad, total), rim, hbm=pieces,
        scratch=[pltpu.VMEM((fsdp, *w_bc.shape), BF16), pltpu.SemaphoreType.DMA((fsdp,))],
    )
    ssm_out, grad_values, grad_raw = call(
        join_kernel, "join", [full, full, shape((total_heads, tokens), F32)],
        (), raw_own, raw_back, *backs, hbm=finals, hbm_outs=2,
        aliases={0: 0, 1: 1}, scratch=[pltpu.SemaphoreType.DMA((2 * GROUPS,))],
    )
    return (
        ssm_out[None],
        grad_values[None],
        grad_tokens[None],
        grad_raw.T[None],
        grad_weight,
        grad_cw,
        grad_cb[0],
        *[a[0] for a in per_head],
    )


def solution(mesh):
    tokens = P("fsdp", "ctx", None)
    in_specs = (tokens, P("fsdp", None), P(), P(), tokens, tokens, P(), P(), P(), tokens)
    out_specs = (tokens, tokens, tokens, tokens, P("fsdp", None), P(), P(), P(), P(), P())
    return jax.shard_map(body, mesh=mesh, in_specs=in_specs, out_specs=out_specs, check_vma=False)
```

profile of v0, /device:TPU:0, one launch (start us, length us, event | category | flops | bytes accessed | tf_op | source)
XLA Modules:
  0.0 138.3 jit_solution(4483734407263279454)
XLA Ops:
  1.6 4.8 %collective-permute-start = (bf16[16,4096]{1,0:T(8,128)(2,1)S(1)}, bf16[16,4096]{1,0:T(8,128)(2,1)S(1)}, u32[]{:S(2)}, u32[]{:S(2)}) collective-permute-start(bf16[16,4096]{1,0:T(8,128)(2,1)S(1)} %tail.1), channel_id=1, source_target_pairs={{0,4},{4,8},{8,12},{12,16},{16,20},{20,24},{24,28},{1,5},{5,9},{9,... | collective-permute-start | bytes 393224 | tf_op jit(solution)/shard_map/ppermute | solution.py:590
  11.1 2.2 %collective-permute-done.1.back_ref = f32[32,128]{1,0:T(8,128)S(1)} collective-permute-done((f32[32,128]{1,0:T(8,128)S(1)}, f32[32,128]{1,0:T(8,128)S(1)}, u32[]{:S(2)}, u32[]{:S(2)}) %collective-permute-start.1) | collective-permute-done | bytes 16416 | tf_op jit(solution)/shard_map/ppermute | solution.py:553
  19.0 3.3 %collective-permute-done.4.refs_2_ = bf16[1024,256]{1,0:T(8,128)(2,1)S(1)} collective-permute-done((bf16[1024,256]{1,0:T(8,128)(2,1)S(1)}, bf16[1024,256]{1,0:T(8,128)(2,1)S(1)}, u32[]{:S(2)}, u32[]{:S(2)}) %collective-permute-start.4) | collective-permute-done | bytes 524320 | tf_op jit(solution)/shard_map/ppermute | solution.py:553
  24.2 2.1 %project.1 = (f32[272,256]{1,0:T(8,128)S(1)}, bf16[128,256]{1,0:T(8,128)(2,1)S(1)}) custom-call(bf16[128,4096]{1,0:T(8,128)(2,1)} %bitcast.41, bf16[1024,256]{1,0:T(8,128)(2,1)S(1)} %copy-done.2, bf16[1024,256]{1,0:T(8,128)(2,1)S(1)} %collective-permute-done.3.refs_1_, bf16[1024,256]{1,0:T(8,128)(2,1)S(1)} %collective-permute-done.4.refs_2_, ...), custom_call_target="tpu_custom_call" | custom-call | tf_op jit(solution)/shard_map/project/pallas_call | solution.py:37
  28.0 2.2 %inside.4 = (f32[128,1024]{1,0:T(8,128)S(1)}, f32[128,1024]{1,0:T(8,128)S(1)}, f32[128,128]{1,0:T(8,128)S(1)}, f32[128,128]{1,0:T(8,128)S(1)}, f32[128,128]{1,0:T(8,128)S(1)}, /*index=5*/f32[8,128]{1,0:T(8,128)S(1)}) custom-call(f32[32]{0:T(128)S(1)} %copy-done.7, bf16[128,4096]{1,0:T(8,128)(2,1)S(1)} %bitcast.22, bf16[128,4096]{1,0:T(8,128)(2,1)S(1)} %bitcast.29, ...), custom_call_target="tpu_custom_call" | custom-call | tf_op jit(solution)/shard_map/inside/pallas_call | solution.py:37
  30.2 2.2 %inside.5 = (f32[128,1024]{1,0:T(8,128)S(1)}, f32[128,1024]{1,0:T(8,128)S(1)}, f32[128,128]{1,0:T(8,128)S(1)}, f32[128,128]{1,0:T(8,128)S(1)}, f32[128,128]{1,0:T(8,128)S(1)}, /*index=5*/f32[8,128]{1,0:T(8,128)S(1)}) custom-call(f32[32]{0:T(128)S(1)} %copy-done.7, bf16[128,4096]{1,0:T(8,128)(2,1)S(1)} %bitcast.23, bf16[128,4096]{1,0:T(8,128)(2,1)S(1)} %bitcast.30, ...), custom_call_target="tpu_custom_call" | custom-call | tf_op jit(solution)/shard_map/inside/pallas_call | solution.py:37
  32.5 5.9 %collective-permute-done.2.x_ref.g_ref.refs_2_.refs_3_.refs_4_.refs_5_ = bf16[128,4096]{1,0:T(8,128)(2,1)S(1)} collective-permute-done((bf16[128,4096]{1,0:T(8,128)(2,1)S(1)}, bf16[128,4096]{1,0:T(8,128)(2,1)S(1)}, u32[]{:S(2)}, u32[]{:S(2)}) %collective-permute-start.2) | collective-permute-done | bytes 1048608 | tf_op jit(solution)/shard_map/ppermute | solution.py:553
  39.9 3.5 %collective-permute-start.7 = (bf16[128,1024]{1,0:T(8,128)(2,1)S(1)}, bf16[128,1024]{1,0:T(8,128)(2,1)S(1)}, u32[]{:S(2)}, u32[]{:S(2)}) collective-permute-start(bf16[128,1024]{1,0:T(8,128)(2,1)S(1)} %get-tuple-element.153), channel_id=1, source_target_pairs={{0,8},{4,12},{24,16},{28,20},{1,9},{5,13},{25,17},{29,21},{2,10},{... | collective-permute-start | bytes 786440 | tf_op jit(solution)/shard_map/ppermute | solution.py:701
  46.0 2.3 %inside.6 = (f32[128,1024]{1,0:T(8,128)S(1)}, f32[128,1024]{1,0:T(8,128)S(1)}, f32[128,128]{1,0:T(8,128)S(1)}, f32[128,128]{1,0:T(8,128)S(1)}, f32[128,128]{1,0:T(8,128)S(1)}, /*index=5*/f32[8,128]{1,0:T(8,128)S(1)}) custom-call(f32[32]{0:T(128)S(1)} %copy-done.7, bf16[128,4096]{1,0:T(8,128)(2,1)S(1)} %collective-permute-done.2.x_ref.g_ref.refs_2_.refs_3_.refs_4_.refs_5_, ...), custom_call_target="tpu_custom_call" | custom-call | tf_op jit(solution)/shard_map/inside/pallas_call | solution.py:37
  48.2 2.3 %inside.7 = (f32[128,1024]{1,0:T(8,128)S(1)}, f32[128,1024]{1,0:T(8,128)S(1)}, f32[128,128]{1,0:T(8,128)S(1)}, f32[128,128]{1,0:T(8,128)S(1)}, f32[128,128]{1,0:T(8,128)S(1)}, /*index=5*/f32[8,128]{1,0:T(8,128)S(1)}) custom-call(f32[32]{0:T(128)S(1)} %copy-done.7, bf16[128,4096]{1,0:T(8,128)(2,1)S(1)} %collective-permute-done.2.x_ref.g_ref.refs_2_.refs_3_.refs_4_.refs_5_, ...), custom_call_target="tpu_custom_call" | custom-call | tf_op jit(solution)/shard_map/inside/pallas_call | solution.py:37
  51.3 1.7 %collective-permute-done.9.received_ref.refs_25_ = bf16[128,1024]{1,0:T(8,128)(2,1)S(1)} collective-permute-done((bf16[128,1024]{1,0:T(8,128)(2,1)S(1)}, bf16[128,1024]{1,0:T(8,128)(2,1)S(1)}, u32[]{:S(2)}, u32[]{:S(2)}) %collective-permute-start.9) | collective-permute-done | bytes 262176 | tf_op jit(solution)/shard_map/ppermute | solution.py:701
  56.9 14.9 %collective-permute-done.10.refs_25_ = bf16[128,1024]{1,0:T(8,128)(2,1)S(1)} collective-permute-done((bf16[128,1024]{1,0:T(8,128)(2,1)S(1)}, bf16[128,1024]{1,0:T(8,128)(2,1)S(1)}, u32[]{:S(2)}, u32[]{:S(2)}) %collective-permute-start.10) | collective-permute-done | bytes 262176 | tf_op jit(solution)/shard_map/ppermute | solution.py:701
  71.9 3.1 %across.2 = (bf16[128,4096]{1,0:T(8,128)(2,1)}, bf16[128,4096]{1,0:T(8,128)(2,1)}, bf16[128,1024]{1,0:T(8,128)(2,1)S(1)}, bf16[128,1024]{1,0:T(8,128)(2,1)S(1)},...) custom-call(bf16[128,4096]{1,0:T(8,128)(2,1)S(1)} %bitcast.24, ...), custom_call_target="tpu_custom_call" | custom-call | tf_op jit(solution)/shard_map/across/pallas_call | solution.py:37
  77.0 2.9 %across.3 = (bf16[128,4096]{1,0:T(8,128)(2,1)}, bf16[128,4096]{1,0:T(8,128)(2,1)}, bf16[128,1024]{1,0:T(8,128)(2,1)S(1)}, bf16[128,1024]{1,0:T(8,128)(2,1)S(1)},...) custom-call(bf16[128,4096]{1,0:T(8,128)(2,1)} %get-tuple-element.171, ...), custom_call_target="tpu_custom_call", output_to_operand_aliasing={{0}: (0, {}), {1}: (1, {})} | custom-call | tf_op jit(solution)/shard_map/across/pallas_call | solution.py:37
  80.8 4.2 %collective-permute-done.16.ret_ref = bf16[144,256]{1,0:T(8,128)(2,1)S(1)} collective-permute-done((bf16[144,256]{1,0:T(8,128)(2,1)S(1)}, bf16[144,256]{1,0:T(8,128)(2,1)S(1)}, u32[]{:S(2)}, u32[]{:S(2)}) %collective-permute-start.16) | collective-permute-done | bytes 73760 | tf_op jit(solution)/shard_map/ppermute | solution.py:553
  87.4 1.7 %collective-permute-start.21 = (bf16[160,256]{1,0:T(8,128)(2,1)S(1)}, bf16[160,256]{1,0:T(8,128)(2,1)S(1)}, u32[]{:S(2)}, u32[]{:S(2)}) collective-permute-start(bf16[160,256]{1,0:T(8,128)(2,1)S(1)} %get-tuple-element.222.refs_0_), channel_id=1, source_target_pairs={{0,3},{1,2},{2,1},{3,0},{4,7},{5,6},{6,5},{7,4},{8,11},{9,10},{10,... | collective-permute-start | bytes 245768 | tf_op jit(solution)/shard_map/ppermute | solution.py:553
  90.3 4.2 %collective-permute-done.18.refs_5_ = f32[8,256]{1,0:T(8,128)S(1)} collective-permute-done((f32[8,256]{1,0:T(8,128)S(1)}, f32[8,256]{1,0:T(8,128)S(1)}, u32[]{:S(2)}, u32[]{:S(2)}) %collective-permute-start.18) | collective-permute-done | bytes 8224 | tf_op jit(solution)/shard_map/ppermute | solution.py:781
  96.0 3.5 %all-to-all-start = ((bf16[8,144,256]{2,1,0:T(8,128)(2,1)}), bf16[8,144,256]{2,1,0:T(8,128)(2,1)S(1)}, u32[]{:S(2)}, u32[]{:S(2)}) async-start(bf16[8,144,256]{2,1,0:T(8,128)(2,1)} %weight.1), calls=%async_computation | async-start | bytes 1179648 | tf_op jit(solution)/shard_map/all_to_all | solution.py:557
  99.5 1.9 %collective-permute-start.22 = (bf16[128,1024]{1,0:T(8,128)(2,1)}, bf16[128,1024]{1,0:T(8,128)(2,1)S(1)}, u32[]{:S(2)}, u32[]{:S(2)}) collective-permute-start(bf16[128,1024]{1,0:T(8,128)(2,1)} %copy-done.12), channel_id=1, source_target_pairs={{0,4},{4,0},{8,12},{12,8},{16,20},{20,16},{24,28},{28,24},{1,5},{5... | collective-permute-start | bytes 786440 | tf_op jit(solution)/shard_map/ppermute | solution.py:553
  101.5 12.0 %collective-permute-done.22.refs_6_ = bf16[128,1024]{1,0:T(8,128)(2,1)S(1)} collective-permute-done((bf16[128,1024]{1,0:T(8,128)(2,1)}, bf16[128,1024]{1,0:T(8,128)(2,1)S(1)}, u32[]{:S(2)}, u32[]{:S(2)}) %collective-permute-start.22) | collective-permute-done | bytes 262176 | tf_op jit(solution)/shard_map/ppermute | solution.py:553
  116.0 3.6 %all-to-all-start.1 = ((bf16[8,128,256]{2,1,0:T(8,128)(2,1)}), bf16[8,128,256]{2,1,0:T(8,128)(2,1)S(1)}, u32[]{:S(2)}, u32[]{:S(2)}) async-start(bf16[8,128,256]{2,1,0:T(8,128)(2,1)} %get-tuple-element.230), calls=%async_computation.1 | async-start | bytes 1048576 | tf_op jit(solution)/shard_map/all_to_all | solution.py:557
  119.6 2.0 %collective-permute-start.23 = (bf16[128,1024]{1,0:T(8,128)(2,1)}, bf16[128,1024]{1,0:T(8,128)(2,1)S(1)}, u32[]{:S(2)}, u32[]{:S(2)}) collective-permute-start(bf16[128,1024]{1,0:T(8,128)(2,1)} %copy-done.11), channel_id=1, source_target_pairs={{0,4},{4,0},{8,12},{12,8},{16,20},{20,16},{24,28},{28,24},{1,5},{5... | collective-permute-start | bytes 786440 | tf_op jit(solution)/shard_map/ppermute | solution.py:553
  121.6 11.6 %collective-permute-done.23.refs_7_ = bf16[128,1024]{1,0:T(8,128)(2,1)S(1)} collective-permute-done((bf16[128,1024]{1,0:T(8,128)(2,1)}, bf16[128,1024]{1,0:T(8,128)(2,1)S(1)}, u32[]{:S(2)}, u32[]{:S(2)}) %collective-permute-start.23) | collective-permute-done | bytes 262176 | tf_op jit(solution)/shard_map/ppermute | solution.py:553
  134.8 2.4 %grad_tokens.1 = bf16[128,4096]{1,0:T(8,128)(2,1)} custom-call(bf16[1024,256]{1,0:T(8,128)(2,1)S(1)} %copy-done.2, bf16[1024,256]{1,0:T(8,128)(2,1)S(1)} %collective-permute-done.3.refs_1_, bf16[1024,256]{1,0:T(8,128)(2,1)S(1)} %collective-permute-done.4.refs_2_, bf16[1024,256]{1,0:T(8,128)(2,1)S(1)} %collective-permute-done.5.refs_3_, ...), custom_call_target="tpu_custom_call" | custom-call | tf_op jit(solution)/shard_map/grad_tokens/pallas_call | solution.py:37
  (86 shorter events, 36.3 us)
Async XLA Ops:
  1.6 11.7 %collective-permute-start = (bf16[16,4096]{1,0:T(8,128)(2,1)S(1)}, bf16[16,4096]{1,0:T(8,128)(2,1)S(1)}, u32[]{:S(2)}, u32[]{:S(2)}) collective-permute-start(bf16[16,4096]{1,0:T(8,128)(2,1)S(1)} %tail.1), channel_id=1, source_target_pairs={{0,4},{4,8},{8,12},{12,16},{16,20},{20,24},{24,28},{1,5},{5,9},{9,... | collective-permute-start | bytes 393224 | tf_op jit(solution)/shard_map/ppermute | solution.py:590
  7.9 9.5 %collective-permute-start.3 = (bf16[1024,256]{1,0:T(8,128)(2,1)S(1)}, bf16[1024,256]{1,0:T(8,128)(2,1)S(1)}, u32[]{:S(2)}, u32[]{:S(2)}) collective-permute-start(bf16[1024,256]{1,0:T(8,128)(2,1)S(1)} %copy-done.2), channel_id=1, source_target_pairs={{0,1},{1,0},{2,3},{3,2},{4,5},{5,4},{6,7},{7,6},{8,9},{9,8},{10,11... | collective-permute-start | bytes 1572872 | tf_op jit(solution)/shard_map/ppermute | solution.py:553
  8.0 14.3 %collective-permute-start.4 = (bf16[1024,256]{1,0:T(8,128)(2,1)S(1)}, bf16[1024,256]{1,0:T(8,128)(2,1)S(1)}, u32[]{:S(2)}, u32[]{:S(2)}) collective-permute-start(bf16[1024,256]{1,0:T(8,128)(2,1)S(1)} %copy-done.2), channel_id=1, source_target_pairs={{0,2},{1,3},{2,0},{3,1},{4,6},{5,7},{6,4},{7,5},{8,10},{9,11},{10,... | collective-permute-start | bytes 1572872 | tf_op jit(solution)/shard_map/ppermute | solution.py:553
  9.6 3.7 %collective-permute-start.1 = (f32[32,128]{1,0:T(8,128)S(1)}, f32[32,128]{1,0:T(8,128)S(1)}, u32[]{:S(2)}, u32[]{:S(2)}) collective-permute-start(f32[32,128]{1,0:T(8,128)S(1)} %bitcast.33), channel_id=1, source_target_pairs={{0,4},{4,0},{8,12},{12,8},{16,20},{20,16},{24,28},{28,24},{1,5},{5... | collective-permute-start | bytes 49160 | tf_op jit(solution)/shard_map/ppermute | solution.py:553
  13.3 25.1 %collective-permute-start.2 = (bf16[128,4096]{1,0:T(8,128)(2,1)S(1)}, bf16[128,4096]{1,0:T(8,128)(2,1)S(1)}, u32[]{:S(2)}, u32[]{:S(2)}) collective-permute-start(bf16[128,4096]{1,0:T(8,128)(2,1)S(1)} %swap.1), channel_id=1, source_target_pairs={{0,4},{4,0},{8,12},{12,8},{16,20},{20,16},{24,28},{28,24},{1,5},{5... | collective-permute-start | bytes 3145736 | tf_op jit(solution)/shard_map/ppermute | solution.py:553
  22.3 23.5 %collective-permute-start.11 = (bf16[2,144,1024]{2,1,0:T(8,128)(2,1)S(1)}, bf16[2,144,1024]{2,1,0:T(8,128)(2,1)S(1)}, u32[]{:S(2)}, u32[]{:S(2)}) collective-permute-start(bf16[2,144,1024]{2,1,0:T(8,128)(2,1)S(1)} %get-tuple-element.176), channel_id=1, source_target_pairs={{0,2},{1,3},{2,0},{3,1},{4,6},{5,7},{6,4},{7,5},{8,10},{9,11},{10,... | collective-permute-start | bytes 1769480 | tf_op jit(solution)/shard_map/ppermute | solution.py:553
  26.4 12.7 %collective-permute-start.6 = (bf16[128,256]{1,0:T(8,128)(2,1)S(1)}, bf16[128,256]{1,0:T(8,128)(2,1)S(1)}, u32[]{:S(2)}, u32[]{:S(2)}) collective-permute-start(bf16[128,256]{1,0:T(8,128)(2,1)S(1)} %get-tuple-element.178.bc_ref.bc0_ref.refs_4_.refs_6_), channel_id=1, source_target_pairs={{0,4},{4,0},{8,12},{12,8},{16,20},{20,16},{24,28},{28,24},{1,5},{5... | collective-permute-start | bytes 196616 | tf_op jit(solution)/shard_map/ppermute | solution.py:553
  39.9 10.6 %collective-permute-start.7 = (bf16[128,1024]{1,0:T(8,128)(2,1)S(1)}, bf16[128,1024]{1,0:T(8,128)(2,1)S(1)}, u32[]{:S(2)}, u32[]{:S(2)}) collective-permute-start(bf16[128,1024]{1,0:T(8,128)(2,1)S(1)} %get-tuple-element.153), channel_id=1, source_target_pairs={{0,8},{4,12},{24,16},{28,20},{1,9},{5,13},{25,17},{29,21},{2,10},{... | collective-permute-start | bytes 786440 | tf_op jit(solution)/shard_map/ppermute | solution.py:701
  44.5 8.5 %collective-permute-start.9 = (bf16[128,1024]{1,0:T(8,128)(2,1)S(1)}, bf16[128,1024]{1,0:T(8,128)(2,1)S(1)}, u32[]{:S(2)}, u32[]{:S(2)}) collective-permute-start(bf16[128,1024]{1,0:T(8,128)(2,1)S(1)} %get-tuple-element.155), channel_id=1, source_target_pairs={{0,8},{4,12},{24,16},{28,20},{1,9},{5,13},{25,17},{29,21},{2,10},{... | collective-permute-start | bytes 786440 | tf_op jit(solution)/shard_map/ppermute | solution.py:701
  45.9 30.7 %collective-permute-start.12 = (bf16[2,144,1024]{2,1,0:T(8,128)(2,1)S(1)}, bf16[2,144,1024]{2,1,0:T(8,128)(2,1)S(1)}, u32[]{:S(2)}, u32[]{:S(2)}) collective-permute-start(bf16[2,144,1024]{2,1,0:T(8,128)(2,1)S(1)} %relay.1), channel_id=1, source_target_pairs={{0,1},{1,0},{2,3},{3,2},{4,5},{5,4},{6,7},{7,6},{8,9},{9,8},{10,11... | collective-permute-start | bytes 1769480 | tf_op jit(solution)/shard_map/ppermute | solution.py:553
  50.6 3.2 %collective-permute-start.8 = (bf16[128,1024]{1,0:T(8,128)(2,1)S(1)}, bf16[128,1024]{1,0:T(8,128)(2,1)S(1)}, u32[]{:S(2)}, u32[]{:S(2)}) collective-permute-start(bf16[128,1024]{1,0:T(8,128)(2,1)S(1)} %hop.4), channel_id=1, source_target_pairs={{8,16},{12,20},{16,8},{20,12},{9,17},{13,21},{17,9},{21,13},{10,18... | collective-permute-start | bytes 786440 | tf_op jit(solution)/shard_map/ppermute | solution.py:701
  54.0 17.9 %collective-permute-start.10 = (bf16[128,1024]{1,0:T(8,128)(2,1)S(1)}, bf16[128,1024]{1,0:T(8,128)(2,1)S(1)}, u32[]{:S(2)}, u32[]{:S(2)}) collective-permute-start(bf16[128,1024]{1,0:T(8,128)(2,1)S(1)} %hop.6), channel_id=1, source_target_pairs={{16,24},{20,28},{8,0},{12,4},{17,25},{21,29},{9,1},{13,5},{18,26},... | collective-permute-start | bytes 786440 | tf_op jit(solution)/shard_map/ppermute | solution.py:701
  55.4 21.6 %collective-permute-start.14 = (bf16[128,1024]{1,0:T(8,128)(2,1)S(1)}, bf16[128,1024]{1,0:T(8,128)(2,1)S(1)}, u32[]{:S(2)}, u32[]{:S(2)}) collective-permute-start(bf16[128,1024]{1,0:T(8,128)(2,1)S(1)} %hop.7), channel_id=1, source_target_pairs={{16,24},{20,28},{8,0},{12,4},{17,25},{21,29},{9,1},{13,5},{18,26},... | collective-permute-start | bytes 786440 | tf_op jit(solution)/shard_map/ppermute | solution.py:701
  75.0 11.1 %collective-permute-start.15 = (bf16[128,1024]{1,0:T(8,128)(2,1)S(1)}, bf16[128,1024]{1,0:T(8,128)(2,1)S(1)}, u32[]{:S(2)}, u32[]{:S(2)}) collective-permute-start(bf16[128,1024]{1,0:T(8,128)(2,1)S(1)} %get-tuple-element.173), channel_id=1, source_target_pairs={{0,4},{4,0},{8,12},{12,8},{16,20},{20,16},{24,28},{28,24},{1,5},{5... | collective-permute-start | bytes 786440 | tf_op jit(solution)/shard_map/ppermute | solution.py:553
  80.3 4.7 %collective-permute-start.16 = (bf16[144,256]{1,0:T(8,128)(2,1)S(1)}, bf16[144,256]{1,0:T(8,128)(2,1)S(1)}, u32[]{:S(2)}, u32[]{:S(2)}) collective-permute-start(bf16[144,256]{1,0:T(8,128)(2,1)S(1)} %get-tuple-element.214), channel_id=1, source_target_pairs={{0,4},{4,0},{8,12},{12,8},{16,20},{20,16},{24,28},{28,24},{1,5},{5... | collective-permute-start | bytes 221192 | tf_op jit(solution)/shard_map/ppermute | solution.py:553
  85.0 9.5 %collective-permute-start.17 = (bf16[128,1024]{1,0:T(8,128)(2,1)S(1)}, bf16[128,1024]{1,0:T(8,128)(2,1)S(1)}, u32[]{:S(2)}, u32[]{:S(2)}) collective-permute-start(bf16[128,1024]{1,0:T(8,128)(2,1)S(1)} %get-tuple-element.218), channel_id=1, source_target_pairs={{0,4},{4,0},{8,12},{12,8},{16,20},{20,16},{24,28},{28,24},{1,5},{5... | collective-permute-start | bytes 786440 | tf_op jit(solution)/shard_map/ppermute | solution.py:553
  87.2 7.4 %collective-permute-start.19 = (bf16[160,256]{1,0:T(8,128)(2,1)S(1)}, bf16[160,256]{1,0:T(8,128)(2,1)S(1)}, u32[]{:S(2)}, u32[]{:S(2)}) collective-permute-start(bf16[160,256]{1,0:T(8,128)(2,1)S(1)} %get-tuple-element.222.refs_0_), channel_id=1, source_target_pairs={{0,1},{1,0},{2,3},{3,2},{4,5},{5,4},{6,7},{7,6},{8,9},{9,8},{10,11... | collective-permute-start | bytes 245768 | tf_op jit(solution)/shard_map/ppermute | solution.py:553
  87.2 7.4 %collective-permute-start.20 = (bf16[160,256]{1,0:T(8,128)(2,1)S(1)}, bf16[160,256]{1,0:T(8,128)(2,1)S(1)}, u32[]{:S(2)}, u32[]{:S(2)}) collective-permute-start(bf16[160,256]{1,0:T(8,128)(2,1)S(1)} %get-tuple-element.222.refs_0_), channel_id=1, source_target_pairs={{0,2},{1,3},{2,0},{3,1},{4,6},{5,7},{6,4},{7,5},{8,10},{9,11},{10,... | collective-permute-start | bytes 245768 | tf_op jit(solution)/shard_map/ppermute | solution.py:553
  87.4 7.2 %collective-permute-start.21 = (bf16[160,256]{1,0:T(8,128)(2,1)S(1)}, bf16[160,256]{1,0:T(8,128)(2,1)S(1)}, u32[]{:S(2)}, u32[]{:S(2)}) collective-permute-start(bf16[160,256]{1,0:T(8,128)(2,1)S(1)} %get-tuple-element.222.refs_0_), channel_id=1, source_target_pairs={{0,3},{1,2},{2,1},{3,0},{4,7},{5,6},{6,5},{7,4},{8,11},{9,10},{10,... | collective-permute-start | bytes 245768 | tf_op jit(solution)/shard_map/ppermute | solution.py:553
  89.0 5.5 %collective-permute-start.18 = (f32[8,256]{1,0:T(8,128)S(1)}, f32[8,256]{1,0:T(8,128)S(1)}, u32[]{:S(2)}, u32[]{:S(2)}) collective-permute-start(f32[8,256]{1,0:T(8,128)S(1)} %get-tuple-element.221), channel_id=1, source_target_pairs={{4,0},{8,4},{12,8},{16,12},{20,16},{24,20},{28,24},{5,1},{9,5},{13... | collective-permute-start | bytes 24584 | tf_op jit(solution)/shard_map/ppermute | solution.py:781
  96.0 19.0 %all-to-all-start = ((bf16[8,144,256]{2,1,0:T(8,128)(2,1)}), bf16[8,144,256]{2,1,0:T(8,128)(2,1)S(1)}, u32[]{:S(2)}, u32[]{:S(2)}) async-start(bf16[8,144,256]{2,1,0:T(8,128)(2,1)} %weight.1), calls=%async_computation | async-start | bytes 1179648 | tf_op jit(solution)/shard_map/all_to_all | solution.py:557
  99.5 13.9 %collective-permute-start.22 = (bf16[128,1024]{1,0:T(8,128)(2,1)}, bf16[128,1024]{1,0:T(8,128)(2,1)S(1)}, u32[]{:S(2)}, u32[]{:S(2)}) collective-permute-start(bf16[128,1024]{1,0:T(8,128)(2,1)} %copy-done.12), channel_id=1, source_target_pairs={{0,4},{4,0},{8,12},{12,8},{16,20},{20,16},{24,28},{28,24},{1,5},{5... | collective-permute-start | bytes 786440 | tf_op jit(solution)/shard_map/ppermute | solution.py:553
  116.0 21.3 %all-to-all-start.1 = ((bf16[8,128,256]{2,1,0:T(8,128)(2,1)}), bf16[8,128,256]{2,1,0:T(8,128)(2,1)S(1)}, u32[]{:S(2)}, u32[]{:S(2)}) async-start(bf16[8,128,256]{2,1,0:T(8,128)(2,1)} %get-tuple-element.230), calls=%async_computation.1 | async-start | bytes 1048576 | tf_op jit(solution)/shard_map/all_to_all | solution.py:557
  119.6 13.6 %collective-permute-start.23 = (bf16[128,1024]{1,0:T(8,128)(2,1)}, bf16[128,1024]{1,0:T(8,128)(2,1)S(1)}, u32[]{:S(2)}, u32[]{:S(2)}) collective-permute-start(bf16[128,1024]{1,0:T(8,128)(2,1)} %copy-done.11), channel_id=1, source_target_pairs={{0,4},{4,0},{8,12},{12,8},{16,20},{20,16},{24,28},{28,24},{1,5},{5... | collective-permute-start | bytes 786440 | tf_op jit(solution)/shard_map/ppermute | solution.py:553
  (15 other events, 92.0 us)
where the time goes:
time: 139 us; the launch traced here: 138 us
  waiting for transfers between devices  62.4 us (45%)
  starting transfers between devices  38.9 us (28%)
  Pallas kernels  35.2 us (25%)
    ppermute x16, waiting for transfers between devices, toggled(): return lax.ppermute(x, axis, [(i, i ^ bits) for i in range(size)])  39.9 us
    pallas_call x32, Pallas kernels, call(): pl.pallas_call(kernel, out_shape=outs, in_specs=[pl.BlockSpec(memory_spac...  35.2 us
    ppermute x16, starting transfers between devices, toggled(): return lax.ppermute(x, axis, [(i, i ^ bits) for i in range(size)])  16.9 us
    ppermute x6, waiting for transfers between devices, body(): received[i].append(lax.ppermute(value, 'ctx', moves))  16.7 us
    ppermute x6, starting transfers between devices, body(): received[i].append(lax.ppermute(value, 'ctx', moves))  8.71 us
    all_to_all x2, starting transfers between devices, exchanged(): return lax.all_to_all(x, axis, 0, 0)  7.17 us
    ppermute x1, starting transfers between devices, body(): halo = lax.ppermute(tail, 'ctx', [(i, i + 1) for i in range(ctx - 1)])  4.85 us
    ppermute x1, waiting for transfers between devices, body(): rim = lax.ppermute(rim_send, 'ctx', [(i + 1, i) for i in range(ctx - 1)])  4.24 us
  transfers between devices with their start and end apart: 26, of which 12 were waited for; matrix products, arithmetic and copies ran while one was open for 0% of the time, Pallas kernels for 22%

commit v1 on v0

--- a/solution.py
+++ b/solution.py
@@ -81,18 +81,16 @@
     return jnp.concatenate([high, value - high], 0).astype(BF16)
 
 
-def tail_kernel(layer_ref, out_ref, sems):
+def swap_kernel(layer_ref, x_ref, g_ref, halo_ref, first_ref, x_out_ref, g_out_ref, sems):
+    width = x_out_ref.shape[1]
     tokens = layer_ref.shape[0]
-    for copy in copy_all([(layer_ref.at[tokens - HALO : tokens, :], out_ref)], sems):
-        copy.wait()
-
-
-def swap_kernel(x_ref, g_ref, out_ref, sems):
-    width = out_ref.shape[1] // 2
-    other = aligned((1 - side()) * width, width)
+    base = (1 - side()) * (2 * width)
     pairs = [
-        (x_ref.at[:, other], out_ref.at[:, :width]),
-        (g_ref.at[:, other], out_ref.at[:, width:]),
+        (layer_ref.at[tokens - HALO : tokens, :], halo_ref),
+        (x_ref.at[:, aligned(base, width)], first_ref.at[:, :width]),
+        (g_ref.at[:, aligned(base, width)], first_ref.at[:, width:]),
+        (x_ref.at[:, aligned(base + width, width)], x_out_ref),
+        (g_ref.at[:, aligned(base + width, width)], g_out_ref),
     ]
     for copy in copy_all(pairs, sems):
         copy.wait()
@@ -583,17 +581,15 @@
     turned = shape((heads, tokens), F32)
     both_bc = [shape((tokens, 2 * state), F32)] * 2
 
-    tail = call(
-        tail_kernel, "tail", shape((HALO, layer.shape[1]), BF16), (), hbm=(pinned(layer),),
-        scratch=[pltpu.SemaphoreType.DMA((1,))],
-    )
-    halo = lax.ppermute(tail, "ctx", [(i, i + 1) for i in range(ctx - 1)])
     dt_back = toggled(dt, "ctx", 1)
-    swap = call(
-        swap_kernel, "swap", shape((tokens, width), BF16), (), hbm=(pinned(x), pinned(g)),
-        scratch=[pltpu.SemaphoreType.DMA((2,))],
-    )
-    swapped = toggled(after(swap, halo, dt_back), "ctx", 1)
+    halo_send, *swaps = call(
+        swap_kernel, "swap",
+        [shape((HALO, layer.shape[1]), BF16), shape((tokens, half), BF16), flats[1], flats[1]], (),
+        hbm=(pinned(layer), pinned(x), pinned(g)), scratch=[pltpu.SemaphoreType.DMA((5,))],
+    )
+    halo = lax.ppermute(halo_send, "ctx", [(i, i + 1) for i in range(ctx - 1)])
+    swapped_first = toggled(after(swaps[0], dt_back), "ctx", 1)
+    swapped_x = toggled(after(swaps[1], halo), "ctx", 1)
 
     step, cum, cumt, grow, endw, sig, rate = call(
         vectors_kernel, "vectors", [square] * 6 + [shape((8, LANES), F32)], (), dt, dt_back,
@@ -604,7 +600,9 @@
     def source(slot, i):
         if slot == 0:
             return (ats[i], half), (ats[i], half), x, g
-        return (ats[i], 0), (half + ats[i], 0), swapped, swapped
+        if i == 0:
+            return (0, 0), (widths[0], 0), swapped_first, swapped_first
+        return (0, 0), (0, 0), swapped_x, swapped_g
 
     def scale(slot, i):
         x_at, g_at, xa, ga = source(slot, i)
@@ -614,6 +612,7 @@
         )
 
     scaled = {(0, i): scale(0, i) for i in range(GROUPS)}
+    scaled[1, 0] = scale(1, 0)
     def landing(count):
         return [
             pltpu.VMEM(layer.shape, BF16),
@@ -627,17 +626,18 @@
         scratch=[pltpu.SemaphoreType.DMA((2 * fsdp,))],
     )
     far_bit = fsdp // 2
-    own = after(w_bc, swap)
-    far = [toggled(own, "fsdp", far_bit)]
-    near = [own]
+    far = [toggled(w_bc, "fsdp", far_bit)]
+    near = [w_bc]
     while len(near) < far_bit:
         near += [toggled(a, "fsdp", len(near)) for a in near]
     early = call(
         functools.partial(early_kernel, len(near)), "project_early",
-        shape((tokens, 2 * state), F32), (), hbm=(pinned(layer), after(near[0], packs[0]), *near[1:]),
+        shape((tokens, 2 * state), F32), (), hbm=(pinned(layer), *near),
         scratch=landing(len(near)),
     )
-    far[0] = after(far[0], early, *[scaled[0, i][0] for i in range(GROUPS)])
+    far[0] = after(
+        far[0], early, halo, scaled[1, 0][0], *[scaled[0, i][0] for i in range(GROUPS)]
+    )
     while len(far) < far_bit:
         far += [toggled(a, "fsdp", len(far)) for a in far]
     pieces = near + far
@@ -648,7 +648,7 @@
             shape((2 * tokens + HALO, 2 * state), F32),
             shape((tokens, 2 * state), BF16),
         ],
-        (), halo, early, conv_w, conv_b[None, :], hbm=(pinned(layer), *pieces),
+        (), after(halo, packs[0]), early, conv_w, conv_b[None, :], hbm=(pinned(layer), *pieces),
         scratch=[layer_scr, w_scr, pltpu.VMEM((tokens + HALO, 2 * state), F32), sems],
     )
     bcs = [bc, toggled(bc, "ctx", 1)]
@@ -666,12 +666,13 @@
 
     order = [(slot, i) for slot in range(2) for i in range(GROUPS)]
     inside, states, received, earlier = {}, [], [], []
-    for key in order[:GROUPS]:
-        inside[key] = within(*key, *earlier)
-        earlier = [inside[key][2]]
+    inside[0, 0] = within(0, 0)
+    swapped_g = toggled(after(swaps[2], bcs[1], inside[0, 0][2]), "ctx", 1)
+    earlier = [inside[0, 0][2]]
     for i in range(GROUPS):
         lanes = (starts[i], heads + starts[i])
-        scaled[1, i] = scale(1, i)
+        if i:
+            scaled[1, i] = scale(1, i)
         wide = shape((state, widths[i]), BF16)
         first, p, q, s_first, d_second, decays = call(
             functools.partial(states_kernel, counts[i], lanes), "states",
@@ -683,9 +684,11 @@
         states.append((decays, p, s_first, d_second, q))
         received.append([first])
         earlier = [first]
-    for slot, i in order[GROUPS:]:
-        inside[slot, i] = within(slot, i, *earlier)
-        earlier = [inside[slot, i][2]]
+        if i == 0:
+            for key in order[1:GROUPS]:
+                inside[key] = within(*key, first)
+                earlier.append(inside[key][2])
+    waiting = order[GROUPS:]
     for hop in range(hops):
         moves = [(hop, hop + 1), (pairs - 1 - hop, pairs - 2 - hop)]
         moves = [(2 * a + i, 2 * b + i) for a, b in moves for i in range(2)]
@@ -698,6 +701,10 @@
                     after(value, *earlier), p, q, decays,
                 )
                 earlier = [value]
+                if waiting and i == 0:
+                    key = waiting.pop(0)
+                    inside[key] = within(*key, *earlier)
+                    earlier = [inside[key][2]]
             received[i].append(lax.ppermute(value, "ctx", moves))
     arrays = [packs[0]]
     at = {(0, k): (0, k) for k in range(fsdp // 2)}
@@ -716,6 +723,8 @@
                 *arrays[1:],
             )
     picks = [at[k, 0] for k in range(fsdp)]
+    for key in waiting:
+        inside[key] = within(*key, *earlier)
     dbcs = call(inside_bc_kernel, "inside_bc", both_bc, (), *bcs, *[inside[key][2] for key in order])
 
     full = shape((tokens, width), BF16)

time: 139 us -> 134 us (0.964)
  waiting for transfers between devices: 62.4 us -> 50.7 us
  starting transfers between devices: 38.9 us -> 46.7 us
    ppermute x16 -> x18, starting transfers between devices: 16.9 us -> 23.5 us  [toggled(): return lax.ppermute(x, axis, [(i, i ^ bits) for i in range(size)])]
    ppermute x6, waiting for transfers between devices: 16.7 us -> 10.2 us  [body(): received[i].append(lax.ppermute(value, 'ctx', moves))]
    ppermute x16 -> x18, waiting for transfers between devices: 39.9 us -> 34.1 us  [toggled(): return lax.ppermute(x, axis, [(i, i ^ bits) for i in range(size)])]
    ppermute x6, starting transfers between devices: 8.71 us -> 12.3 us  [body(): received[i].append(lax.ppermute(value, 'ctx', moves))]
    ppermute x1, starting transfers between devices: 4.85 us -> 2.43 us  [body(): halo = lax.ppermute(halo_send, 'ctx', [(i, i + 1) for i in range(ctx - 1)])]
    pallas_call x32 -> x31, Pallas kernels: 35.2 us -> 34.4 us  [call(): pl.pallas_call(kernel, out_shape=outs, in_specs=[pl.BlockSpec(memory_spac...]
  transfers between devices with their start and end apart: 26 -> 28, of which waited for: 12 -> 12; matrix products, arithmetic and copies ran while one was open for 0% -> 0% of each run, Pallas kernels for 22% -> 23%
where the time goes in v1:
time: 134 us
  waiting for transfers between devices  50.7 us (38%)
  starting transfers between devices  46.7 us (35%)
  Pallas kernels  34.4 us (26%)
    pallas_call x31, Pallas kernels, call(): pl.pallas_call(kernel, out_shape=outs, in_specs=[pl.BlockSpec(memory_spac...  34.4 us
    ppermute x18, waiting for transfers between devices, toggled(): return lax.ppermute(x, axis, [(i, i ^ bits) for i in range(size)])  34.1 us
    ppermute x18, starting transfers between devices, toggled(): return lax.ppermute(x, axis, [(i, i ^ bits) for i in range(size)])  23.5 us
    ppermute x6, starting transfers between devices, body(): received[i].append(lax.ppermute(value, 'ctx', moves))  12.3 us
    ppermute x6, waiting for transfers between devices, body(): received[i].append(lax.ppermute(value, 'ctx', moves))  10.2 us
    all_to_all x2, starting transfers between devices, exchanged(): return lax.all_to_all(x, axis, 0, 0)  7.21 us
    ppermute x1, waiting for transfers between devices, body(): rim = lax.ppermute(rim_send, 'ctx', [(i + 1, i) for i in range(ctx - 1)])  4.24 us
  transfers between devices with their start and end apart: 28, of which 12 were waited for; matrix products, arithmetic and copies ran while one was open for 0% of the time, Pallas kernels for 23%

profile of v1, /device:TPU:0, one launch (start us, length us, event | category | flops | bytes accessed | tf_op | source)
XLA Modules:
  0.0 133.7 jit_solution(1910026639985114101)
XLA Ops:
  0.6 3.0 %collective-permute-start = (f32[32,128]{1,0:T(8,128)}, f32[32,128]{1,0:T(8,128)S(1)}, u32[]{:S(2)}, u32[]{:S(2)}) collective-permute-start(f32[32,128]{1,0:T(8,128)} %bitcast.33), channel_id=1, source_target_pairs={{0,4},{4,0},{8,12},{12,8},{16,20},{20,16},{24,28},{28,24},{1,5},{5... | collective-permute-start | bytes 49160 | tf_op jit(solution)/shard_map/ppermute | solution.py:551
  9.1 2.4 %collective-permute-start.4 = (bf16[16,4096]{1,0:T(8,128)(2,1)S(1)}, bf16[16,4096]{1,0:T(8,128)(2,1)S(1)}, u32[]{:S(2)}, u32[]{:S(2)}) collective-permute-start(bf16[16,4096]{1,0:T(8,128)(2,1)S(1)} %get-tuple-element.131), channel_id=1, source_target_pairs={{0,4},{4,8},{8,12},{12,16},{16,20},{20,24},{24,28},{1,5},{5,9},{9,... | collective-permute-start | bytes 393224 | tf_op jit(solution)/shard_map/ppermute | solution.py:590
  14.5 5.1 %collective-permute-done.1.x_ref.g_ref.refs_2_.refs_3_ = bf16[128,2048]{1,0:T(8,128)(2,1)S(1)} collective-permute-done((bf16[128,2048]{1,0:T(8,128)(2,1)S(1)}, bf16[128,2048]{1,0:T(8,128)(2,1)S(1)}, u32[]{:S(2)}, u32[]{:S(2)}) %collective-permute-start.1) | collective-permute-done | bytes 524320 | tf_op jit(solution)/shard_map/ppermute | solution.py:551
  23.4 2.1 %project.1 = (f32[272,256]{1,0:T(8,128)S(1)}, bf16[128,256]{1,0:T(8,128)(2,1)S(1)}) custom-call(bf16[128,4096]{1,0:T(8,128)(2,1)} %bitcast.41, bf16[1024,256]{1,0:T(8,128)(2,1)S(1)} %copy-done.2, bf16[1024,256]{1,0:T(8,128)(2,1)S(1)} %collective-permute-done.2.refs_1_, bf16[1024,256]{1,0:T(8,128)(2,1)S(1)} %collective-permute-done.3.refs_2_, ...), custom_call_target="tpu_custom_call" | custom-call | tf_op jit(solution)/shard_map/project/pallas_call | solution.py:37
  25.5 2.5 %collective-permute-start.6 = (bf16[128,256]{1,0:T(8,128)(2,1)S(1)}, bf16[128,256]{1,0:T(8,128)(2,1)S(1)}, u32[]{:S(2)}, u32[]{:S(2)}) collective-permute-start(bf16[128,256]{1,0:T(8,128)(2,1)S(1)} %get-tuple-element.188.bc_ref.bc0_ref.refs_4_.refs_6_), channel_id=1, source_target_pairs={{0,4},{4,0},{8,12},{12,8},{16,20},{20,16},{24,28},{28,24},{1,5},{5... | collective-permute-start | bytes 196616 | tf_op jit(solution)/shard_map/ppermute | solution.py:551
  28.1 2.2 %inside.4 = (f32[128,1024]{1,0:T(8,128)S(1)}, f32[128,1024]{1,0:T(8,128)S(1)}, f32[128,128]{1,0:T(8,128)S(1)}, f32[128,128]{1,0:T(8,128)S(1)}, f32[128,128]{1,0:T(8,128)S(1)}, /*index=5*/f32[8,128]{1,0:T(8,128)S(1)}) custom-call(f32[32]{0:T(128)S(1)} %copy-done.7, bf16[128,4096]{1,0:T(8,128)(2,1)S(1)} %bitcast.22, bf16[128,4096]{1,0:T(8,128)(2,1)S(1)} %bitcast.29, ...), custom_call_target="tpu_custom_call" | custom-call | tf_op jit(solution)/shard_map/inside/pallas_call | solution.py:37
  30.5 2.5 %collective-permute-start.9 = (bf16[128,1024]{1,0:T(8,128)(2,1)S(1)}, bf16[128,1024]{1,0:T(8,128)(2,1)S(1)}, u32[]{:S(2)}, u32[]{:S(2)}) collective-permute-start(bf16[128,1024]{1,0:T(8,128)(2,1)S(1)} %get-tuple-element.159), channel_id=1, source_target_pairs={{0,4},{4,0},{8,12},{12,8},{16,20},{20,16},{24,28},{28,24},{1,5},{5... | collective-permute-start | bytes 786440 | tf_op jit(solution)/shard_map/ppermute | solution.py:551
  33.8 3.4 %collective-permute-start.7 = (bf16[128,1024]{1,0:T(8,128)(2,1)S(1)}, bf16[128,1024]{1,0:T(8,128)(2,1)S(1)}, u32[]{:S(2)}, u32[]{:S(2)}) collective-permute-start(bf16[128,1024]{1,0:T(8,128)(2,1)S(1)} %get-tuple-element.154), channel_id=1, source_target_pairs={{0,8},{4,12},{24,16},{28,20},{1,9},{5,13},{25,17},{29,21},{2,10},{... | collective-permute-start | bytes 786440 | tf_op jit(solution)/shard_map/ppermute | solution.py:708
  37.1 2.2 %inside.5 = (f32[128,1024]{1,0:T(8,128)S(1)}, f32[128,1024]{1,0:T(8,128)S(1)}, f32[128,128]{1,0:T(8,128)S(1)}, f32[128,128]{1,0:T(8,128)S(1)}, f32[128,128]{1,0:T(8,128)S(1)}, /*index=5*/f32[8,128]{1,0:T(8,128)S(1)}) custom-call(f32[32]{0:T(128)S(1)} %copy-done.7, bf16[128,4096]{1,0:T(8,128)(2,1)S(1)} %bitcast.23, bf16[128,4096]{1,0:T(8,128)(2,1)S(1)} %bitcast.30, ...), custom_call_target="tpu_custom_call" | custom-call | tf_op jit(solution)/shard_map/inside/pallas_call | solution.py:37
  39.4 2.4 %collective-permute-done.9.g_ref.refs_5_ = bf16[128,1024]{1,0:T(8,128)(2,1)S(1)} collective-permute-done((bf16[128,1024]{1,0:T(8,128)(2,1)S(1)}, bf16[128,1024]{1,0:T(8,128)(2,1)S(1)}, u32[]{:S(2)}, u32[]{:S(2)}) %collective-permute-start.9) | collective-permute-done | bytes 262176 | tf_op jit(solution)/shard_map/ppermute | solution.py:551
  43.0 5.0 %collective-permute-start.11 = (bf16[128,1024]{1,0:T(8,128)(2,1)S(1)}, bf16[128,1024]{1,0:T(8,128)(2,1)S(1)}, u32[]{:S(2)}, u32[]{:S(2)}) collective-permute-start(bf16[128,1024]{1,0:T(8,128)(2,1)S(1)} %get-tuple-element.165), channel_id=1, source_target_pairs={{0,8},{4,12},{24,16},{28,20},{1,9},{5,13},{25,17},{29,21},{2,10},{... | collective-permute-start | bytes 786440 | tf_op jit(solution)/shard_map/ppermute | solution.py:708
  49.0 2.3 %inside.6 = (f32[128,1024]{1,0:T(8,128)S(1)}, f32[128,1024]{1,0:T(8,128)S(1)}, f32[128,128]{1,0:T(8,128)S(1)}, f32[128,128]{1,0:T(8,128)S(1)}, f32[128,128]{1,0:T(8,128)S(1)}, /*index=5*/f32[8,128]{1,0:T(8,128)S(1)}) custom-call(f32[32]{0:T(128)S(1)} %copy-done.7, bf16[128,2048]{1,0:T(8,128)(2,1)S(1)} %collective-permute-done.1.x_ref.g_ref.refs_2_.refs_3_, ...), custom_call_target="tpu_custom_call" | custom-call | tf_op jit(solution)/shard_map/inside/pallas_call | solution.py:37
  55.3 2.3 %inside.7 = (f32[128,1024]{1,0:T(8,128)S(1)}, f32[128,1024]{1,0:T(8,128)S(1)}, f32[128,128]{1,0:T(8,128)S(1)}, f32[128,128]{1,0:T(8,128)S(1)}, f32[128,128]{1,0:T(8,128)S(1)}, /*index=5*/f32[8,128]{1,0:T(8,128)S(1)}) custom-call(f32[32]{0:T(128)S(1)} %copy-done.7, bf16[128,1024]{1,0:T(8,128)(2,1)S(1)} %collective-permute-done.8.x_ref.refs_4_, ...), custom_call_target="tpu_custom_call" | custom-call | tf_op jit(solution)/shard_map/inside/pallas_call | solution.py:37
  59.2 8.4 %collective-permute-done.12.refs_25_ = bf16[128,1024]{1,0:T(8,128)(2,1)S(1)} collective-permute-done((bf16[128,1024]{1,0:T(8,128)(2,1)S(1)}, bf16[128,1024]{1,0:T(8,128)(2,1)S(1)}, u32[]{:S(2)}, u32[]{:S(2)}) %collective-permute-start.12) | collective-permute-done | bytes 262176 | tf_op jit(solution)/shard_map/ppermute | solution.py:708
  67.6 3.1 %across.2 = (bf16[128,4096]{1,0:T(8,128)(2,1)}, bf16[128,4096]{1,0:T(8,128)(2,1)}, bf16[128,1024]{1,0:T(8,128)(2,1)S(1)}, bf16[128,1024]{1,0:T(8,128)(2,1)S(1)},...) custom-call(bf16[128,4096]{1,0:T(8,128)(2,1)S(1)} %bitcast.24, ...), custom_call_target="tpu_custom_call" | custom-call | tf_op jit(solution)/shard_map/across/pallas_call | solution.py:37
  71.4 3.0 %across.3 = (bf16[128,4096]{1,0:T(8,128)(2,1)}, bf16[128,4096]{1,0:T(8,128)(2,1)}, bf16[128,1024]{1,0:T(8,128)(2,1)S(1)}, bf16[128,1024]{1,0:T(8,128)(2,1)S(1)},...) custom-call(bf16[128,4096]{1,0:T(8,128)(2,1)} %get-tuple-element.181, ...), custom_call_target="tpu_custom_call", output_to_operand_aliasing={{0}: (0, {}), {1}: (1, {})} | custom-call | tf_op jit(solution)/shard_map/across/pallas_call | solution.py:37
  76.6 2.6 %collective-permute-done.18.ret_ref = bf16[144,256]{1,0:T(8,128)(2,1)S(1)} collective-permute-done((bf16[144,256]{1,0:T(8,128)(2,1)S(1)}, bf16[144,256]{1,0:T(8,128)(2,1)S(1)}, u32[]{:S(2)}, u32[]{:S(2)}) %collective-permute-start.18) | collective-permute-done | bytes 73760 | tf_op jit(solution)/shard_map/ppermute | solution.py:551
  79.2 2.3 %collective-permute-start.19 = (bf16[128,1024]{1,0:T(8,128)(2,1)S(1)}, bf16[128,1024]{1,0:T(8,128)(2,1)S(1)}, u32[]{:S(2)}, u32[]{:S(2)}) collective-permute-start(bf16[128,1024]{1,0:T(8,128)(2,1)S(1)} %get-tuple-element.228), channel_id=1, source_target_pairs={{0,4},{4,0},{8,12},{12,8},{16,20},{20,16},{24,28},{28,24},{1,5},{5... | collective-permute-start | bytes 786440 | tf_op jit(solution)/shard_map/ppermute | solution.py:551
  85.7 4.2 %collective-permute-done.20.refs_5_ = f32[8,256]{1,0:T(8,128)S(1)} collective-permute-done((f32[8,256]{1,0:T(8,128)S(1)}, f32[8,256]{1,0:T(8,128)S(1)}, u32[]{:S(2)}, u32[]{:S(2)}) %collective-permute-start.20) | collective-permute-done | bytes 8224 | tf_op jit(solution)/shard_map/ppermute | solution.py:790
  91.4 3.5 %all-to-all-start = ((bf16[8,144,256]{2,1,0:T(8,128)(2,1)}), bf16[8,144,256]{2,1,0:T(8,128)(2,1)S(1)}, u32[]{:S(2)}, u32[]{:S(2)}) async-start(bf16[8,144,256]{2,1,0:T(8,128)(2,1)} %weight.1), calls=%async_computation | async-start | bytes 1179648 | tf_op jit(solution)/shard_map/all_to_all | solution.py:555
  96.8 11.8 %collective-permute-done.24.refs_6_ = bf16[128,1024]{1,0:T(8,128)(2,1)S(1)} collective-permute-done((bf16[128,1024]{1,0:T(8,128)(2,1)}, bf16[128,1024]{1,0:T(8,128)(2,1)S(1)}, u32[]{:S(2)}, u32[]{:S(2)}) %collective-permute-start.24) | collective-permute-done | bytes 262176 | tf_op jit(solution)/shard_map/ppermute | solution.py:551
  111.3 3.7 %all-to-all-start.1 = ((bf16[8,128,256]{2,1,0:T(8,128)(2,1)}), bf16[8,128,256]{2,1,0:T(8,128)(2,1)S(1)}, u32[]{:S(2)}, u32[]{:S(2)}) async-start(bf16[8,128,256]{2,1,0:T(8,128)(2,1)} %get-tuple-element.240), calls=%async_computation.1 | async-start | bytes 1048576 | tf_op jit(solution)/shard_map/all_to_all | solution.py:555
  117.0 11.6 %collective-permute-done.25.refs_7_ = bf16[128,1024]{1,0:T(8,128)(2,1)S(1)} collective-permute-done((bf16[128,1024]{1,0:T(8,128)(2,1)}, bf16[128,1024]{1,0:T(8,128)(2,1)S(1)}, u32[]{:S(2)}, u32[]{:S(2)}) %collective-permute-start.25) | collective-permute-done | bytes 262176 | tf_op jit(solution)/shard_map/ppermute | solution.py:551
  130.2 2.4 %grad_tokens.1 = bf16[128,4096]{1,0:T(8,128)(2,1)} custom-call(bf16[1024,256]{1,0:T(8,128)(2,1)S(1)} %copy-done.2, bf16[1024,256]{1,0:T(8,128)(2,1)S(1)} %collective-permute-done.2.refs_1_, bf16[1024,256]{1,0:T(8,128)(2,1)S(1)} %collective-permute-done.3.refs_2_, bf16[1024,256]{1,0:T(8,128)(2,1)S(1)} %collective-permute-done.5.refs_3_, ...), custom_call_target="tpu_custom_call" | custom-call | tf_op jit(solution)/shard_map/grad_tokens/pallas_call | solution.py:37
  (89 shorter events, 38.5 us)
Async XLA Ops:
  3.6 9.2 %collective-permute-start.2 = (bf16[1024,256]{1,0:T(8,128)(2,1)}, bf16[1024,256]{1,0:T(8,128)(2,1)S(1)}, u32[]{:S(2)}, u32[]{:S(2)}) collective-permute-start(bf16[1024,256]{1,0:T(8,128)(2,1)} %refs_0_.5), channel_id=1, source_target_pairs={{0,1},{1,0},{2,3},{3,2},{4,5},{5,4},{6,7},{7,6},{8,9},{9,8},{10,11... | collective-permute-start | bytes 1572872 | tf_op jit(solution)/shard_map/ppermute | solution.py:551
  5.6 14.0 %collective-permute-start.1 = (bf16[128,2048]{1,0:T(8,128)(2,1)S(1)}, bf16[128,2048]{1,0:T(8,128)(2,1)S(1)}, u32[]{:S(2)}, u32[]{:S(2)}) collective-permute-start(bf16[128,2048]{1,0:T(8,128)(2,1)S(1)} %get-tuple-element.130), channel_id=1, source_target_pairs={{0,4},{4,0},{8,12},{12,8},{16,20},{20,16},{24,28},{28,24},{1,5},{5... | collective-permute-start | bytes 1572872 | tf_op jit(solution)/shard_map/ppermute | solution.py:551
  7.6 12.8 %collective-permute-start.3 = (bf16[1024,256]{1,0:T(8,128)(2,1)S(1)}, bf16[1024,256]{1,0:T(8,128)(2,1)S(1)}, u32[]{:S(2)}, u32[]{:S(2)}) collective-permute-start(bf16[1024,256]{1,0:T(8,128)(2,1)S(1)} %copy-done.2), channel_id=1, source_target_pairs={{0,2},{1,3},{2,0},{3,1},{4,6},{5,7},{6,4},{7,5},{8,10},{9,11},{10,... | collective-permute-start | bytes 1572872 | tf_op jit(solution)/shard_map/ppermute | solution.py:551
  9.1 11.3 %collective-permute-start.4 = (bf16[16,4096]{1,0:T(8,128)(2,1)S(1)}, bf16[16,4096]{1,0:T(8,128)(2,1)S(1)}, u32[]{:S(2)}, u32[]{:S(2)}) collective-permute-start(bf16[16,4096]{1,0:T(8,128)(2,1)S(1)} %get-tuple-element.131), channel_id=1, source_target_pairs={{0,4},{4,8},{8,12},{12,16},{16,20},{20,24},{24,28},{1,5},{5,9},{9,... | collective-permute-start | bytes 393224 | tf_op jit(solution)/shard_map/ppermute | solution.py:590
  21.7 26.3 %collective-permute-start.13 = (bf16[2,144,1024]{2,1,0:T(8,128)(2,1)S(1)}, bf16[2,144,1024]{2,1,0:T(8,128)(2,1)S(1)}, u32[]{:S(2)}, u32[]{:S(2)}) collective-permute-start(bf16[2,144,1024]{2,1,0:T(8,128)(2,1)S(1)} %get-tuple-element.186), channel_id=1, source_target_pairs={{0,2},{1,3},{2,0},{3,1},{4,6},{5,7},{6,4},{7,5},{8,10},{9,11},{10,... | collective-permute-start | bytes 1769480 | tf_op jit(solution)/shard_map/ppermute | solution.py:551
  25.5 5.0 %collective-permute-start.6 = (bf16[128,256]{1,0:T(8,128)(2,1)S(1)}, bf16[128,256]{1,0:T(8,128)(2,1)S(1)}, u32[]{:S(2)}, u32[]{:S(2)}) collective-permute-start(bf16[128,256]{1,0:T(8,128)(2,1)S(1)} %get-tuple-element.188.bc_ref.bc0_ref.refs_4_.refs_6_), channel_id=1, source_target_pairs={{0,4},{4,0},{8,12},{12,8},{16,20},{20,16},{24,28},{28,24},{1,5},{5... | collective-permute-start | bytes 196616 | tf_op jit(solution)/shard_map/ppermute | solution.py:551
  28.0 11.4 %collective-permute-start.8 = (bf16[128,1024]{1,0:T(8,128)(2,1)S(1)}, bf16[128,1024]{1,0:T(8,128)(2,1)S(1)}, u32[]{:S(2)}, u32[]{:S(2)}) collective-permute-start(bf16[128,1024]{1,0:T(8,128)(2,1)S(1)} %get-tuple-element.157), channel_id=1, source_target_pairs={{0,4},{4,0},{8,12},{12,8},{16,20},{20,16},{24,28},{28,24},{1,5},{5... | collective-permute-start | bytes 786440 | tf_op jit(solution)/shard_map/ppermute | solution.py:551
  30.5 11.3 %collective-permute-start.9 = (bf16[128,1024]{1,0:T(8,128)(2,1)S(1)}, bf16[128,1024]{1,0:T(8,128)(2,1)S(1)}, u32[]{:S(2)}, u32[]{:S(2)}) collective-permute-start(bf16[128,1024]{1,0:T(8,128)(2,1)S(1)} %get-tuple-element.159), channel_id=1, source_target_pairs={{0,4},{4,0},{8,12},{12,8},{16,20},{20,16},{24,28},{28,24},{1,5},{5... | collective-permute-start | bytes 786440 | tf_op jit(solution)/shard_map/ppermute | solution.py:551
  33.8 14.4 %collective-permute-start.7 = (bf16[128,1024]{1,0:T(8,128)(2,1)S(1)}, bf16[128,1024]{1,0:T(8,128)(2,1)S(1)}, u32[]{:S(2)}, u32[]{:S(2)}) collective-permute-start(bf16[128,1024]{1,0:T(8,128)(2,1)S(1)} %get-tuple-element.154), channel_id=1, source_target_pairs={{0,8},{4,12},{24,16},{28,20},{1,9},{5,13},{25,17},{29,21},{2,10},{... | collective-permute-start | bytes 786440 | tf_op jit(solution)/shard_map/ppermute | solution.py:708
  43.0 10.1 %collective-permute-start.11 = (bf16[128,1024]{1,0:T(8,128)(2,1)S(1)}, bf16[128,1024]{1,0:T(8,128)(2,1)S(1)}, u32[]{:S(2)}, u32[]{:S(2)}) collective-permute-start(bf16[128,1024]{1,0:T(8,128)(2,1)S(1)} %get-tuple-element.165), channel_id=1, source_target_pairs={{0,8},{4,12},{24,16},{28,20},{1,9},{5,13},{25,17},{29,21},{2,10},{... | collective-permute-start | bytes 786440 | tf_op jit(solution)/shard_map/ppermute | solution.py:708
  48.1 22.9 %collective-permute-start.14 = (bf16[2,144,1024]{2,1,0:T(8,128)(2,1)S(1)}, bf16[2,144,1024]{2,1,0:T(8,128)(2,1)S(1)}, u32[]{:S(2)}, u32[]{:S(2)}) collective-permute-start(bf16[2,144,1024]{2,1,0:T(8,128)(2,1)S(1)} %relay.1), channel_id=1, source_target_pairs={{0,1},{1,0},{2,3},{3,2},{4,5},{5,4},{6,7},{7,6},{8,9},{9,8},{10,11... | collective-permute-start | bytes 1769480 | tf_op jit(solution)/shard_map/ppermute | solution.py:551
  48.3 5.6 %collective-permute-start.10 = (bf16[128,1024]{1,0:T(8,128)(2,1)S(1)}, bf16[128,1024]{1,0:T(8,128)(2,1)S(1)}, u32[]{:S(2)}, u32[]{:S(2)}) collective-permute-start(bf16[128,1024]{1,0:T(8,128)(2,1)S(1)} %hop.4), channel_id=1, source_target_pairs={{8,16},{12,20},{16,8},{20,12},{9,17},{13,21},{17,9},{21,13},{10,18... | collective-permute-start | bytes 786440 | tf_op jit(solution)/shard_map/ppermute | solution.py:708
  54.0 13.6 %collective-permute-start.12 = (bf16[128,1024]{1,0:T(8,128)(2,1)S(1)}, bf16[128,1024]{1,0:T(8,128)(2,1)S(1)}, u32[]{:S(2)}, u32[]{:S(2)}) collective-permute-start(bf16[128,1024]{1,0:T(8,128)(2,1)S(1)} %hop.6), channel_id=1, source_target_pairs={{16,24},{20,28},{8,0},{12,4},{17,25},{21,29},{9,1},{13,5},{18,26},... | collective-permute-start | bytes 786440 | tf_op jit(solution)/shard_map/ppermute | solution.py:708
  57.7 13.7 %collective-permute-start.16 = (bf16[128,1024]{1,0:T(8,128)(2,1)S(1)}, bf16[128,1024]{1,0:T(8,128)(2,1)S(1)}, u32[]{:S(2)}, u32[]{:S(2)}) collective-permute-start(bf16[128,1024]{1,0:T(8,128)(2,1)S(1)} %hop.7), channel_id=1, source_target_pairs={{16,24},{20,28},{8,0},{12,4},{17,25},{21,29},{9,1},{13,5},{18,26},... | collective-permute-start | bytes 786440 | tf_op jit(solution)/shard_map/ppermute | solution.py:708
  70.7 10.7 %collective-permute-start.17 = (bf16[128,1024]{1,0:T(8,128)(2,1)S(1)}, bf16[128,1024]{1,0:T(8,128)(2,1)S(1)}, u32[]{:S(2)}, u32[]{:S(2)}) collective-permute-start(bf16[128,1024]{1,0:T(8,128)(2,1)S(1)} %get-tuple-element.183), channel_id=1, source_target_pairs={{0,4},{4,0},{8,12},{12,8},{16,20},{20,16},{24,28},{28,24},{1,5},{5... | collective-permute-start | bytes 786440 | tf_op jit(solution)/shard_map/ppermute | solution.py:551
  79.2 10.8 %collective-permute-start.19 = (bf16[128,1024]{1,0:T(8,128)(2,1)S(1)}, bf16[128,1024]{1,0:T(8,128)(2,1)S(1)}, u32[]{:S(2)}, u32[]{:S(2)}) collective-permute-start(bf16[128,1024]{1,0:T(8,128)(2,1)S(1)} %get-tuple-element.228), channel_id=1, source_target_pairs={{0,4},{4,0},{8,12},{12,8},{16,20},{20,16},{24,28},{28,24},{1,5},{5... | collective-permute-start | bytes 786440 | tf_op jit(solution)/shard_map/ppermute | solution.py:551
  82.5 7.4 %collective-permute-start.21 = (bf16[160,256]{1,0:T(8,128)(2,1)S(1)}, bf16[160,256]{1,0:T(8,128)(2,1)S(1)}, u32[]{:S(2)}, u32[]{:S(2)}) collective-permute-start(bf16[160,256]{1,0:T(8,128)(2,1)S(1)} %get-tuple-element.232.refs_0_), channel_id=1, source_target_pairs={{0,1},{1,0},{2,3},{3,2},{4,5},{5,4},{6,7},{7,6},{8,9},{9,8},{10,11... | collective-permute-start | bytes 245768 | tf_op jit(solution)/shard_map/ppermute | solution.py:551
  82.5 7.4 %collective-permute-start.22 = (bf16[160,256]{1,0:T(8,128)(2,1)S(1)}, bf16[160,256]{1,0:T(8,128)(2,1)S(1)}, u32[]{:S(2)}, u32[]{:S(2)}) collective-permute-start(bf16[160,256]{1,0:T(8,128)(2,1)S(1)} %get-tuple-element.232.refs_0_), channel_id=1, source_target_pairs={{0,2},{1,3},{2,0},{3,1},{4,6},{5,7},{6,4},{7,5},{8,10},{9,11},{10,... | collective-permute-start | bytes 245768 | tf_op jit(solution)/shard_map/ppermute | solution.py:551
  83.0 6.9 %collective-permute-start.23 = (bf16[160,256]{1,0:T(8,128)(2,1)S(1)}, bf16[160,256]{1,0:T(8,128)(2,1)S(1)}, u32[]{:S(2)}, u32[]{:S(2)}) collective-permute-start(bf16[160,256]{1,0:T(8,128)(2,1)S(1)} %get-tuple-element.232.refs_0_), channel_id=1, source_target_pairs={{0,3},{1,2},{2,1},{3,0},{4,7},{5,6},{6,5},{7,4},{8,11},{9,10},{10,... | collective-permute-start | bytes 245768 | tf_op jit(solution)/shard_map/ppermute | solution.py:551
  84.4 5.5 %collective-permute-start.20 = (f32[8,256]{1,0:T(8,128)S(1)}, f32[8,256]{1,0:T(8,128)S(1)}, u32[]{:S(2)}, u32[]{:S(2)}) collective-permute-start(f32[8,256]{1,0:T(8,128)S(1)} %get-tuple-element.231), channel_id=1, source_target_pairs={{4,0},{8,4},{12,8},{16,12},{20,16},{24,20},{28,24},{5,1},{9,5},{13... | collective-permute-start | bytes 24584 | tf_op jit(solution)/shard_map/ppermute | solution.py:790
  91.4 19.0 %all-to-all-start = ((bf16[8,144,256]{2,1,0:T(8,128)(2,1)}), bf16[8,144,256]{2,1,0:T(8,128)(2,1)S(1)}, u32[]{:S(2)}, u32[]{:S(2)}) async-start(bf16[8,144,256]{2,1,0:T(8,128)(2,1)} %weight.1), calls=%async_computation | async-start | bytes 1179648 | tf_op jit(solution)/shard_map/all_to_all | solution.py:555
  94.9 13.8 %collective-permute-start.24 = (bf16[128,1024]{1,0:T(8,128)(2,1)}, bf16[128,1024]{1,0:T(8,128)(2,1)S(1)}, u32[]{:S(2)}, u32[]{:S(2)}) collective-permute-start(bf16[128,1024]{1,0:T(8,128)(2,1)} %copy-done.12), channel_id=1, source_target_pairs={{0,4},{4,0},{8,12},{12,8},{16,20},{20,16},{24,28},{28,24},{1,5},{5... | collective-permute-start | bytes 786440 | tf_op jit(solution)/shard_map/ppermute | solution.py:551
  111.3 21.3 %all-to-all-start.1 = ((bf16[8,128,256]{2,1,0:T(8,128)(2,1)}), bf16[8,128,256]{2,1,0:T(8,128)(2,1)S(1)}, u32[]{:S(2)}, u32[]{:S(2)}) async-start(bf16[8,128,256]{2,1,0:T(8,128)(2,1)} %get-tuple-element.240), calls=%async_computation.1 | async-start | bytes 1048576 | tf_op jit(solution)/shard_map/all_to_all | solution.py:555
  115.0 13.6 %collective-permute-start.25 = (bf16[128,1024]{1,0:T(8,128)(2,1)}, bf16[128,1024]{1,0:T(8,128)(2,1)S(1)}, u32[]{:S(2)}, u32[]{:S(2)}) collective-permute-start(bf16[128,1024]{1,0:T(8,128)(2,1)} %copy-done.11), channel_id=1, source_target_pairs={{0,4},{4,0},{8,12},{12,8},{16,20},{20,16},{24,28},{28,24},{1,5},{5... | collective-permute-start | bytes 786440 | tf_op jit(solution)/shard_map/ppermute | solution.py:551
  (17 other events, 117.0 us)

commit v2 on v1

--- a/solution.py
+++ b/solution.py
@@ -521,25 +521,23 @@
         out_ref[:, peer_columns(k, rows)] = dot(g, w_scr[k], NT).astype(BF16)
 
 
-def join_kernel(*refs):
-    own_ref, back_ref = refs[2:4]
-    backs = refs[4 : 4 + 2 * GROUPS]
-    y_ref, dx_ref, raw_ref, sems = refs[4 + 2 * GROUPS :]
+def join_kernel(targets, *refs):
+    blocks = refs[2 : 2 + len(targets)]
+    *outs, sems = refs[2 + len(targets) :]
+    half = outs[0].shape[1] // 2
+    base = (1 - side()) * half
+    pairs = []
+    for block, (which, at) in zip(blocks, targets):
+        pairs.append((block, outs[which].at[:, aligned(base + at, block.shape[1])]))
+    for copy in copy_all(pairs, sems):
+        copy.wait()
+
+
+def join_steps_kernel(own_ref, back_ref, out_ref):
+    heads = own_ref.shape[0]
     r = side()
-    at = (1 - r) * (y_ref.shape[1] // 2)
-    pairs = []
-    for i in range(GROUPS):
-        y, dx = backs[2 * i : 2 * i + 2]
-        columns = aligned(at, y.shape[1])
-        at += y.shape[1]
-        pairs.append((y, y_ref.at[:, columns]))
-        pairs.append((dx, dx_ref.at[:, columns]))
-    copies = copy_all(pairs, sems)
-    heads = own_ref.shape[0]
-    raw_ref[pl.ds(pl.multiple_of(r * heads, 8), heads), :] = own_ref[...]
-    raw_ref[pl.ds(pl.multiple_of((1 - r) * heads, 8), heads), :] = back_ref[...]
-    for copy in copies:
-        copy.wait()
+    out_ref[pl.ds(pl.multiple_of(r * heads, 8), heads), :] = own_ref[...]
+    out_ref[pl.ds(pl.multiple_of((1 - r) * heads, 8), heads), :] = back_ref[...]
 
 
 def pinned(x):
@@ -793,7 +791,7 @@
     rights = [message] + [toggled(message, "fsdp", k) for k in range(fsdp - 1, 0, -1)][::-1]
     terms = call(
         functools.partial(weight_kernel, fsdp), "weight",
-        shape((ctx, chunk_rows + 16, 2 * state), BF16), (), left, after(message, rim, *backs), *rights[1:],
+        shape((ctx, chunk_rows + 16, 2 * state), BF16), (), left, after(message, *backs), *rights[1:],
     )
     backs += [toggled(after(a, terms), "ctx", 1) for a in sends[2:]]
     total, grad_cw, grad_cb, *per_head = call(
@@ -804,7 +802,7 @@
             shape((1, 2 * state), F32),
         ]
         + [shape((1, total_heads), F32)] * 3,
-        (), after(exchanged(terms, "ctx"), *backs[:-1]),
+        (), after(exchanged(terms, "ctx"), rim, *backs[:-1]),
     )
     grad_weight = call(
         place_rows_kernel, "place_rows", shape((rows, 2 * state), F32), (), exchanged(total, "ctx")
@@ -814,10 +812,23 @@
         (), after(grad, total), rim, hbm=pieces,
         scratch=[pltpu.VMEM((fsdp, *w_bc.shape), BF16), pltpu.SemaphoreType.DMA((fsdp,))],
     )
-    ssm_out, grad_values, grad_raw = call(
-        join_kernel, "join", [full, full, shape((total_heads, tokens), F32)],
-        (), raw_own, raw_back, *backs, hbm=finals, hbm_outs=2,
-        aliases={0: 0, 1: 1}, scratch=[pltpu.SemaphoreType.DMA((2 * GROUPS,))],
+    grad_raw = call(
+        join_steps_kernel, "join_steps", shape((total_heads, tokens), F32), (), raw_own,
+        after(raw_back, total),
+    )
+    targets = [(k % 2, ats[k // 2]) for k in range(2 * GROUPS)]
+
+    def join(arrays, which, blocks):
+        return call(
+            functools.partial(join_kernel, [targets[k] for k in which]), "join", [full, full], (),
+            *blocks, hbm=arrays, hbm_outs=2, aliases={0: 0, 1: 1},
+            scratch=[pltpu.SemaphoreType.DMA((len(which),))],
+        )
+
+    early_backs = range(2 * GROUPS - 1)
+    finals = join(finals, early_backs, [after(backs[0], total), *backs[1:-1]])
+    ssm_out, grad_values = join(
+        finals, [2 * GROUPS - 1], [after(backs[-1], grad_tokens, finals[0], grad_raw)]
     )
     return (
         ssm_out[None],

time: 134 us -> 132 us (0.985)
  waiting for transfers between devices: 50.7 us -> 46.3 us
  local copies, waits for them, and re-layouts: 0.69 us -> 2.29 us
    ppermute x18, waiting for transfers between devices: 34.1 us -> 22.1 us  [toggled(): return lax.ppermute(x, axis, [(i, i ^ bits) for i in range(size)])]
    ppermute x1, waiting for transfers between devices: 4.24 us -> 11.8 us  [body(): rim = lax.ppermute(rim_send, 'ctx', [(i + 1, i) for i in range(ctx - 1)])]
    unnamed x26, local copies, waits for them, and re-layouts: 0.69 us -> 2.29 us
    pallas_call x31 -> x33, Pallas kernels: 34.4 us -> 34.9 us  [call(): pl.pallas_call(kernel, out_shape=outs, in_specs=[pl.BlockSpec(memory_spac...]
  transfers between devices with their start and end apart: 28 -> 28, of which waited for: 12 -> 15; matrix products, arithmetic and copies ran while one was open for 0% -> 0% of each run, Pallas kernels for 23% -> 24%
where the time goes in v2:
time: 132 us; the launch traced here: 131 us
  starting transfers between devices  46.9 us (36%)
  waiting for transfers between devices  46.3 us (35%)
  Pallas kernels  34.9 us (26%)
  local copies, waits for them, and re-layouts  2.29 us (2%)
    pallas_call x33, Pallas kernels, call(): pl.pallas_call(kernel, out_shape=outs, in_specs=[pl.BlockSpec(memory_spac...  34.9 us
    ppermute x18, starting transfers between devices, toggled(): return lax.ppermute(x, axis, [(i, i ^ bits) for i in range(size)])  23.7 us
    ppermute x18, waiting for transfers between devices, toggled(): return lax.ppermute(x, axis, [(i, i ^ bits) for i in range(size)])  22.1 us
    ppermute x6, starting transfers between devices, body(): received[i].append(lax.ppermute(value, 'ctx', moves))  12.3 us
    ppermute x1, waiting for transfers between devices, body(): rim = lax.ppermute(rim_send, 'ctx', [(i + 1, i) for i in range(ctx - 1)])  11.8 us
    ppermute x6, waiting for transfers between devices, body(): received[i].append(lax.ppermute(value, 'ctx', moves))  10.2 us
    all_to_all x2, starting transfers between devices, exchanged(): return lax.all_to_all(x, axis, 0, 0)  7.11 us
  transfers between devices with their start and end apart: 28, of which 15 were waited for; matrix products, arithmetic and copies ran while one was open for 0% of the time, Pallas kernels for 24%

profile of v2, /device:TPU:0, one launch (start us, length us, event | category | flops | bytes accessed | tf_op | source)
XLA Modules:
  0.0 131.5 jit_solution(11824174582886445682)
XLA Ops:
  0.6 3.0 %collective-permute-start = (f32[32,128]{1,0:T(8,128)}, f32[32,128]{1,0:T(8,128)S(1)}, u32[]{:S(2)}, u32[]{:S(2)}) collective-permute-start(f32[32,128]{1,0:T(8,128)} %bitcast.33), channel_id=1, source_target_pairs={{0,4},{4,0},{8,12},{12,8},{16,20},{20,16},{24,28},{28,24},{1,5},{5... | collective-permute-start | bytes 49160 | tf_op jit(solution)/shard_map/ppermute | solution.py:549
  9.1 2.4 %collective-permute-start.4 = (bf16[16,4096]{1,0:T(8,128)(2,1)S(1)}, bf16[16,4096]{1,0:T(8,128)(2,1)S(1)}, u32[]{:S(2)}, u32[]{:S(2)}) collective-permute-start(bf16[16,4096]{1,0:T(8,128)(2,1)S(1)} %get-tuple-element.135), channel_id=1, source_target_pairs={{0,4},{4,8},{8,12},{12,16},{16,20},{20,24},{24,28},{1,5},{5,9},{9,... | collective-permute-start | bytes 393224 | tf_op jit(solution)/shard_map/ppermute | solution.py:588
  14.5 5.1 %collective-permute-done.1.x_ref.g_ref.refs_2_.refs_3_ = bf16[128,2048]{1,0:T(8,128)(2,1)S(1)} collective-permute-done((bf16[128,2048]{1,0:T(8,128)(2,1)S(1)}, bf16[128,2048]{1,0:T(8,128)(2,1)S(1)}, u32[]{:S(2)}, u32[]{:S(2)}) %collective-permute-start.1) | collective-permute-done | bytes 524320 | tf_op jit(solution)/shard_map/ppermute | solution.py:549
  23.4 2.1 %project.1 = (f32[272,256]{1,0:T(8,128)S(1)}, bf16[128,256]{1,0:T(8,128)(2,1)S(1)}) custom-call(bf16[128,4096]{1,0:T(8,128)(2,1)} %bitcast.41, bf16[1024,256]{1,0:T(8,128)(2,1)S(1)} %copy-done.2, bf16[1024,256]{1,0:T(8,128)(2,1)S(1)} %collective-permute-done.2.refs_1_, bf16[1024,256]{1,0:T(8,128)(2,1)S(1)} %collective-permute-done.3.refs_2_, ...), custom_call_target="tpu_custom_call" | custom-call | tf_op jit(solution)/shard_map/project/pallas_call | solution.py:37
  25.5 2.5 %collective-permute-start.6 = (bf16[128,256]{1,0:T(8,128)(2,1)S(1)}, bf16[128,256]{1,0:T(8,128)(2,1)S(1)}, u32[]{:S(2)}, u32[]{:S(2)}) collective-permute-start(bf16[128,256]{1,0:T(8,128)(2,1)S(1)} %get-tuple-element.192.bc_ref.bc0_ref.refs_4_.refs_6_), channel_id=1, source_target_pairs={{0,4},{4,0},{8,12},{12,8},{16,20},{20,16},{24,28},{28,24},{1,5},{5... | collective-permute-start | bytes 196616 | tf_op jit(solution)/shard_map/ppermute | solution.py:549
  28.1 2.2 %inside.4 = (f32[128,1024]{1,0:T(8,128)S(1)}, f32[128,1024]{1,0:T(8,128)S(1)}, f32[128,128]{1,0:T(8,128)S(1)}, f32[128,128]{1,0:T(8,128)S(1)}, f32[128,128]{1,0:T(8,128)S(1)}, /*index=5*/f32[8,128]{1,0:T(8,128)S(1)}) custom-call(f32[32]{0:T(128)S(1)} %copy-done.7, bf16[128,4096]{1,0:T(8,128)(2,1)S(1)} %bitcast.22, bf16[128,4096]{1,0:T(8,128)(2,1)S(1)} %bitcast.29, ...), custom_call_target="tpu_custom_call" | custom-call | tf_op jit(solution)/shard_map/inside/pallas_call | solution.py:37
  30.5 2.5 %collective-permute-start.9 = (bf16[128,1024]{1,0:T(8,128)(2,1)S(1)}, bf16[128,1024]{1,0:T(8,128)(2,1)S(1)}, u32[]{:S(2)}, u32[]{:S(2)}) collective-permute-start(bf16[128,1024]{1,0:T(8,128)(2,1)S(1)} %get-tuple-element.163), channel_id=1, source_target_pairs={{0,4},{4,0},{8,12},{12,8},{16,20},{20,16},{24,28},{28,24},{1,5},{5... | collective-permute-start | bytes 786440 | tf_op jit(solution)/shard_map/ppermute | solution.py:549
  33.8 3.4 %collective-permute-start.7 = (bf16[128,1024]{1,0:T(8,128)(2,1)S(1)}, bf16[128,1024]{1,0:T(8,128)(2,1)S(1)}, u32[]{:S(2)}, u32[]{:S(2)}) collective-permute-start(bf16[128,1024]{1,0:T(8,128)(2,1)S(1)} %get-tuple-element.158), channel_id=1, source_target_pairs={{0,8},{4,12},{24,16},{28,20},{1,9},{5,13},{25,17},{29,21},{2,10},{... | collective-permute-start | bytes 786440 | tf_op jit(solution)/shard_map/ppermute | solution.py:706
  37.1 2.2 %inside.5 = (f32[128,1024]{1,0:T(8,128)S(1)}, f32[128,1024]{1,0:T(8,128)S(1)}, f32[128,128]{1,0:T(8,128)S(1)}, f32[128,128]{1,0:T(8,128)S(1)}, f32[128,128]{1,0:T(8,128)S(1)}, /*index=5*/f32[8,128]{1,0:T(8,128)S(1)}) custom-call(f32[32]{0:T(128)S(1)} %copy-done.7, bf16[128,4096]{1,0:T(8,128)(2,1)S(1)} %bitcast.23, bf16[128,4096]{1,0:T(8,128)(2,1)S(1)} %bitcast.30, ...), custom_call_target="tpu_custom_call" | custom-call | tf_op jit(solution)/shard_map/inside/pallas_call | solution.py:37
  39.4 2.4 %collective-permute-done.9.g_ref.refs_5_ = bf16[128,1024]{1,0:T(8,128)(2,1)S(1)} collective-permute-done((bf16[128,1024]{1,0:T(8,128)(2,1)S(1)}, bf16[128,1024]{1,0:T(8,128)(2,1)S(1)}, u32[]{:S(2)}, u32[]{:S(2)}) %collective-permute-start.9) | collective-permute-done | bytes 262176 | tf_op jit(solution)/shard_map/ppermute | solution.py:549
  43.0 5.0 %collective-permute-start.11 = (bf16[128,1024]{1,0:T(8,128)(2,1)S(1)}, bf16[128,1024]{1,0:T(8,128)(2,1)S(1)}, u32[]{:S(2)}, u32[]{:S(2)}) collective-permute-start(bf16[128,1024]{1,0:T(8,128)(2,1)S(1)} %get-tuple-element.169), channel_id=1, source_target_pairs={{0,8},{4,12},{24,16},{28,20},{1,9},{5,13},{25,17},{29,21},{2,10},{... | collective-permute-start | bytes 786440 | tf_op jit(solution)/shard_map/ppermute | solution.py:706
  48.9 2.3 %inside.6 = (f32[128,1024]{1,0:T(8,128)S(1)}, f32[128,1024]{1,0:T(8,128)S(1)}, f32[128,128]{1,0:T(8,128)S(1)}, f32[128,128]{1,0:T(8,128)S(1)}, f32[128,128]{1,0:T(8,128)S(1)}, /*index=5*/f32[8,128]{1,0:T(8,128)S(1)}) custom-call(f32[32]{0:T(128)S(1)} %copy-done.7, bf16[128,2048]{1,0:T(8,128)(2,1)S(1)} %collective-permute-done.1.x_ref.g_ref.refs_2_.refs_3_, ...), custom_call_target="tpu_custom_call" | custom-call | tf_op jit(solution)/shard_map/inside/pallas_call | solution.py:37
  55.3 2.3 %inside.7 = (f32[128,1024]{1,0:T(8,128)S(1)}, f32[128,1024]{1,0:T(8,128)S(1)}, f32[128,128]{1,0:T(8,128)S(1)}, f32[128,128]{1,0:T(8,128)S(1)}, f32[128,128]{1,0:T(8,128)S(1)}, /*index=5*/f32[8,128]{1,0:T(8,128)S(1)}) custom-call(f32[32]{0:T(128)S(1)} %copy-done.7, bf16[128,1024]{1,0:T(8,128)(2,1)S(1)} %collective-permute-done.8.x_ref.refs_4_, ...), custom_call_target="tpu_custom_call" | custom-call | tf_op jit(solution)/shard_map/inside/pallas_call | solution.py:37
  59.2 8.4 %collective-permute-done.12.refs_25_ = bf16[128,1024]{1,0:T(8,128)(2,1)S(1)} collective-permute-done((bf16[128,1024]{1,0:T(8,128)(2,1)S(1)}, bf16[128,1024]{1,0:T(8,128)(2,1)S(1)}, u32[]{:S(2)}, u32[]{:S(2)}) %collective-permute-start.12) | collective-permute-done | bytes 262176 | tf_op jit(solution)/shard_map/ppermute | solution.py:706
  67.5 3.1 %across.2 = (bf16[128,4096]{1,0:T(8,128)(2,1)}, bf16[128,4096]{1,0:T(8,128)(2,1)}, bf16[128,1024]{1,0:T(8,128)(2,1)S(1)}, bf16[128,1024]{1,0:T(8,128)(2,1)S(1)},...) custom-call(bf16[128,4096]{1,0:T(8,128)(2,1)S(1)} %bitcast.24, ...), custom_call_target="tpu_custom_call" | custom-call | tf_op jit(solution)/shard_map/across/pallas_call | solution.py:37
  71.4 3.0 %across.3 = (bf16[128,4096]{1,0:T(8,128)(2,1)}, bf16[128,4096]{1,0:T(8,128)(2,1)}, bf16[128,1024]{1,0:T(8,128)(2,1)S(1)}, bf16[128,1024]{1,0:T(8,128)(2,1)S(1)},...) custom-call(bf16[128,4096]{1,0:T(8,128)(2,1)} %get-tuple-element.185, ...), custom_call_target="tpu_custom_call", output_to_operand_aliasing={{0}: (0, {}), {1}: (1, {})} | custom-call | tf_op jit(solution)/shard_map/across/pallas_call | solution.py:37
  77.2 2.7 %collective-permute-done.18.ret_ref = bf16[144,256]{1,0:T(8,128)(2,1)S(1)} collective-permute-done((bf16[144,256]{1,0:T(8,128)(2,1)S(1)}, bf16[144,256]{1,0:T(8,128)(2,1)S(1)}, u32[]{:S(2)}, u32[]{:S(2)}) %collective-permute-start.18) | collective-permute-done | bytes 73760 | tf_op jit(solution)/shard_map/ppermute | solution.py:549
  79.9 2.5 %collective-permute-start.19 = (bf16[128,1024]{1,0:T(8,128)(2,1)S(1)}, bf16[128,1024]{1,0:T(8,128)(2,1)S(1)}, u32[]{:S(2)}, u32[]{:S(2)}) collective-permute-start(bf16[128,1024]{1,0:T(8,128)(2,1)S(1)} %get-tuple-element.231), channel_id=1, source_target_pairs={{0,4},{4,0},{8,12},{12,8},{16,20},{20,16},{24,28},{28,24},{1,5},{5... | collective-permute-start | bytes 786440 | tf_op jit(solution)/shard_map/ppermute | solution.py:549
  91.1 3.5 %all-to-all-start = ((bf16[8,144,256]{2,1,0:T(8,128)(2,1)}), bf16[8,144,256]{2,1,0:T(8,128)(2,1)S(1)}, u32[]{:S(2)}, u32[]{:S(2)}) async-start(bf16[8,144,256]{2,1,0:T(8,128)(2,1)} %weight.1), calls=%async_computation | async-start | bytes 1179648 | tf_op jit(solution)/shard_map/all_to_all | solution.py:553
  97.9 11.8 %collective-permute-done.23.refs_5_ = f32[8,256]{1,0:T(8,128)S(1)} collective-permute-done((f32[8,256]{1,0:T(8,128)S(1)}, f32[8,256]{1,0:T(8,128)S(1)}, u32[]{:S(2)}, u32[]{:S(2)}) %collective-permute-start.23) | collective-permute-done | bytes 8224 | tf_op jit(solution)/shard_map/ppermute | solution.py:788
  112.2 3.6 %all-to-all-start.1 = ((bf16[8,128,256]{2,1,0:T(8,128)(2,1)}), bf16[8,128,256]{2,1,0:T(8,128)(2,1)S(1)}, u32[]{:S(2)}, u32[]{:S(2)}) async-start(bf16[8,128,256]{2,1,0:T(8,128)(2,1)} %get-tuple-element.237), calls=%async_computation.1 | async-start | bytes 1048576 | tf_op jit(solution)/shard_map/all_to_all | solution.py:553
  115.7 2.0 %collective-permute-start.25 = (bf16[128,1024]{1,0:T(8,128)(2,1)}, bf16[128,1024]{1,0:T(8,128)(2,1)S(1)}, u32[]{:S(2)}, u32[]{:S(2)}) collective-permute-start(bf16[128,1024]{1,0:T(8,128)(2,1)} %copy-done.11), channel_id=1, source_target_pairs={{0,4},{4,0},{8,12},{12,8},{16,20},{20,16},{24,28},{28,24},{1,5},{5... | collective-permute-start | bytes 786440 | tf_op jit(solution)/shard_map/ppermute | solution.py:549
  119.3 2.4 %grad_tokens.1 = bf16[128,4096]{1,0:T(8,128)(2,1)} custom-call(bf16[1024,256]{1,0:T(8,128)(2,1)S(1)} %copy-done.2, bf16[1024,256]{1,0:T(8,128)(2,1)S(1)} %collective-permute-done.2.refs_1_, bf16[1024,256]{1,0:T(8,128)(2,1)S(1)} %collective-permute-done.3.refs_2_, bf16[1024,256]{1,0:T(8,128)(2,1)S(1)} %collective-permute-done.5.refs_3_, ...), custom_call_target="tpu_custom_call" | custom-call | tf_op jit(solution)/shard_map/grad_tokens/pallas_call | solution.py:37
  122.6 6.9 %collective-permute-done.25.refs_2_ = bf16[128,1024]{1,0:T(8,128)(2,1)S(1)} collective-permute-done((bf16[128,1024]{1,0:T(8,128)(2,1)}, bf16[128,1024]{1,0:T(8,128)(2,1)S(1)}, u32[]{:S(2)}, u32[]{:S(2)}) %collective-permute-start.25) | collective-permute-done | bytes 262176 | tf_op jit(solution)/shard_map/ppermute | solution.py:549
  (91 shorter events, 43.1 us)
Async XLA Ops:
  0.6 4.9 %collective-permute-start = (f32[32,128]{1,0:T(8,128)}, f32[32,128]{1,0:T(8,128)S(1)}, u32[]{:S(2)}, u32[]{:S(2)}) collective-permute-start(f32[32,128]{1,0:T(8,128)} %bitcast.33), channel_id=1, source_target_pairs={{0,4},{4,0},{8,12},{12,8},{16,20},{20,16},{24,28},{28,24},{1,5},{5... | collective-permute-start | bytes 49160 | tf_op jit(solution)/shard_map/ppermute | solution.py:549
  3.6 9.2 %collective-permute-start.2 = (bf16[1024,256]{1,0:T(8,128)(2,1)}, bf16[1024,256]{1,0:T(8,128)(2,1)S(1)}, u32[]{:S(2)}, u32[]{:S(2)}) collective-permute-start(bf16[1024,256]{1,0:T(8,128)(2,1)} %refs_0_.5), channel_id=1, source_target_pairs={{0,1},{1,0},{2,3},{3,2},{4,5},{5,4},{6,7},{7,6},{8,9},{9,8},{10,11... | collective-permute-start | bytes 1572872 | tf_op jit(solution)/shard_map/ppermute | solution.py:549
  5.6 14.0 %collective-permute-start.1 = (bf16[128,2048]{1,0:T(8,128)(2,1)S(1)}, bf16[128,2048]{1,0:T(8,128)(2,1)S(1)}, u32[]{:S(2)}, u32[]{:S(2)}) collective-permute-start(bf16[128,2048]{1,0:T(8,128)(2,1)S(1)} %get-tuple-element.134), channel_id=1, source_target_pairs={{0,4},{4,0},{8,12},{12,8},{16,20},{20,16},{24,28},{28,24},{1,5},{5... | collective-permute-start | bytes 1572872 | tf_op jit(solution)/shard_map/ppermute | solution.py:549
  7.6 12.8 %collective-permute-start.3 = (bf16[1024,256]{1,0:T(8,128)(2,1)S(1)}, bf16[1024,256]{1,0:T(8,128)(2,1)S(1)}, u32[]{:S(2)}, u32[]{:S(2)}) collective-permute-start(bf16[1024,256]{1,0:T(8,128)(2,1)S(1)} %copy-done.2), channel_id=1, source_target_pairs={{0,2},{1,3},{2,0},{3,1},{4,6},{5,7},{6,4},{7,5},{8,10},{9,11},{10,... | collective-permute-start | bytes 1572872 | tf_op jit(solution)/shard_map/ppermute | solution.py:549
  9.1 11.3 %collective-permute-start.4 = (bf16[16,4096]{1,0:T(8,128)(2,1)S(1)}, bf16[16,4096]{1,0:T(8,128)(2,1)S(1)}, u32[]{:S(2)}, u32[]{:S(2)}) collective-permute-start(bf16[16,4096]{1,0:T(8,128)(2,1)S(1)} %get-tuple-element.135), channel_id=1, source_target_pairs={{0,4},{4,8},{8,12},{12,16},{16,20},{20,24},{24,28},{1,5},{5,9},{9,... | collective-permute-start | bytes 393224 | tf_op jit(solution)/shard_map/ppermute | solution.py:588
  21.7 26.2 %collective-permute-start.13 = (bf16[2,144,1024]{2,1,0:T(8,128)(2,1)S(1)}, bf16[2,144,1024]{2,1,0:T(8,128)(2,1)S(1)}, u32[]{:S(2)}, u32[]{:S(2)}) collective-permute-start(bf16[2,144,1024]{2,1,0:T(8,128)(2,1)S(1)} %get-tuple-element.190), channel_id=1, source_target_pairs={{0,2},{1,3},{2,0},{3,1},{4,6},{5,7},{6,4},{7,5},{8,10},{9,11},{10,... | collective-permute-start | bytes 1769480 | tf_op jit(solution)/shard_map/ppermute | solution.py:549
  25.5 5.0 %collective-permute-start.6 = (bf16[128,256]{1,0:T(8,128)(2,1)S(1)}, bf16[128,256]{1,0:T(8,128)(2,1)S(1)}, u32[]{:S(2)}, u32[]{:S(2)}) collective-permute-start(bf16[128,256]{1,0:T(8,128)(2,1)S(1)} %get-tuple-element.192.bc_ref.bc0_ref.refs_4_.refs_6_), channel_id=1, source_target_pairs={{0,4},{4,0},{8,12},{12,8},{16,20},{20,16},{24,28},{28,24},{1,5},{5... | collective-permute-start | bytes 196616 | tf_op jit(solution)/shard_map/ppermute | solution.py:549
  28.0 11.3 %collective-permute-start.8 = (bf16[128,1024]{1,0:T(8,128)(2,1)S(1)}, bf16[128,1024]{1,0:T(8,128)(2,1)S(1)}, u32[]{:S(2)}, u32[]{:S(2)}) collective-permute-start(bf16[128,1024]{1,0:T(8,128)(2,1)S(1)} %get-tuple-element.161), channel_id=1, source_target_pairs={{0,4},{4,0},{8,12},{12,8},{16,20},{20,16},{24,28},{28,24},{1,5},{5... | collective-permute-start | bytes 786440 | tf_op jit(solution)/shard_map/ppermute | solution.py:549
  30.5 11.3 %collective-permute-start.9 = (bf16[128,1024]{1,0:T(8,128)(2,1)S(1)}, bf16[128,1024]{1,0:T(8,128)(2,1)S(1)}, u32[]{:S(2)}, u32[]{:S(2)}) collective-permute-start(bf16[128,1024]{1,0:T(8,128)(2,1)S(1)} %get-tuple-element.163), channel_id=1, source_target_pairs={{0,4},{4,0},{8,12},{12,8},{16,20},{20,16},{24,28},{28,24},{1,5},{5... | collective-permute-start | bytes 786440 | tf_op jit(solution)/shard_map/ppermute | solution.py:549
  33.8 14.3 %collective-permute-start.7 = (bf16[128,1024]{1,0:T(8,128)(2,1)S(1)}, bf16[128,1024]{1,0:T(8,128)(2,1)S(1)}, u32[]{:S(2)}, u32[]{:S(2)}) collective-permute-start(bf16[128,1024]{1,0:T(8,128)(2,1)S(1)} %get-tuple-element.158), channel_id=1, source_target_pairs={{0,8},{4,12},{24,16},{28,20},{1,9},{5,13},{25,17},{29,21},{2,10},{... | collective-permute-start | bytes 786440 | tf_op jit(solution)/shard_map/ppermute | solution.py:706
  43.0 10.1 %collective-permute-start.11 = (bf16[128,1024]{1,0:T(8,128)(2,1)S(1)}, bf16[128,1024]{1,0:T(8,128)(2,1)S(1)}, u32[]{:S(2)}, u32[]{:S(2)}) collective-permute-start(bf16[128,1024]{1,0:T(8,128)(2,1)S(1)} %get-tuple-element.169), channel_id=1, source_target_pairs={{0,8},{4,12},{24,16},{28,20},{1,9},{5,13},{25,17},{29,21},{2,10},{... | collective-permute-start | bytes 786440 | tf_op jit(solution)/shard_map/ppermute | solution.py:706
  48.0 22.9 %collective-permute-start.14 = (bf16[2,144,1024]{2,1,0:T(8,128)(2,1)S(1)}, bf16[2,144,1024]{2,1,0:T(8,128)(2,1)S(1)}, u32[]{:S(2)}, u32[]{:S(2)}) collective-permute-start(bf16[2,144,1024]{2,1,0:T(8,128)(2,1)S(1)} %relay.1), channel_id=1, source_target_pairs={{0,1},{1,0},{2,3},{3,2},{4,5},{5,4},{6,7},{7,6},{8,9},{9,8},{10,11... | collective-permute-start | bytes 1769480 | tf_op jit(solution)/shard_map/ppermute | solution.py:549
  48.2 5.6 %collective-permute-start.10 = (bf16[128,1024]{1,0:T(8,128)(2,1)S(1)}, bf16[128,1024]{1,0:T(8,128)(2,1)S(1)}, u32[]{:S(2)}, u32[]{:S(2)}) collective-permute-start(bf16[128,1024]{1,0:T(8,128)(2,1)S(1)} %hop.4), channel_id=1, source_target_pairs={{8,16},{12,20},{16,8},{20,12},{9,17},{13,21},{17,9},{21,13},{10,18... | collective-permute-start | bytes 786440 | tf_op jit(solution)/shard_map/ppermute | solution.py:706
  54.0 13.6 %collective-permute-start.12 = (bf16[128,1024]{1,0:T(8,128)(2,1)S(1)}, bf16[128,1024]{1,0:T(8,128)(2,1)S(1)}, u32[]{:S(2)}, u32[]{:S(2)}) collective-permute-start(bf16[128,1024]{1,0:T(8,128)(2,1)S(1)} %hop.6), channel_id=1, source_target_pairs={{16,24},{20,28},{8,0},{12,4},{17,25},{21,29},{9,1},{13,5},{18,26},... | collective-permute-start | bytes 786440 | tf_op jit(solution)/shard_map/ppermute | solution.py:706
  57.6 13.7 %collective-permute-start.16 = (bf16[128,1024]{1,0:T(8,128)(2,1)S(1)}, bf16[128,1024]{1,0:T(8,128)(2,1)S(1)}, u32[]{:S(2)}, u32[]{:S(2)}) collective-permute-start(bf16[128,1024]{1,0:T(8,128)(2,1)S(1)} %hop.7), channel_id=1, source_target_pairs={{16,24},{20,28},{8,0},{12,4},{17,25},{21,29},{9,1},{13,5},{18,26},... | collective-permute-start | bytes 786440 | tf_op jit(solution)/shard_map/ppermute | solution.py:706
  70.7 11.7 %collective-permute-start.17 = (bf16[128,1024]{1,0:T(8,128)(2,1)S(1)}, bf16[128,1024]{1,0:T(8,128)(2,1)S(1)}, u32[]{:S(2)}, u32[]{:S(2)}) collective-permute-start(bf16[128,1024]{1,0:T(8,128)(2,1)S(1)} %get-tuple-element.187), channel_id=1, source_target_pairs={{0,4},{4,0},{8,12},{12,8},{16,20},{20,16},{24,28},{28,24},{1,5},{5... | collective-permute-start | bytes 786440 | tf_op jit(solution)/shard_map/ppermute | solution.py:549
  79.9 6.8 %collective-permute-start.19 = (bf16[128,1024]{1,0:T(8,128)(2,1)S(1)}, bf16[128,1024]{1,0:T(8,128)(2,1)S(1)}, u32[]{:S(2)}, u32[]{:S(2)}) collective-permute-start(bf16[128,1024]{1,0:T(8,128)(2,1)S(1)} %get-tuple-element.231), channel_id=1, source_target_pairs={{0,4},{4,0},{8,12},{12,8},{16,20},{20,16},{24,28},{28,24},{1,5},{5... | collective-permute-start | bytes 786440 | tf_op jit(solution)/shard_map/ppermute | solution.py:549
  83.5 5.2 %collective-permute-start.21 = (bf16[160,256]{1,0:T(8,128)(2,1)S(1)}, bf16[160,256]{1,0:T(8,128)(2,1)S(1)}, u32[]{:S(2)}, u32[]{:S(2)}) collective-permute-start(bf16[160,256]{1,0:T(8,128)(2,1)S(1)} %get-tuple-element.232.refs_0_), channel_id=1, source_target_pairs={{0,2},{1,3},{2,0},{3,1},{4,6},{5,7},{6,4},{7,5},{8,10},{9,11},{10,... | collective-permute-start | bytes 245768 | tf_op jit(solution)/shard_map/ppermute | solution.py:549
  84.0 5.7 %collective-permute-start.22 = (bf16[160,256]{1,0:T(8,128)(2,1)S(1)}, bf16[160,256]{1,0:T(8,128)(2,1)S(1)}, u32[]{:S(2)}, u32[]{:S(2)}) collective-permute-start(bf16[160,256]{1,0:T(8,128)(2,1)S(1)} %get-tuple-element.232.refs_0_), channel_id=1, source_target_pairs={{0,3},{1,2},{2,1},{3,0},{4,7},{5,6},{6,5},{7,4},{8,11},{9,10},{10,... | collective-permute-start | bytes 245768 | tf_op jit(solution)/shard_map/ppermute | solution.py:549
  91.1 20.1 %all-to-all-start = ((bf16[8,144,256]{2,1,0:T(8,128)(2,1)}), bf16[8,144,256]{2,1,0:T(8,128)(2,1)S(1)}, u32[]{:S(2)}, u32[]{:S(2)}) async-start(bf16[8,144,256]{2,1,0:T(8,128)(2,1)} %weight.1), calls=%async_computation | async-start | bytes 1179648 | tf_op jit(solution)/shard_map/all_to_all | solution.py:553
  94.6 15.0 %collective-permute-start.24 = (bf16[128,1024]{1,0:T(8,128)(2,1)}, bf16[128,1024]{1,0:T(8,128)(2,1)S(1)}, u32[]{:S(2)}, u32[]{:S(2)}) collective-permute-start(bf16[128,1024]{1,0:T(8,128)(2,1)} %copy-done.12), channel_id=1, source_target_pairs={{0,4},{4,0},{8,12},{12,8},{16,20},{20,16},{24,28},{28,24},{1,5},{5... | collective-permute-start | bytes 786440 | tf_op jit(solution)/shard_map/ppermute | solution.py:549
  96.6 13.1 %collective-permute-start.23 = (f32[8,256]{1,0:T(8,128)S(1)}, f32[8,256]{1,0:T(8,128)S(1)}, u32[]{:S(2)}, u32[]{:S(2)}) collective-permute-start(f32[8,256]{1,0:T(8,128)S(1)} %get-tuple-element.233), channel_id=1, source_target_pairs={{4,0},{8,4},{12,8},{16,12},{20,16},{24,20},{28,24},{5,1},{9,5},{13... | collective-permute-start | bytes 24584 | tf_op jit(solution)/shard_map/ppermute | solution.py:788
  112.2 18.3 %all-to-all-start.1 = ((bf16[8,128,256]{2,1,0:T(8,128)(2,1)}), bf16[8,128,256]{2,1,0:T(8,128)(2,1)S(1)}, u32[]{:S(2)}, u32[]{:S(2)}) async-start(bf16[8,128,256]{2,1,0:T(8,128)(2,1)} %get-tuple-element.237), calls=%async_computation.1 | async-start | bytes 1048576 | tf_op jit(solution)/shard_map/all_to_all | solution.py:553
  115.7 13.8 %collective-permute-start.25 = (bf16[128,1024]{1,0:T(8,128)(2,1)}, bf16[128,1024]{1,0:T(8,128)(2,1)S(1)}, u32[]{:S(2)}, u32[]{:S(2)}) collective-permute-start(bf16[128,1024]{1,0:T(8,128)(2,1)} %copy-done.11), channel_id=1, source_target_pairs={{0,4},{4,0},{8,12},{12,8},{16,20},{20,16},{24,28},{28,24},{1,5},{5... | collective-permute-start | bytes 786440 | tf_op jit(solution)/shard_map/ppermute | solution.py:549
  (17 other events, 92.3 us)

commit v3 on v2

--- a/solution.py
+++ b/solution.py
@@ -281,23 +281,12 @@
         outs[slot][:, LANES:] = dot(ds, bc_ref[:, :LANES])
 
 
-def across_kernel(heads, lanes, hops, filled, own_at, columns, *refs):
-    refs = refs[2 * filled :]
-    across_block(heads, lanes, hops, own_at, columns, *refs)
-
-
-def across_block(
-    heads, lanes, hops, own_at, columns, x0_ref, g0_ref, x1_ref, g1_ref, bc0_ref, bc1_ref, xe0_ref,
-    ge0_ref, xe1_ref, ge1_ref, step_ref, grow_ref, endw_ref, dec_ref, p_ref, sf_ref, ds_ref,
-    y0_ref, dx0_ref, y1_ref, dx1_ref, dbc0_ref, dbc1_ref, *refs
+def enter_kernel(
+    hops, xe0_ref, ge0_ref, xe1_ref, ge1_ref, dec_ref, p_ref, sf_ref, ds_ref, dbc0_ref, dbc1_ref, *refs
 ):
     received = refs[:hops]
-    (
-        yf_ref, dxf_ref, ys_ref, dxs_ref, dbco0_ref, dbco1_ref, u_ref, t_ref, re_ref,
-        e_in, r_in, e_scr, r_scr, n_scr, yo_ref, dxo_ref, sems,
-    ) = refs[hops:]
+    e_ref, r_ref, n_ref, dbco0_ref, dbco1_ref, e_in, r_in = refs[hops:]
     r, pos = side(), place()
-    width = yo_ref.shape[1]
     e_in[...] = jnp.zeros_like(e_in)
     r_in[...] = jnp.zeros_like(r_in)
     for k in range(hops):
@@ -316,28 +305,41 @@
     middle = dec_first * entering + sf_ref[...].astype(F32)
     leaving = dec_pair * entering + p_ref[...].astype(F32)
     earlier = dec_second * later + ds_ref[...].astype(F32)
-    e_scr[r] = e_in[...]
-    e_scr[1 - r] = middle.astype(BF16)
-    r_scr[1 - r] = r_in[...]
-    r_scr[r] = earlier.astype(BF16)
-    n_scr[1 - r] = jnp.sum(later * leaving, axis=0, keepdims=True)
-    n_scr[r] = jnp.sum(earlier * middle, axis=0, keepdims=True)
-
+    e_ref[r] = e_in[...]
+    e_ref[1 - r] = middle.astype(BF16)
+    r_ref[1 - r] = r_in[...]
+    r_ref[r] = earlier.astype(BF16)
+    n_ref[1 - r] = jnp.sum(later * leaving, axis=0, keepdims=True)
+    n_ref[r] = jnp.sum(earlier * middle, axis=0, keepdims=True)
+    for slot, (xe_ref, ge_ref, dbc_ref, dbco_ref) in enumerate(
+        ((xe0_ref, ge0_ref, dbc0_ref, dbco0_ref), (xe1_ref, ge1_ref, dbc1_ref, dbco1_ref))
+    ):
+        db = dbc_ref[:, :LANES] + dot(xe_ref[...], r_ref[slot], NT)
+        dc = dbc_ref[:, LANES:] + dot(ge_ref[...], e_ref[slot], NT)
+        dbco_ref[:, :LANES] = db.astype(dbco_ref.dtype)
+        dbco_ref[:, LANES:] = dc.astype(dbco_ref.dtype)
+
+
+def across_kernel(heads, lanes, filled, own_at, columns, *refs):
+    refs = refs[2 * filled :]
+    across_block(heads, lanes, own_at, columns, *refs)
+
+
+def across_block(
+    heads, lanes, own_at, columns, x0_ref, g0_ref, x1_ref, g1_ref, bc0_ref, bc1_ref, step_ref,
+    grow_ref, endw_ref, e_ref, r_ref, n_ref, y0_ref, dx0_ref, y1_ref, dx1_ref, yf_ref, dxf_ref,
+    ys_ref, dxs_ref, u_ref, t_ref, re_ref, yo_ref, dxo_ref, sems
+):
+    r = side()
+    width, cut = yo_ref.shape[1], ys_ref.shape[1]
     u_ref[...] = jnp.zeros_like(u_ref)
     t_ref[...] = jnp.zeros_like(t_ref)
     re_ref[...] = jnp.zeros_like(re_ref)
-    for slot, (bc_ref, xe_ref, ge_ref, y_ref, dx_ref, dbc_ref, dbco_ref) in enumerate(
-        (
-            (bc0_ref, xe0_ref, ge0_ref, y0_ref, dx0_ref, dbc0_ref, dbco0_ref),
-            (bc1_ref, xe1_ref, ge1_ref, y1_ref, dx1_ref, dbc1_ref, dbco1_ref),
-        )
+    for slot, (bc_ref, y_ref, dx_ref) in enumerate(
+        ((bc0_ref, y0_ref, dx0_ref), (bc1_ref, y1_ref, dx1_ref))
     ):
-        e_all = e_scr[slot]
-        r_all = r_scr[slot]
-        db = dbc_ref[:, :LANES] + dot(xe_ref[...], r_all, NT)
-        dc = dbc_ref[:, LANES:] + dot(ge_ref[...], e_all, NT)
-        dbco_ref[:, :LANES] = db.astype(dbco_ref.dtype)
-        dbco_ref[:, LANES:] = dc.astype(dbco_ref.dtype)
+        e_all = e_ref[slot]
+        r_all = r_ref[slot]
         ce_all = dot(bc_ref[:, LANES:], e_all)
         br_all = dot(bc_ref[:, :LANES], r_all)
         for h in range(heads):
@@ -353,13 +355,17 @@
                 x = x0_ref[:, head_columns(own_at, h)].astype(F32)
                 g = g0_ref[:, head_columns(own_at, h)].astype(F32)
             else:
-                ys_ref[:, at] = y
-                dxs_ref[:, at] = dx
+                first = h * LANES
+                if first < cut:
+                    ys_ref[:, at] = y
+                else:
+                    dxs_ref[:, first - cut : first - cut + LANES] = y
+                dxs_ref[:, first + width - cut : first + width - cut + LANES] = dx
                 x = x1_ref[:, head_columns(columns[0], h)].astype(F32)
                 g = g1_ref[:, head_columns(columns[1], h)].astype(F32)
             u_ref[:, one] = jnp.sum(g * ce, axis=1, keepdims=True)
             t_ref[:, one] = jnp.sum(x * br, axis=1, keepdims=True)
-            re_ref[0:1, one] = jnp.sum(n_scr[slot][:, at], axis=1, keepdims=True)
+            re_ref[0:1, one] = jnp.sum(n_ref[slot][:, at], axis=1, keepdims=True)
         if slot == 0:
             final = aligned(own_at[0] + r * own_at[1], width)
             pairs = [(yo_ref, yf_ref.at[:, final]), (dxo_ref, dxf_ref.at[:, final])]
@@ -373,7 +379,7 @@
     gys, dss, gxs = refs[:count], refs[count : 2 * count], refs[2 * count : 3 * count]
     refs = refs[3 * count :]
     us, ts, res = refs[:GROUPS], refs[GROUPS : 2 * GROUPS], refs[2 * GROUPS : 3 * GROUPS]
-    dbc_ref, own_ref, send_ref, sums_ref = refs[3 * GROUPS :]
+    own_ref, send_ref, sums_ref = refs[3 * GROUPS :]
 
     def total(parts):
         value = parts[0][...]
@@ -394,10 +400,7 @@
     turned = draw.T
     heads = own_ref.shape[0]
     own_ref[...] = turned[:heads, :]
-    both = split(turned[heads : 2 * heads, :])
-    send_ref[0:n, :] = dbc_ref[...]
-    send_ref[n:, :LANES] = both[:heads]
-    send_ref[n:, LANES:] = both[heads:]
+    send_ref[...] = turned[heads : 2 * heads, :]
     sums_ref[0:1, :] = jnp.sum(draw, axis=0, keepdims=True)
     sums_ref[1:2, :] = jnp.sum(dlog * (-step * rate), axis=0, keepdims=True)
     sums_ref[2:3, :] = total(gxs)[0:1, :]
@@ -405,23 +408,19 @@
 
 
 def conv_back_kernel(
-    own_ref, ret_ref, kept_ref, cw_ref, heads_ref, grad_ref, raw_ref, rim_ref, message_ref, z_scr,
-    sum_scr, grad_scr, raw_scr, sems,
+    own_ref, ret_ref, kept_ref, cw_ref, heads_ref, grad_ref, rim_ref, message_ref, z_scr, sum_scr,
 ):
     tokens = own_ref.shape[0]
     taps = cw_ref.shape[0]
     pre = kept_ref[HALO + tokens :, :]
     sig = jax.nn.sigmoid(pre)
-    dconv = (own_ref[...] + ret_ref[0:tokens, :].astype(F32)) * sig * (1.0 + pre * (1.0 - sig))
+    dconv = (own_ref[...] + ret_ref[...].astype(F32)) * sig * (1.0 + pre * (1.0 - sig))
     z_scr[...] = jnp.zeros_like(z_scr)
     z_scr[HALO : HALO + tokens, :] = dconv
     grad = cw_ref[0:1, :] * z_scr[taps - 1 : taps - 1 + tokens + HALO, :]
     for k in range(1, taps):
         grad = grad + cw_ref[k : k + 1, :] * z_scr[taps - 1 - k : taps - 1 - k + tokens + HALO, :]
-    grad_scr[...] = grad[HALO:, :]
-    raw = ret_ref[tokens:, :].astype(F32)
-    raw_scr[...] = raw[:, :LANES] + raw[:, LANES:]
-    copies = copy_all([(grad_scr, grad_ref), (raw_scr, raw_ref)], sems)
+    grad_ref[...] = grad[HALO:, :]
     rim_ref[...] = grad[HALO - 8 : HALO, :]
     first = HALO - taps + 1
     sum_scr[...] = jnp.zeros_like(sum_scr)
@@ -434,8 +433,6 @@
     small = split(sum_scr[...])
     message_ref[0 : tokens + HALO, :] = grad.astype(BF16)
     message_ref[tokens + HALO :, :] = small
-    for copy in copies:
-        copy.wait()
 
 
 def pack_kernel(layer_ref, halo_ref, keep_ref, send_ref, sems):
@@ -527,8 +524,9 @@
     half = outs[0].shape[1] // 2
     base = (1 - side()) * half
     pairs = []
-    for block, (which, at) in zip(blocks, targets):
-        pairs.append((block, outs[which].at[:, aligned(base + at, block.shape[1])]))
+    for block, pieces in zip(blocks, targets):
+        for first, width, which, at in pieces:
+            pairs.append((block.at[:, first : first + width], outs[which].at[:, aligned(base + at, width)]))
     for copy in copy_all(pairs, sems):
         copy.wait()
 
@@ -727,66 +725,71 @@
 
     full = shape((tokens, width), BF16)
     finals, sends, us, ts, res = (), [], [], [], []
+    cuts = [widths[0] // 2, *widths[1:]]
+    returns = [
+        (shape((tokens, cut), BF16), shape((tokens, 2 * w - cut), BF16)) for cut, w in zip(cuts, widths)
+    ]
     for i in range(GROUPS):
         last = i == GROUPS - 1
         own_at, _, xa, ga = source(0, i)
         x_at, g_at, xb, gb = source(1, i)
         if i == 1:
+            backs = [toggled(sends[0], "ctx", 1)]
             left = call(
                 functools.partial(turn_kernel, picks), "turn",
-                shape((rows, fsdp * (tokens + HALO)), BF16), (), after(arrays[0], *sends), *arrays[1:],
+                shape((rows, fsdp * (tokens + HALO)), BF16), (), after(arrays[0], *sends, *backs),
+                *arrays[1:],
             )
         lanes = (starts[i], heads + starts[i])
-        y, dx, y_send, dx_send, dbc_own, dbc_other, u, t, re = call(
+        pair = [shape((2, state, widths[i]), BF16)] * 2
+        *both, n, dbc_own, dbc_other = call(
+            functools.partial(enter_kernel, hops), "enter",
+            [*pair, shape((2, 1, widths[i]), F32), both_bc[0]]
+            + [shape((tokens, 2 * state), BF16 if last else F32)],
+            (), after(scaled[0, i][0], *sends), scaled[0, i][1], *scaled[1, i], *states[i][:4], *dbcs,
+            *received[i][1:],
+            scratch=[pltpu.VMEM((state, widths[i]), BF16)] * 2,
+        )
+        dbcs = (dbc_own, dbc_other)
+        if last:
+            dbc_ret = toggled(dbc_other, "ctx", 1)
+        y, dx, y_send, dx_send, u, t, re = call(
             functools.partial(
-                across_kernel, counts[i], lanes, hops, len(finals) // 2, own_at, (x_at, g_at)
+                across_kernel, counts[i], lanes, len(finals) // 2, own_at, (x_at, g_at)
             ),
-            "across",
-            [full, full, flats[i], flats[i]]
-            + [both_bc[0], shape((tokens, 2 * state), BF16 if last else F32)]
-            + [square, square, shape((8, LANES), F32)],
-            (), xa, ga, xb, gb, after(bcs[0], left) if i == 1 else bcs[0], bcs[1], *scaled[0, i],
-            *scaled[1, i], step, grow, endw,
-            *states[i][:4], *inside[0, i][:2], *inside[1, i][:2], *dbcs, *received[i][1:],
+            "across", [full, full, *returns[i], square, square, shape((8, LANES), F32)],
+            (), xa, ga, xb, gb, after(bcs[0], left) if i == 1 else bcs[0], bcs[1], step, grow, endw,
+            *both, n, *inside[0, i][:2], *inside[1, i][:2],
             hbm=finals, hbm_outs=2, aliases={0: 0, 1: 1} if finals else None,
-            scratch=[pltpu.VMEM((state, widths[i]), BF16)] * 2
-            + [pltpu.VMEM((2, state, widths[i]), BF16)] * 2
-            + [pltpu.VMEM((2, 1, widths[i]), F32)] + [pltpu.VMEM((tokens, widths[i]), BF16)] * 2
-            + [pltpu.SemaphoreType.DMA((2,))],
+            scratch=[pltpu.VMEM((tokens, widths[i]), BF16)] * 2 + [pltpu.SemaphoreType.DMA((2,))],
         )
-        finals, dbcs = (y, dx), (dbc_own, dbc_other)
+        finals = (y, dx)
         sends += [y_send, dx_send]
         us.append(u)
         ts.append(t)
         res.append(re)
 
-    raw_own, dbc_send, head_sums = call(
-        steps_kernel, "steps",
-        [turned, shape((tokens + heads, 2 * state), BF16), shape((8, LANES), F32)], (),
+    raw_own, raw_send, head_sums = call(
+        steps_kernel, "steps", [turned, turned, shape((8, LANES), F32)], (),
         sig, rate, step, grow, endw, *[inside[key][j] for j in (3, 4, 5) for key in order],
-        *us, *ts, *res, dbcs[1],
-    )
-    dbc_ret = toggled(dbc_send, "ctx", 1)
-    backs = [toggled(sends[0], "ctx", 1)]
-    grad, raw_back, rim_send, message = call(
+        *us, *ts, *res,
+    )
+    raw_back = toggled(raw_send, "ctx", 1)
+    grad, rim_send, message = call(
         conv_back_kernel, "conv_back",
         [
             shape((tokens, 2 * state), F32),
-            turned,
             shape((8, 2 * state), F32),
             shape((tokens + HALO + 16, 2 * state), BF16),
         ],
-        (), after(dbcs[0], *backs), dbc_ret, kept, conv_w, head_sums, hbm_outs=2,
+        (), after(dbcs[0], *backs), dbc_ret, kept, conv_w, head_sums,
         scratch=[
             pltpu.VMEM((tokens + 2 * HALO, 2 * state), F32),
             pltpu.VMEM((8, 2 * state), F32),
-            pltpu.VMEM((tokens, 2 * state), F32),
-            pltpu.VMEM(turned.shape, F32),
-            pltpu.SemaphoreType.DMA((2,)),
         ],
     )
     rim = lax.ppermute(rim_send, "ctx", [(i + 1, i) for i in range(ctx - 1)])
-    backs.append(toggled(after(sends[1], dbc_ret), "ctx", 1))
+    backs.append(toggled(after(sends[1], dbc_ret, head_sums), "ctx", 1))
 
     rights = [message] + [toggled(message, "fsdp", k) for k in range(fsdp - 1, 0, -1)][::-1]
     terms = call(
@@ -802,7 +805,7 @@
             shape((1, 2 * state), F32),
         ]
         + [shape((1, total_heads), F32)] * 3,
-        (), after(exchanged(terms, "ctx"), rim, *backs[:-1]),
+        (), after(exchanged(terms, "ctx"), rim, raw_back, *backs[:-1]),
     )
     grad_weight = call(
         place_rows_kernel, "place_rows", shape((rows, 2 * state), F32), (), exchanged(total, "ctx")
@@ -816,13 +819,16 @@
         join_steps_kernel, "join_steps", shape((total_heads, tokens), F32), (), raw_own,
         after(raw_back, total),
     )
-    targets = [(k % 2, ats[k // 2]) for k in range(2 * GROUPS)]
+    targets = []
+    for at, cut, w in zip(ats, cuts, widths):
+        rest = [(0, w - cut, 0, at + cut)] if cut < w else []
+        targets += [[(0, cut, 0, at)], [*rest, (w - cut, w, 1, at)]]
 
     def join(arrays, which, blocks):
         return call(
             functools.partial(join_kernel, [targets[k] for k in which]), "join", [full, full], (),
             *blocks, hbm=arrays, hbm_outs=2, aliases={0: 0, 1: 1},
-            scratch=[pltpu.SemaphoreType.DMA((len(which),))],
+            scratch=[pltpu.SemaphoreType.DMA((2 * len(which),))],
         )
 
     early_backs = range(2 * GROUPS - 1)

time: 132 us -> 128 us (0.970)
  starting transfers between devices: 46.9 us -> 43.8 us
    ppermute x1, waiting for transfers between devices: 11.8 us -> 0.09 us  [body(): rim = lax.ppermute(rim_send, 'ctx', [(i + 1, i) for i in range(ctx - 1)])]
    ppermute x18 -> x19, waiting for transfers between devices: 22.1 us -> 33.3 us  [toggled(): return lax.ppermute(x, axis, [(i, i ^ bits) for i in range(size)])]
    ppermute x18 -> x19, starting transfers between devices: 23.7 us -> 20.7 us  [toggled(): return lax.ppermute(x, axis, [(i, i ^ bits) for i in range(size)])]
    pallas_call x33 -> x35, Pallas kernels: 34.9 us -> 35.7 us  [call(): pl.pallas_call(kernel, out_shape=outs, in_specs=[pl.BlockSpec(memory_spac...]
  transfers between devices with their start and end apart: 28 -> 29, of which waited for: 15 -> 15; matrix products, arithmetic and copies ran while one was open for 0% -> 0% of each run, Pallas kernels for 24% -> 25%
where the time goes in v3:
time: 128 us
  waiting for transfers between devices  45.3 us (35%)
  starting transfers between devices  43.8 us (34%)
  Pallas kernels  35.7 us (28%)
  local copies, waits for them, and re-layouts  1.6 us (1%)
    pallas_call x35, Pallas kernels, call(): pl.pallas_call(kernel, out_shape=outs, in_specs=[pl.BlockSpec(memory_spac...  35.7 us
    ppermute x19, waiting for transfers between devices, toggled(): return lax.ppermute(x, axis, [(i, i ^ bits) for i in range(size)])  33.3 us
    ppermute x19, starting transfers between devices, toggled(): return lax.ppermute(x, axis, [(i, i ^ bits) for i in range(size)])  20.7 us
    ppermute x6, starting transfers between devices, body(): received[i].append(lax.ppermute(value, 'ctx', moves))  12.3 us
    ppermute x6, waiting for transfers between devices, body(): received[i].append(lax.ppermute(value, 'ctx', moves))  9.78 us
    all_to_all x2, starting transfers between devices, exchanged(): return lax.all_to_all(x, axis, 0, 0)  7.11 us
  transfers between devices with their start and end apart: 29, of which 15 were waited for; matrix products, arithmetic and copies ran while one was open for 0% of the time, Pallas kernels for 25%

profile of v3, /device:TPU:0, one launch (start us, length us, event | category | flops | bytes accessed | tf_op | source)
XLA Modules:
  0.0 127.5 jit_solution(6502771101053008879)
XLA Ops:
  0.6 3.0 %collective-permute-start = (f32[32,128]{1,0:T(8,128)}, f32[32,128]{1,0:T(8,128)S(1)}, u32[]{:S(2)}, u32[]{:S(2)}) collective-permute-start(f32[32,128]{1,0:T(8,128)} %bitcast.33), channel_id=1, source_target_pairs={{0,4},{4,0},{8,12},{12,8},{16,20},{20,16},{24,28},{28,24},{1,5},{5... | collective-permute-start | bytes 49160 | tf_op jit(solution)/shard_map/ppermute | solution.py:547
  5.6 2.0 %collective-permute-start.1 = (bf16[128,2048]{1,0:T(8,128)(2,1)S(1)}, bf16[128,2048]{1,0:T(8,128)(2,1)S(1)}, u32[]{:S(2)}, u32[]{:S(2)}) collective-permute-start(bf16[128,2048]{1,0:T(8,128)(2,1)S(1)} %get-tuple-element.140), channel_id=1, source_target_pairs={{0,4},{4,0},{8,12},{12,8},{16,20},{20,16},{24,28},{28,24},{1,5},{5... | collective-permute-start | bytes 1572872 | tf_op jit(solution)/shard_map/ppermute | solution.py:547
  9.1 2.4 %collective-permute-start.4 = (bf16[16,4096]{1,0:T(8,128)(2,1)S(1)}, bf16[16,4096]{1,0:T(8,128)(2,1)S(1)}, u32[]{:S(2)}, u32[]{:S(2)}) collective-permute-start(bf16[16,4096]{1,0:T(8,128)(2,1)S(1)} %get-tuple-element.141), channel_id=1, source_target_pairs={{0,4},{4,8},{8,12},{12,16},{16,20},{20,24},{24,28},{1,5},{5,9},{9,... | collective-permute-start | bytes 393224 | tf_op jit(solution)/shard_map/ppermute | solution.py:586
  14.5 5.1 %collective-permute-done.1.x_ref.g_ref.refs_2_.refs_3_ = bf16[128,2048]{1,0:T(8,128)(2,1)S(1)} collective-permute-done((bf16[128,2048]{1,0:T(8,128)(2,1)S(1)}, bf16[128,2048]{1,0:T(8,128)(2,1)S(1)}, u32[]{:S(2)}, u32[]{:S(2)}) %collective-permute-start.1) | collective-permute-done | bytes 524320 | tf_op jit(solution)/shard_map/ppermute | solution.py:547
  23.4 2.1 %project.1 = (f32[272,256]{1,0:T(8,128)S(1)}, bf16[128,256]{1,0:T(8,128)(2,1)S(1)}) custom-call(bf16[128,4096]{1,0:T(8,128)(2,1)} %bitcast.41, bf16[1024,256]{1,0:T(8,128)(2,1)S(1)} %copy-done.2, bf16[1024,256]{1,0:T(8,128)(2,1)S(1)} %collective-permute-done.2.refs_1_, bf16[1024,256]{1,0:T(8,128)(2,1)S(1)} %collective-permute-done.3.refs_2_, ...), custom_call_target="tpu_custom_call" | custom-call | tf_op jit(solution)/shard_map/project/pallas_call | solution.py:37
  25.5 2.5 %collective-permute-start.6 = (bf16[128,256]{1,0:T(8,128)(2,1)S(1)}, bf16[128,256]{1,0:T(8,128)(2,1)S(1)}, u32[]{:S(2)}, u32[]{:S(2)}) collective-permute-start(bf16[128,256]{1,0:T(8,128)(2,1)S(1)} %get-tuple-element.201.bc_ref.bc0_ref.refs_4_.refs_6_), channel_id=1, source_target_pairs={{0,4},{4,0},{8,12},{12,8},{16,20},{20,16},{24,28},{28,24},{1,5},{5... | collective-permute-start | bytes 196616 | tf_op jit(solution)/shard_map/ppermute | solution.py:547
  28.1 2.2 %inside.4 = (f32[128,1024]{1,0:T(8,128)S(1)}, f32[128,1024]{1,0:T(8,128)S(1)}, f32[128,128]{1,0:T(8,128)S(1)}, f32[128,128]{1,0:T(8,128)S(1)}, f32[128,128]{1,0:T(8,128)S(1)}, /*index=5*/f32[8,128]{1,0:T(8,128)S(1)}) custom-call(f32[32]{0:T(128)S(1)} %copy-done.7, bf16[128,4096]{1,0:T(8,128)(2,1)S(1)} %bitcast.22, bf16[128,4096]{1,0:T(8,128)(2,1)S(1)} %bitcast.29, ...), custom_call_target="tpu_custom_call" | custom-call | tf_op jit(solution)/shard_map/inside/pallas_call | solution.py:37
  30.5 2.5 %collective-permute-start.9 = (bf16[128,1024]{1,0:T(8,128)(2,1)S(1)}, bf16[128,1024]{1,0:T(8,128)(2,1)S(1)}, u32[]{:S(2)}, u32[]{:S(2)}) collective-permute-start(bf16[128,1024]{1,0:T(8,128)(2,1)S(1)} %get-tuple-element.169), channel_id=1, source_target_pairs={{0,4},{4,0},{8,12},{12,8},{16,20},{20,16},{24,28},{28,24},{1,5},{5... | collective-permute-start | bytes 786440 | tf_op jit(solution)/shard_map/ppermute | solution.py:547
  33.8 3.4 %collective-permute-start.7 = (bf16[128,1024]{1,0:T(8,128)(2,1)S(1)}, bf16[128,1024]{1,0:T(8,128)(2,1)S(1)}, u32[]{:S(2)}, u32[]{:S(2)}) collective-permute-start(bf16[128,1024]{1,0:T(8,128)(2,1)S(1)} %get-tuple-element.162), channel_id=1, source_target_pairs={{0,8},{4,12},{24,16},{28,20},{1,9},{5,13},{25,17},{29,21},{2,10},{... | collective-permute-start | bytes 786440 | tf_op jit(solution)/shard_map/ppermute | solution.py:704
  37.1 2.2 %inside.5 = (f32[128,1024]{1,0:T(8,128)S(1)}, f32[128,1024]{1,0:T(8,128)S(1)}, f32[128,128]{1,0:T(8,128)S(1)}, f32[128,128]{1,0:T(8,128)S(1)}, f32[128,128]{1,0:T(8,128)S(1)}, /*index=5*/f32[8,128]{1,0:T(8,128)S(1)}) custom-call(f32[32]{0:T(128)S(1)} %copy-done.7, bf16[128,4096]{1,0:T(8,128)(2,1)S(1)} %bitcast.23, bf16[128,4096]{1,0:T(8,128)(2,1)S(1)} %bitcast.30, ...), custom_call_target="tpu_custom_call" | custom-call | tf_op jit(solution)/shard_map/inside/pallas_call | solution.py:37
  39.4 2.4 %collective-permute-done.9.g_ref.refs_5_ = bf16[128,1024]{1,0:T(8,128)(2,1)S(1)} collective-permute-done((bf16[128,1024]{1,0:T(8,128)(2,1)S(1)}, bf16[128,1024]{1,0:T(8,128)(2,1)S(1)}, u32[]{:S(2)}, u32[]{:S(2)}) %collective-permute-start.9) | collective-permute-done | bytes 262176 | tf_op jit(solution)/shard_map/ppermute | solution.py:547
  43.0 5.0 %collective-permute-start.11 = (bf16[128,1024]{1,0:T(8,128)(2,1)S(1)}, bf16[128,1024]{1,0:T(8,128)(2,1)S(1)}, u32[]{:S(2)}, u32[]{:S(2)}) collective-permute-start(bf16[128,1024]{1,0:T(8,128)(2,1)S(1)} %get-tuple-element.173), channel_id=1, source_target_pairs={{0,8},{4,12},{24,16},{28,20},{1,9},{5,13},{25,17},{29,21},{2,10},{... | collective-permute-start | bytes 786440 | tf_op jit(solution)/shard_map/ppermute | solution.py:704
  48.9 2.3 %inside.6 = (f32[128,1024]{1,0:T(8,128)S(1)}, f32[128,1024]{1,0:T(8,128)S(1)}, f32[128,128]{1,0:T(8,128)S(1)}, f32[128,128]{1,0:T(8,128)S(1)}, f32[128,128]{1,0:T(8,128)S(1)}, /*index=5*/f32[8,128]{1,0:T(8,128)S(1)}) custom-call(f32[32]{0:T(128)S(1)} %copy-done.7, bf16[128,2048]{1,0:T(8,128)(2,1)S(1)} %collective-permute-done.1.x_ref.g_ref.refs_2_.refs_3_, ...), custom_call_target="tpu_custom_call" | custom-call | tf_op jit(solution)/shard_map/inside/pallas_call | solution.py:37
  55.3 2.3 %inside.7 = (f32[128,1024]{1,0:T(8,128)S(1)}, f32[128,1024]{1,0:T(8,128)S(1)}, f32[128,128]{1,0:T(8,128)S(1)}, f32[128,128]{1,0:T(8,128)S(1)}, f32[128,128]{1,0:T(8,128)S(1)}, /*index=5*/f32[8,128]{1,0:T(8,128)S(1)}) custom-call(f32[32]{0:T(128)S(1)} %copy-done.7, bf16[128,1024]{1,0:T(8,128)(2,1)S(1)} %collective-permute-done.8.x_ref.refs_4_, ...), custom_call_target="tpu_custom_call" | custom-call | tf_op jit(solution)/shard_map/inside/pallas_call | solution.py:37
  59.2 7.1 %collective-permute-done.12.refs_2_ = bf16[128,1024]{1,0:T(8,128)(2,1)S(1)} collective-permute-done((bf16[128,1024]{1,0:T(8,128)(2,1)S(1)}, bf16[128,1024]{1,0:T(8,128)(2,1)S(1)}, u32[]{:S(2)}, u32[]{:S(2)}) %collective-permute-start.12) | collective-permute-done | bytes 262176 | tf_op jit(solution)/shard_map/ppermute | solution.py:704
  67.4 2.5 %across.2 = (bf16[128,4096]{1,0:T(8,128)(2,1)}, bf16[128,4096]{1,0:T(8,128)(2,1)}, bf16[128,512]{1,0:T(8,128)(2,1)S(1)}, bf16[128,1536]{1,0:T(8,128)(2,1)S(1)}, ...) custom-call(bf16[128,4096]{1,0:T(8,128)(2,1)S(1)} %bitcast.24, ...), custom_call_target="tpu_custom_call" | custom-call | tf_op jit(solution)/shard_map/across/pallas_call | solution.py:37
  75.3 2.5 %across.3 = (bf16[128,4096]{1,0:T(8,128)(2,1)}, bf16[128,4096]{1,0:T(8,128)(2,1)}, bf16[128,1024]{1,0:T(8,128)(2,1)S(1)}, bf16[128,1024]{1,0:T(8,128)(2,1)S(1)},...) custom-call(bf16[128,4096]{1,0:T(8,128)(2,1)} %get-tuple-element.194, ...), custom_call_target="tpu_custom_call", output_to_operand_aliasing={{0}: (0, {}), {1}: (1, {})} | custom-call | tf_op jit(solution)/shard_map/across/pallas_call | solution.py:37
  81.1 5.0 %collective-permute-done.19.refs_3_ = bf16[128,1536]{1,0:T(8,128)(2,1)S(1)} collective-permute-done((bf16[128,1536]{1,0:T(8,128)(2,1)S(1)}, bf16[128,1536]{1,0:T(8,128)(2,1)S(1)}, u32[]{:S(2)}, u32[]{:S(2)}) %collective-permute-start.19) | collective-permute-done | bytes 393248 | tf_op jit(solution)/shard_map/ppermute | solution.py:547
  87.5 3.5 %all-to-all-start = ((bf16[8,144,256]{2,1,0:T(8,128)(2,1)}), bf16[8,144,256]{2,1,0:T(8,128)(2,1)S(1)}, u32[]{:S(2)}, u32[]{:S(2)}) async-start(bf16[8,144,256]{2,1,0:T(8,128)(2,1)} %weight.1), calls=%async_computation | async-start | bytes 1179648 | tf_op jit(solution)/shard_map/all_to_all | solution.py:551
  94.4 11.4 %collective-permute-done.24.back_ref = f32[16,128]{1,0:T(8,128)S(1)} collective-permute-done((f32[16,128]{1,0:T(8,128)S(1)}, f32[16,128]{1,0:T(8,128)S(1)}, u32[]{:S(2)}, u32[]{:S(2)}) %collective-permute-start.24) | collective-permute-done | bytes 8224 | tf_op jit(solution)/shard_map/ppermute | solution.py:547
  108.2 3.6 %all-to-all-start.1 = ((bf16[8,128,256]{2,1,0:T(8,128)(2,1)}), bf16[8,128,256]{2,1,0:T(8,128)(2,1)S(1)}, u32[]{:S(2)}, u32[]{:S(2)}) async-start(bf16[8,128,256]{2,1,0:T(8,128)(2,1)} %get-tuple-element.250), calls=%async_computation.1 | async-start | bytes 1048576 | tf_op jit(solution)/shard_map/all_to_all | solution.py:551
  111.8 2.0 %collective-permute-start.26 = (bf16[128,1024]{1,0:T(8,128)(2,1)}, bf16[128,1024]{1,0:T(8,128)(2,1)S(1)}, u32[]{:S(2)}, u32[]{:S(2)}) collective-permute-start(bf16[128,1024]{1,0:T(8,128)(2,1)} %copy-done.11), channel_id=1, source_target_pairs={{0,4},{4,0},{8,12},{12,8},{16,20},{20,16},{24,28},{28,24},{1,5},{5... | collective-permute-start | bytes 786440 | tf_op jit(solution)/shard_map/ppermute | solution.py:547
  115.3 2.4 %grad_tokens.1 = bf16[128,4096]{1,0:T(8,128)(2,1)} custom-call(bf16[1024,256]{1,0:T(8,128)(2,1)S(1)} %copy-done.2, bf16[1024,256]{1,0:T(8,128)(2,1)S(1)} %collective-permute-done.2.refs_1_, bf16[1024,256]{1,0:T(8,128)(2,1)S(1)} %collective-permute-done.3.refs_2_, bf16[1024,256]{1,0:T(8,128)(2,1)S(1)} %collective-permute-done.5.refs_3_, ...), custom_call_target="tpu_custom_call" | custom-call | tf_op jit(solution)/shard_map/grad_tokens/pallas_call | solution.py:37
  118.7 6.9 %collective-permute-done.26.refs_2_ = bf16[128,1024]{1,0:T(8,128)(2,1)S(1)} collective-permute-done((bf16[128,1024]{1,0:T(8,128)(2,1)}, bf16[128,1024]{1,0:T(8,128)(2,1)S(1)}, u32[]{:S(2)}, u32[]{:S(2)}) %collective-permute-start.26) | collective-permute-done | bytes 262176 | tf_op jit(solution)/shard_map/ppermute | solution.py:547
  (95 shorter events, 39.9 us)
Async XLA Ops:
  3.6 9.2 %collective-permute-start.2 = (bf16[1024,256]{1,0:T(8,128)(2,1)}, bf16[1024,256]{1,0:T(8,128)(2,1)S(1)}, u32[]{:S(2)}, u32[]{:S(2)}) collective-permute-start(bf16[1024,256]{1,0:T(8,128)(2,1)} %refs_0_.5), channel_id=1, source_target_pairs={{0,1},{1,0},{2,3},{3,2},{4,5},{5,4},{6,7},{7,6},{8,9},{9,8},{10,11... | collective-permute-start | bytes 1572872 | tf_op jit(solution)/shard_map/ppermute | solution.py:547
  5.6 14.0 %collective-permute-start.1 = (bf16[128,2048]{1,0:T(8,128)(2,1)S(1)}, bf16[128,2048]{1,0:T(8,128)(2,1)S(1)}, u32[]{:S(2)}, u32[]{:S(2)}) collective-permute-start(bf16[128,2048]{1,0:T(8,128)(2,1)S(1)} %get-tuple-element.140), channel_id=1, source_target_pairs={{0,4},{4,0},{8,12},{12,8},{16,20},{20,16},{24,28},{28,24},{1,5},{5... | collective-permute-start | bytes 1572872 | tf_op jit(solution)/shard_map/ppermute | solution.py:547
  7.6 12.8 %collective-permute-start.3 = (bf16[1024,256]{1,0:T(8,128)(2,1)S(1)}, bf16[1024,256]{1,0:T(8,128)(2,1)S(1)}, u32[]{:S(2)}, u32[]{:S(2)}) collective-permute-start(bf16[1024,256]{1,0:T(8,128)(2,1)S(1)} %copy-done.2), channel_id=1, source_target_pairs={{0,2},{1,3},{2,0},{3,1},{4,6},{5,7},{6,4},{7,5},{8,10},{9,11},{10,... | collective-permute-start | bytes 1572872 | tf_op jit(solution)/shard_map/ppermute | solution.py:547
  9.1 11.3 %collective-permute-start.4 = (bf16[16,4096]{1,0:T(8,128)(2,1)S(1)}, bf16[16,4096]{1,0:T(8,128)(2,1)S(1)}, u32[]{:S(2)}, u32[]{:S(2)}) collective-permute-start(bf16[16,4096]{1,0:T(8,128)(2,1)S(1)} %get-tuple-element.141), channel_id=1, source_target_pairs={{0,4},{4,8},{8,12},{12,16},{16,20},{20,24},{24,28},{1,5},{5,9},{9,... | collective-permute-start | bytes 393224 | tf_op jit(solution)/shard_map/ppermute | solution.py:586
  21.7 27.1 %collective-permute-start.14 = (bf16[2,144,1024]{2,1,0:T(8,128)(2,1)S(1)}, bf16[2,144,1024]{2,1,0:T(8,128)(2,1)S(1)}, u32[]{:S(2)}, u32[]{:S(2)}) collective-permute-start(bf16[2,144,1024]{2,1,0:T(8,128)(2,1)S(1)} %get-tuple-element.199), channel_id=1, source_target_pairs={{0,2},{1,3},{2,0},{3,1},{4,6},{5,7},{6,4},{7,5},{8,10},{9,11},{10,... | collective-permute-start | bytes 1769480 | tf_op jit(solution)/shard_map/ppermute | solution.py:547
  28.0 11.3 %collective-permute-start.8 = (bf16[128,1024]{1,0:T(8,128)(2,1)S(1)}, bf16[128,1024]{1,0:T(8,128)(2,1)S(1)}, u32[]{:S(2)}, u32[]{:S(2)}) collective-permute-start(bf16[128,1024]{1,0:T(8,128)(2,1)S(1)} %get-tuple-element.167), channel_id=1, source_target_pairs={{0,4},{4,0},{8,12},{12,8},{16,20},{20,16},{24,28},{28,24},{1,5},{5... | collective-permute-start | bytes 786440 | tf_op jit(solution)/shard_map/ppermute | solution.py:547
  30.5 11.3 %collective-permute-start.9 = (bf16[128,1024]{1,0:T(8,128)(2,1)S(1)}, bf16[128,1024]{1,0:T(8,128)(2,1)S(1)}, u32[]{:S(2)}, u32[]{:S(2)}) collective-permute-start(bf16[128,1024]{1,0:T(8,128)(2,1)S(1)} %get-tuple-element.169), channel_id=1, source_target_pairs={{0,4},{4,0},{8,12},{12,8},{16,20},{20,16},{24,28},{28,24},{1,5},{5... | collective-permute-start | bytes 786440 | tf_op jit(solution)/shard_map/ppermute | solution.py:547
  33.8 14.2 %collective-permute-start.7 = (bf16[128,1024]{1,0:T(8,128)(2,1)S(1)}, bf16[128,1024]{1,0:T(8,128)(2,1)S(1)}, u32[]{:S(2)}, u32[]{:S(2)}) collective-permute-start(bf16[128,1024]{1,0:T(8,128)(2,1)S(1)} %get-tuple-element.162), channel_id=1, source_target_pairs={{0,8},{4,12},{24,16},{28,20},{1,9},{5,13},{25,17},{29,21},{2,10},{... | collective-permute-start | bytes 786440 | tf_op jit(solution)/shard_map/ppermute | solution.py:704
  43.0 10.1 %collective-permute-start.11 = (bf16[128,1024]{1,0:T(8,128)(2,1)S(1)}, bf16[128,1024]{1,0:T(8,128)(2,1)S(1)}, u32[]{:S(2)}, u32[]{:S(2)}) collective-permute-start(bf16[128,1024]{1,0:T(8,128)(2,1)S(1)} %get-tuple-element.173), channel_id=1, source_target_pairs={{0,8},{4,12},{24,16},{28,20},{1,9},{5,13},{25,17},{29,21},{2,10},{... | collective-permute-start | bytes 786440 | tf_op jit(solution)/shard_map/ppermute | solution.py:704
  48.1 5.7 %collective-permute-start.10 = (bf16[128,1024]{1,0:T(8,128)(2,1)S(1)}, bf16[128,1024]{1,0:T(8,128)(2,1)S(1)}, u32[]{:S(2)}, u32[]{:S(2)}) collective-permute-start(bf16[128,1024]{1,0:T(8,128)(2,1)S(1)} %hop.4), channel_id=1, source_target_pairs={{8,16},{12,20},{16,8},{20,12},{9,17},{13,21},{17,9},{21,13},{10,18... | collective-permute-start | bytes 786440 | tf_op jit(solution)/shard_map/ppermute | solution.py:704
  48.9 26.1 %collective-permute-start.15 = (bf16[2,144,1024]{2,1,0:T(8,128)(2,1)S(1)}, bf16[2,144,1024]{2,1,0:T(8,128)(2,1)S(1)}, u32[]{:S(2)}, u32[]{:S(2)}) collective-permute-start(bf16[2,144,1024]{2,1,0:T(8,128)(2,1)S(1)} %relay.1), channel_id=1, source_target_pairs={{0,1},{1,0},{2,3},{3,2},{4,5},{5,4},{6,7},{7,6},{8,9},{9,8},{10,11... | collective-permute-start | bytes 1769480 | tf_op jit(solution)/shard_map/ppermute | solution.py:547
  54.0 12.3 %collective-permute-start.12 = (bf16[128,1024]{1,0:T(8,128)(2,1)S(1)}, bf16[128,1024]{1,0:T(8,128)(2,1)S(1)}, u32[]{:S(2)}, u32[]{:S(2)}) collective-permute-start(bf16[128,1024]{1,0:T(8,128)(2,1)S(1)} %hop.6), channel_id=1, source_target_pairs={{16,24},{20,28},{8,0},{12,4},{17,25},{21,29},{9,1},{13,5},{18,26},... | collective-permute-start | bytes 786440 | tf_op jit(solution)/shard_map/ppermute | solution.py:704
  57.7 13.1 %collective-permute-start.17 = (bf16[128,1024]{1,0:T(8,128)(2,1)S(1)}, bf16[128,1024]{1,0:T(8,128)(2,1)S(1)}, u32[]{:S(2)}, u32[]{:S(2)}) collective-permute-start(bf16[128,1024]{1,0:T(8,128)(2,1)S(1)} %hop.7), channel_id=1, source_target_pairs={{16,24},{20,28},{8,0},{12,4},{17,25},{21,29},{9,1},{13,5},{18,26},... | collective-permute-start | bytes 786440 | tf_op jit(solution)/shard_map/ppermute | solution.py:704
  71.6 6.6 %collective-permute-start.18 = (bf16[128,256]{1,0:T(8,128)(2,1)S(1)}, bf16[128,256]{1,0:T(8,128)(2,1)S(1)}, u32[]{:S(2)}, u32[]{:S(2)}) collective-permute-start(bf16[128,256]{1,0:T(8,128)(2,1)S(1)} %get-tuple-element.219), channel_id=1, source_target_pairs={{0,4},{4,0},{8,12},{12,8},{16,20},{20,16},{24,28},{28,24},{1,5},{5... | collective-permute-start | bytes 196616 | tf_op jit(solution)/shard_map/ppermute | solution.py:547
  78.2 7.8 %collective-permute-start.19 = (bf16[128,1536]{1,0:T(8,128)(2,1)S(1)}, bf16[128,1536]{1,0:T(8,128)(2,1)S(1)}, u32[]{:S(2)}, u32[]{:S(2)}) collective-permute-start(bf16[128,1536]{1,0:T(8,128)(2,1)S(1)} %get-tuple-element.243), channel_id=1, source_target_pairs={{0,4},{4,0},{8,12},{12,8},{16,20},{20,16},{24,28},{28,24},{1,5},{5... | collective-permute-start | bytes 1179656 | tf_op jit(solution)/shard_map/ppermute | solution.py:547
  79.2 6.8 %collective-permute-start.20 = (bf16[160,256]{1,0:T(8,128)(2,1)S(1)}, bf16[160,256]{1,0:T(8,128)(2,1)S(1)}, u32[]{:S(2)}, u32[]{:S(2)}) collective-permute-start(bf16[160,256]{1,0:T(8,128)(2,1)S(1)} %get-tuple-element.244.refs_0_), channel_id=1, source_target_pairs={{0,1},{1,0},{2,3},{3,2},{4,5},{5,4},{6,7},{7,6},{8,9},{9,8},{10,11... | collective-permute-start | bytes 245768 | tf_op jit(solution)/shard_map/ppermute | solution.py:547
  79.2 6.8 %collective-permute-start.21 = (bf16[160,256]{1,0:T(8,128)(2,1)S(1)}, bf16[160,256]{1,0:T(8,128)(2,1)S(1)}, u32[]{:S(2)}, u32[]{:S(2)}) collective-permute-start(bf16[160,256]{1,0:T(8,128)(2,1)S(1)} %get-tuple-element.244.refs_0_), channel_id=1, source_target_pairs={{0,2},{1,3},{2,0},{3,1},{4,6},{5,7},{6,4},{7,5},{8,10},{9,11},{10,... | collective-permute-start | bytes 245768 | tf_op jit(solution)/shard_map/ppermute | solution.py:547
  79.7 6.4 %collective-permute-start.22 = (bf16[160,256]{1,0:T(8,128)(2,1)S(1)}, bf16[160,256]{1,0:T(8,128)(2,1)S(1)}, u32[]{:S(2)}, u32[]{:S(2)}) collective-permute-start(bf16[160,256]{1,0:T(8,128)(2,1)S(1)} %get-tuple-element.244.refs_0_), channel_id=1, source_target_pairs={{0,3},{1,2},{2,1},{3,0},{4,7},{5,6},{6,5},{7,4},{8,11},{9,10},{10,... | collective-permute-start | bytes 245768 | tf_op jit(solution)/shard_map/ppermute | solution.py:547
  87.5 19.7 %all-to-all-start = ((bf16[8,144,256]{2,1,0:T(8,128)(2,1)}), bf16[8,144,256]{2,1,0:T(8,128)(2,1)S(1)}, u32[]{:S(2)}, u32[]{:S(2)}) async-start(bf16[8,144,256]{2,1,0:T(8,128)(2,1)} %weight.1), calls=%async_computation | async-start | bytes 1179648 | tf_op jit(solution)/shard_map/all_to_all | solution.py:551
  91.1 14.8 %collective-permute-start.25 = (bf16[128,1024]{1,0:T(8,128)(2,1)}, bf16[128,1024]{1,0:T(8,128)(2,1)S(1)}, u32[]{:S(2)}, u32[]{:S(2)}) collective-permute-start(bf16[128,1024]{1,0:T(8,128)(2,1)} %copy-done.12), channel_id=1, source_target_pairs={{0,4},{4,0},{8,12},{12,8},{16,20},{20,16},{24,28},{28,24},{1,5},{5... | collective-permute-start | bytes 786440 | tf_op jit(solution)/shard_map/ppermute | solution.py:547
  93.0 12.8 %collective-permute-start.24 = (f32[16,128]{1,0:T(8,128)S(1)}, f32[16,128]{1,0:T(8,128)S(1)}, u32[]{:S(2)}, u32[]{:S(2)}) collective-permute-start(f32[16,128]{1,0:T(8,128)S(1)} %get-tuple-element.246), channel_id=1, source_target_pairs={{0,4},{4,0},{8,12},{12,8},{16,20},{20,16},{24,28},{28,24},{1,5},{5... | collective-permute-start | bytes 24584 | tf_op jit(solution)/shard_map/ppermute | solution.py:547
  93.2 12.7 %collective-permute-start.23 = (f32[8,256]{1,0:T(8,128)S(1)}, f32[8,256]{1,0:T(8,128)S(1)}, u32[]{:S(2)}, u32[]{:S(2)}) collective-permute-start(f32[8,256]{1,0:T(8,128)S(1)} %get-tuple-element.245), channel_id=1, source_target_pairs={{4,0},{8,4},{12,8},{16,12},{20,16},{24,20},{28,24},{5,1},{9,5},{13... | collective-permute-start | bytes 24584 | tf_op jit(solution)/shard_map/ppermute | solution.py:791
  108.2 18.2 %all-to-all-start.1 = ((bf16[8,128,256]{2,1,0:T(8,128)(2,1)}), bf16[8,128,256]{2,1,0:T(8,128)(2,1)S(1)}, u32[]{:S(2)}, u32[]{:S(2)}) async-start(bf16[8,128,256]{2,1,0:T(8,128)(2,1)} %get-tuple-element.250), calls=%async_computation.1 | async-start | bytes 1048576 | tf_op jit(solution)/shard_map/all_to_all | solution.py:551
  111.8 13.8 %collective-permute-start.26 = (bf16[128,1024]{1,0:T(8,128)(2,1)}, bf16[128,1024]{1,0:T(8,128)(2,1)S(1)}, u32[]{:S(2)}, u32[]{:S(2)}) collective-permute-start(bf16[128,1024]{1,0:T(8,128)(2,1)} %copy-done.11), channel_id=1, source_target_pairs={{0,4},{4,0},{8,12},{12,8},{16,20},{20,16},{24,28},{28,24},{1,5},{5... | collective-permute-start | bytes 786440 | tf_op jit(solution)/shard_map/ppermute | solution.py:547
  (18 other events, 107.3 us)

commit v4 on v3

--- a/solution.py
+++ b/solution.py
@@ -409,6 +409,7 @@
 
 def conv_back_kernel(
     own_ref, ret_ref, kept_ref, cw_ref, heads_ref, grad_ref, rim_ref, message_ref, z_scr, sum_scr,
+    grad_scr, sems,
 ):
     tokens = own_ref.shape[0]
     taps = cw_ref.shape[0]
@@ -420,7 +421,8 @@
     grad = cw_ref[0:1, :] * z_scr[taps - 1 : taps - 1 + tokens + HALO, :]
     for k in range(1, taps):
         grad = grad + cw_ref[k : k + 1, :] * z_scr[taps - 1 - k : taps - 1 - k + tokens + HALO, :]
-    grad_ref[...] = grad[HALO:, :]
+    grad_scr[...] = grad[HALO:, :]
+    copies = copy_all([(grad_scr, grad_ref)], sems)
     rim_ref[...] = grad[HALO - 8 : HALO, :]
     first = HALO - taps + 1
     sum_scr[...] = jnp.zeros_like(sum_scr)
@@ -433,6 +435,8 @@
     small = split(sum_scr[...])
     message_ref[0 : tokens + HALO, :] = grad.astype(BF16)
     message_ref[tokens + HALO :, :] = small
+    for copy in copies:
+        copy.wait()
 
 
 def pack_kernel(layer_ref, halo_ref, keep_ref, send_ref, sems):
@@ -778,14 +782,16 @@
     grad, rim_send, message = call(
         conv_back_kernel, "conv_back",
         [
-            shape((tokens, 2 * state), F32),
+            pltpu.HBM((tokens, 2 * state), F32),
             shape((8, 2 * state), F32),
             shape((tokens + HALO + 16, 2 * state), BF16),
         ],
-        (), after(dbcs[0], *backs), dbc_ret, kept, conv_w, head_sums,
+        (), after(dbcs[0], *backs), dbc_ret, kept, conv_w, head_sums, hbm_outs=1,
         scratch=[
             pltpu.VMEM((tokens + 2 * HALO, 2 * state), F32),
             pltpu.VMEM((8, 2 * state), F32),
+            pltpu.VMEM((tokens, 2 * state), F32),
+            pltpu.SemaphoreType.DMA((1,)),
         ],
     )
     rim = lax.ppermute(rim_send, "ctx", [(i + 1, i) for i in range(ctx - 1)])

time: 128 us -> 128 us (level)
  transfers between devices with their start and end apart: 29 -> 29, of which waited for: 15 -> 15; matrix products, arithmetic and copies ran while one was open for 0% -> 0% of each run, Pallas kernels for 25% -> 26%
where the time goes in v4:
time: 128 us
  waiting for transfers between devices  45.3 us (35%)
  starting transfers between devices  43.9 us (34%)
  Pallas kernels  36.3 us (28%)
    pallas_call x35, Pallas kernels, call(): pl.pallas_call(kernel, out_shape=outs, in_specs=[pl.BlockSpec(memory_spac...  36.3 us
    ppermute x19, waiting for transfers between devices, toggled(): return lax.ppermute(x, axis, [(i, i ^ bits) for i in range(size)])  33.3 us
    ppermute x19, starting transfers between devices, toggled(): return lax.ppermute(x, axis, [(i, i ^ bits) for i in range(size)])  20.8 us
    ppermute x6, starting transfers between devices, body(): received[i].append(lax.ppermute(value, 'ctx', moves))  12.3 us
    ppermute x6, waiting for transfers between devices, body(): received[i].append(lax.ppermute(value, 'ctx', moves))  9.78 us
    all_to_all x2, starting transfers between devices, exchanged(): return lax.all_to_all(x, axis, 0, 0)  7.11 us
  transfers between devices with their start and end apart: 29, of which 15 were waited for; matrix products, arithmetic and copies ran while one was open for 0% of the time, Pallas kernels for 26%

profile of v4, /device:TPU:0, one launch (start us, length us, event | category | flops | bytes accessed | tf_op | source)
XLA Modules:
  0.0 127.5 jit_solution(274779299452476446)
XLA Ops:
  0.6 3.0 %collective-permute-start = (f32[32,128]{1,0:T(8,128)}, f32[32,128]{1,0:T(8,128)S(1)}, u32[]{:S(2)}, u32[]{:S(2)}) collective-permute-start(f32[32,128]{1,0:T(8,128)} %bitcast.33), channel_id=1, source_target_pairs={{0,4},{4,0},{8,12},{12,8},{16,20},{20,16},{24,28},{28,24},{1,5},{5... | collective-permute-start | bytes 49160 | tf_op jit(solution)/shard_map/ppermute | solution.py:551
  5.6 2.0 %collective-permute-start.1 = (bf16[128,2048]{1,0:T(8,128)(2,1)S(1)}, bf16[128,2048]{1,0:T(8,128)(2,1)S(1)}, u32[]{:S(2)}, u32[]{:S(2)}) collective-permute-start(bf16[128,2048]{1,0:T(8,128)(2,1)S(1)} %get-tuple-element.140), channel_id=1, source_target_pairs={{0,4},{4,0},{8,12},{12,8},{16,20},{20,16},{24,28},{28,24},{1,5},{5... | collective-permute-start | bytes 1572872 | tf_op jit(solution)/shard_map/ppermute | solution.py:551
  9.1 2.4 %collective-permute-start.4 = (bf16[16,4096]{1,0:T(8,128)(2,1)S(1)}, bf16[16,4096]{1,0:T(8,128)(2,1)S(1)}, u32[]{:S(2)}, u32[]{:S(2)}) collective-permute-start(bf16[16,4096]{1,0:T(8,128)(2,1)S(1)} %get-tuple-element.141), channel_id=1, source_target_pairs={{0,4},{4,8},{8,12},{12,16},{16,20},{20,24},{24,28},{1,5},{5,9},{9,... | collective-permute-start | bytes 393224 | tf_op jit(solution)/shard_map/ppermute | solution.py:590
  14.5 5.1 %collective-permute-done.1.x_ref.g_ref.refs_2_.refs_3_ = bf16[128,2048]{1,0:T(8,128)(2,1)S(1)} collective-permute-done((bf16[128,2048]{1,0:T(8,128)(2,1)S(1)}, bf16[128,2048]{1,0:T(8,128)(2,1)S(1)}, u32[]{:S(2)}, u32[]{:S(2)}) %collective-permute-start.1) | collective-permute-done | bytes 524320 | tf_op jit(solution)/shard_map/ppermute | solution.py:551
  23.4 2.1 %project.1 = (f32[272,256]{1,0:T(8,128)S(1)}, bf16[128,256]{1,0:T(8,128)(2,1)S(1)}) custom-call(bf16[128,4096]{1,0:T(8,128)(2,1)} %bitcast.41, bf16[1024,256]{1,0:T(8,128)(2,1)S(1)} %copy-done.2, bf16[1024,256]{1,0:T(8,128)(2,1)S(1)} %collective-permute-done.2.refs_1_, bf16[1024,256]{1,0:T(8,128)(2,1)S(1)} %collective-permute-done.3.refs_2_, ...), custom_call_target="tpu_custom_call" | custom-call | tf_op jit(solution)/shard_map/project/pallas_call | solution.py:37
  25.5 2.5 %collective-permute-start.6 = (bf16[128,256]{1,0:T(8,128)(2,1)S(1)}, bf16[128,256]{1,0:T(8,128)(2,1)S(1)}, u32[]{:S(2)}, u32[]{:S(2)}) collective-permute-start(bf16[128,256]{1,0:T(8,128)(2,1)S(1)} %get-tuple-element.201.bc_ref.bc0_ref.refs_4_.refs_6_), channel_id=1, source_target_pairs={{0,4},{4,0},{8,12},{12,8},{16,20},{20,16},{24,28},{28,24},{1,5},{5... | collective-permute-start | bytes 196616 | tf_op jit(solution)/shard_map/ppermute | solution.py:551
  28.1 2.2 %inside.4 = (f32[128,1024]{1,0:T(8,128)S(1)}, f32[128,1024]{1,0:T(8,128)S(1)}, f32[128,128]{1,0:T(8,128)S(1)}, f32[128,128]{1,0:T(8,128)S(1)}, f32[128,128]{1,0:T(8,128)S(1)}, /*index=5*/f32[8,128]{1,0:T(8,128)S(1)}) custom-call(f32[32]{0:T(128)S(1)} %copy-done.6, bf16[128,4096]{1,0:T(8,128)(2,1)S(1)} %bitcast.22, bf16[128,4096]{1,0:T(8,128)(2,1)S(1)} %bitcast.29, ...), custom_call_target="tpu_custom_call" | custom-call | tf_op jit(solution)/shard_map/inside/pallas_call | solution.py:37
  30.5 2.5 %collective-permute-start.9 = (bf16[128,1024]{1,0:T(8,128)(2,1)S(1)}, bf16[128,1024]{1,0:T(8,128)(2,1)S(1)}, u32[]{:S(2)}, u32[]{:S(2)}) collective-permute-start(bf16[128,1024]{1,0:T(8,128)(2,1)S(1)} %get-tuple-element.169), channel_id=1, source_target_pairs={{0,4},{4,0},{8,12},{12,8},{16,20},{20,16},{24,28},{28,24},{1,5},{5... | collective-permute-start | bytes 786440 | tf_op jit(solution)/shard_map/ppermute | solution.py:551
  33.8 3.4 %collective-permute-start.7 = (bf16[128,1024]{1,0:T(8,128)(2,1)S(1)}, bf16[128,1024]{1,0:T(8,128)(2,1)S(1)}, u32[]{:S(2)}, u32[]{:S(2)}) collective-permute-start(bf16[128,1024]{1,0:T(8,128)(2,1)S(1)} %get-tuple-element.162), channel_id=1, source_target_pairs={{0,8},{4,12},{24,16},{28,20},{1,9},{5,13},{25,17},{29,21},{2,10},{... | collective-permute-start | bytes 786440 | tf_op jit(solution)/shard_map/ppermute | solution.py:708
  37.1 2.2 %inside.5 = (f32[128,1024]{1,0:T(8,128)S(1)}, f32[128,1024]{1,0:T(8,128)S(1)}, f32[128,128]{1,0:T(8,128)S(1)}, f32[128,128]{1,0:T(8,128)S(1)}, f32[128,128]{1,0:T(8,128)S(1)}, /*index=5*/f32[8,128]{1,0:T(8,128)S(1)}) custom-call(f32[32]{0:T(128)S(1)} %copy-done.6, bf16[128,4096]{1,0:T(8,128)(2,1)S(1)} %bitcast.23, bf16[128,4096]{1,0:T(8,128)(2,1)S(1)} %bitcast.30, ...), custom_call_target="tpu_custom_call" | custom-call | tf_op jit(solution)/shard_map/inside/pallas_call | solution.py:37
  39.4 2.4 %collective-permute-done.9.g_ref.refs_5_ = bf16[128,1024]{1,0:T(8,128)(2,1)S(1)} collective-permute-done((bf16[128,1024]{1,0:T(8,128)(2,1)S(1)}, bf16[128,1024]{1,0:T(8,128)(2,1)S(1)}, u32[]{:S(2)}, u32[]{:S(2)}) %collective-permute-start.9) | collective-permute-done | bytes 262176 | tf_op jit(solution)/shard_map/ppermute | solution.py:551
  43.0 5.0 %collective-permute-start.11 = (bf16[128,1024]{1,0:T(8,128)(2,1)S(1)}, bf16[128,1024]{1,0:T(8,128)(2,1)S(1)}, u32[]{:S(2)}, u32[]{:S(2)}) collective-permute-start(bf16[128,1024]{1,0:T(8,128)(2,1)S(1)} %get-tuple-element.173), channel_id=1, source_target_pairs={{0,8},{4,12},{24,16},{28,20},{1,9},{5,13},{25,17},{29,21},{2,10},{... | collective-permute-start | bytes 786440 | tf_op jit(solution)/shard_map/ppermute | solution.py:708
  48.9 2.3 %inside.6 = (f32[128,1024]{1,0:T(8,128)S(1)}, f32[128,1024]{1,0:T(8,128)S(1)}, f32[128,128]{1,0:T(8,128)S(1)}, f32[128,128]{1,0:T(8,128)S(1)}, f32[128,128]{1,0:T(8,128)S(1)}, /*index=5*/f32[8,128]{1,0:T(8,128)S(1)}) custom-call(f32[32]{0:T(128)S(1)} %copy-done.6, bf16[128,2048]{1,0:T(8,128)(2,1)S(1)} %collective-permute-done.1.x_ref.g_ref.refs_2_.refs_3_, ...), custom_call_target="tpu_custom_call" | custom-call | tf_op jit(solution)/shard_map/inside/pallas_call | solution.py:37
  55.3 2.3 %inside.7 = (f32[128,1024]{1,0:T(8,128)S(1)}, f32[128,1024]{1,0:T(8,128)S(1)}, f32[128,128]{1,0:T(8,128)S(1)}, f32[128,128]{1,0:T(8,128)S(1)}, f32[128,128]{1,0:T(8,128)S(1)}, /*index=5*/f32[8,128]{1,0:T(8,128)S(1)}) custom-call(f32[32]{0:T(128)S(1)} %copy-done.6, bf16[128,1024]{1,0:T(8,128)(2,1)S(1)} %collective-permute-done.8.x_ref.refs_4_, ...), custom_call_target="tpu_custom_call" | custom-call | tf_op jit(solution)/shard_map/inside/pallas_call | solution.py:37
  59.2 7.1 %collective-permute-done.12.refs_2_ = bf16[128,1024]{1,0:T(8,128)(2,1)S(1)} collective-permute-done((bf16[128,1024]{1,0:T(8,128)(2,1)S(1)}, bf16[128,1024]{1,0:T(8,128)(2,1)S(1)}, u32[]{:S(2)}, u32[]{:S(2)}) %collective-permute-start.12) | collective-permute-done | bytes 262176 | tf_op jit(solution)/shard_map/ppermute | solution.py:708
  67.4 2.5 %across.2 = (bf16[128,4096]{1,0:T(8,128)(2,1)}, bf16[128,4096]{1,0:T(8,128)(2,1)}, bf16[128,512]{1,0:T(8,128)(2,1)S(1)}, bf16[128,1536]{1,0:T(8,128)(2,1)S(1)}, ...) custom-call(bf16[128,4096]{1,0:T(8,128)(2,1)S(1)} %bitcast.24, ...), custom_call_target="tpu_custom_call" | custom-call | tf_op jit(solution)/shard_map/across/pallas_call | solution.py:37
  75.3 2.5 %across.3 = (bf16[128,4096]{1,0:T(8,128)(2,1)}, bf16[128,4096]{1,0:T(8,128)(2,1)}, bf16[128,1024]{1,0:T(8,128)(2,1)S(1)}, bf16[128,1024]{1,0:T(8,128)(2,1)S(1)},...) custom-call(bf16[128,4096]{1,0:T(8,128)(2,1)} %get-tuple-element.194, ...), custom_call_target="tpu_custom_call", output_to_operand_aliasing={{0}: (0, {}), {1}: (1, {})} | custom-call | tf_op jit(solution)/shard_map/across/pallas_call | solution.py:37
  81.1 5.0 %collective-permute-done.19.refs_3_ = bf16[128,1536]{1,0:T(8,128)(2,1)S(1)} collective-permute-done((bf16[128,1536]{1,0:T(8,128)(2,1)S(1)}, bf16[128,1536]{1,0:T(8,128)(2,1)S(1)}, u32[]{:S(2)}, u32[]{:S(2)}) %collective-permute-start.19) | collective-permute-done | bytes 393248 | tf_op jit(solution)/shard_map/ppermute | solution.py:551
  87.5 3.5 %all-to-all-start = ((bf16[8,144,256]{2,1,0:T(8,128)(2,1)}), bf16[8,144,256]{2,1,0:T(8,128)(2,1)S(1)}, u32[]{:S(2)}, u32[]{:S(2)}) async-start(bf16[8,144,256]{2,1,0:T(8,128)(2,1)} %weight.1), calls=%async_computation | async-start | bytes 1179648 | tf_op jit(solution)/shard_map/all_to_all | solution.py:555
  94.4 11.4 %collective-permute-done.24.back_ref = f32[16,128]{1,0:T(8,128)S(1)} collective-permute-done((f32[16,128]{1,0:T(8,128)S(1)}, f32[16,128]{1,0:T(8,128)S(1)}, u32[]{:S(2)}, u32[]{:S(2)}) %collective-permute-start.24) | collective-permute-done | bytes 8224 | tf_op jit(solution)/shard_map/ppermute | solution.py:551
  108.2 3.6 %all-to-all-start.1 = ((bf16[8,128,256]{2,1,0:T(8,128)(2,1)}), bf16[8,128,256]{2,1,0:T(8,128)(2,1)S(1)}, u32[]{:S(2)}, u32[]{:S(2)}) async-start(bf16[8,128,256]{2,1,0:T(8,128)(2,1)} %get-tuple-element.250), calls=%async_computation.1 | async-start | bytes 1048576 | tf_op jit(solution)/shard_map/all_to_all | solution.py:555
  111.8 2.0 %collective-permute-start.26 = (bf16[128,1024]{1,0:T(8,128)(2,1)}, bf16[128,1024]{1,0:T(8,128)(2,1)S(1)}, u32[]{:S(2)}, u32[]{:S(2)}) collective-permute-start(bf16[128,1024]{1,0:T(8,128)(2,1)} %copy-done.10), channel_id=1, source_target_pairs={{0,4},{4,0},{8,12},{12,8},{16,20},{20,16},{24,28},{28,24},{1,5},{5... | collective-permute-start | bytes 786440 | tf_op jit(solution)/shard_map/ppermute | solution.py:551
  115.3 2.4 %grad_tokens.1 = bf16[128,4096]{1,0:T(8,128)(2,1)} custom-call(bf16[1024,256]{1,0:T(8,128)(2,1)S(1)} %copy-done.2, bf16[1024,256]{1,0:T(8,128)(2,1)S(1)} %collective-permute-done.2.refs_1_, bf16[1024,256]{1,0:T(8,128)(2,1)S(1)} %collective-permute-done.3.refs_2_, bf16[1024,256]{1,0:T(8,128)(2,1)S(1)} %collective-permute-done.5.refs_3_, ...), custom_call_target="tpu_custom_call" | custom-call | tf_op jit(solution)/shard_map/grad_tokens/pallas_call | solution.py:37
  118.7 6.9 %collective-permute-done.26.refs_2_ = bf16[128,1024]{1,0:T(8,128)(2,1)S(1)} collective-permute-done((bf16[128,1024]{1,0:T(8,128)(2,1)}, bf16[128,1024]{1,0:T(8,128)(2,1)S(1)}, u32[]{:S(2)}, u32[]{:S(2)}) %collective-permute-start.26) | collective-permute-done | bytes 262176 | tf_op jit(solution)/shard_map/ppermute | solution.py:551
  (93 shorter events, 39.9 us)
Async XLA Ops:
  3.6 9.2 %collective-permute-start.2 = (bf16[1024,256]{1,0:T(8,128)(2,1)}, bf16[1024,256]{1,0:T(8,128)(2,1)S(1)}, u32[]{:S(2)}, u32[]{:S(2)}) collective-permute-start(bf16[1024,256]{1,0:T(8,128)(2,1)} %refs_0_.5), channel_id=1, source_target_pairs={{0,1},{1,0},{2,3},{3,2},{4,5},{5,4},{6,7},{7,6},{8,9},{9,8},{10,11... | collective-permute-start | bytes 1572872 | tf_op jit(solution)/shard_map/ppermute | solution.py:551
  5.6 14.0 %collective-permute-start.1 = (bf16[128,2048]{1,0:T(8,128)(2,1)S(1)}, bf16[128,2048]{1,0:T(8,128)(2,1)S(1)}, u32[]{:S(2)}, u32[]{:S(2)}) collective-permute-start(bf16[128,2048]{1,0:T(8,128)(2,1)S(1)} %get-tuple-element.140), channel_id=1, source_target_pairs={{0,4},{4,0},{8,12},{12,8},{16,20},{20,16},{24,28},{28,24},{1,5},{5... | collective-permute-start | bytes 1572872 | tf_op jit(solution)/shard_map/ppermute | solution.py:551
  7.6 12.8 %collective-permute-start.3 = (bf16[1024,256]{1,0:T(8,128)(2,1)S(1)}, bf16[1024,256]{1,0:T(8,128)(2,1)S(1)}, u32[]{:S(2)}, u32[]{:S(2)}) collective-permute-start(bf16[1024,256]{1,0:T(8,128)(2,1)S(1)} %copy-done.2), channel_id=1, source_target_pairs={{0,2},{1,3},{2,0},{3,1},{4,6},{5,7},{6,4},{7,5},{8,10},{9,11},{10,... | collective-permute-start | bytes 1572872 | tf_op jit(solution)/shard_map/ppermute | solution.py:551
  9.1 11.3 %collective-permute-start.4 = (bf16[16,4096]{1,0:T(8,128)(2,1)S(1)}, bf16[16,4096]{1,0:T(8,128)(2,1)S(1)}, u32[]{:S(2)}, u32[]{:S(2)}) collective-permute-start(bf16[16,4096]{1,0:T(8,128)(2,1)S(1)} %get-tuple-element.141), channel_id=1, source_target_pairs={{0,4},{4,8},{8,12},{12,16},{16,20},{20,24},{24,28},{1,5},{5,9},{9,... | collective-permute-start | bytes 393224 | tf_op jit(solution)/shard_map/ppermute | solution.py:590
  21.7 27.1 %collective-permute-start.14 = (bf16[2,144,1024]{2,1,0:T(8,128)(2,1)S(1)}, bf16[2,144,1024]{2,1,0:T(8,128)(2,1)S(1)}, u32[]{:S(2)}, u32[]{:S(2)}) collective-permute-start(bf16[2,144,1024]{2,1,0:T(8,128)(2,1)S(1)} %get-tuple-element.199), channel_id=1, source_target_pairs={{0,2},{1,3},{2,0},{3,1},{4,6},{5,7},{6,4},{7,5},{8,10},{9,11},{10,... | collective-permute-start | bytes 1769480 | tf_op jit(solution)/shard_map/ppermute | solution.py:551
  28.0 11.3 %collective-permute-start.8 = (bf16[128,1024]{1,0:T(8,128)(2,1)S(1)}, bf16[128,1024]{1,0:T(8,128)(2,1)S(1)}, u32[]{:S(2)}, u32[]{:S(2)}) collective-permute-start(bf16[128,1024]{1,0:T(8,128)(2,1)S(1)} %get-tuple-element.167), channel_id=1, source_target_pairs={{0,4},{4,0},{8,12},{12,8},{16,20},{20,16},{24,28},{28,24},{1,5},{5... | collective-permute-start | bytes 786440 | tf_op jit(solution)/shard_map/ppermute | solution.py:551
  30.5 11.3 %collective-permute-start.9 = (bf16[128,1024]{1,0:T(8,128)(2,1)S(1)}, bf16[128,1024]{1,0:T(8,128)(2,1)S(1)}, u32[]{:S(2)}, u32[]{:S(2)}) collective-permute-start(bf16[128,1024]{1,0:T(8,128)(2,1)S(1)} %get-tuple-element.169), channel_id=1, source_target_pairs={{0,4},{4,0},{8,12},{12,8},{16,20},{20,16},{24,28},{28,24},{1,5},{5... | collective-permute-start | bytes 786440 | tf_op jit(solution)/shard_map/ppermute | solution.py:551
  33.8 14.2 %collective-permute-start.7 = (bf16[128,1024]{1,0:T(8,128)(2,1)S(1)}, bf16[128,1024]{1,0:T(8,128)(2,1)S(1)}, u32[]{:S(2)}, u32[]{:S(2)}) collective-permute-start(bf16[128,1024]{1,0:T(8,128)(2,1)S(1)} %get-tuple-element.162), channel_id=1, source_target_pairs={{0,8},{4,12},{24,16},{28,20},{1,9},{5,13},{25,17},{29,21},{2,10},{... | collective-permute-start | bytes 786440 | tf_op jit(solution)/shard_map/ppermute | solution.py:708
  43.0 10.1 %collective-permute-start.11 = (bf16[128,1024]{1,0:T(8,128)(2,1)S(1)}, bf16[128,1024]{1,0:T(8,128)(2,1)S(1)}, u32[]{:S(2)}, u32[]{:S(2)}) collective-permute-start(bf16[128,1024]{1,0:T(8,128)(2,1)S(1)} %get-tuple-element.173), channel_id=1, source_target_pairs={{0,8},{4,12},{24,16},{28,20},{1,9},{5,13},{25,17},{29,21},{2,10},{... | collective-permute-start | bytes 786440 | tf_op jit(solution)/shard_map/ppermute | solution.py:708
  48.1 5.7 %collective-permute-start.10 = (bf16[128,1024]{1,0:T(8,128)(2,1)S(1)}, bf16[128,1024]{1,0:T(8,128)(2,1)S(1)}, u32[]{:S(2)}, u32[]{:S(2)}) collective-permute-start(bf16[128,1024]{1,0:T(8,128)(2,1)S(1)} %hop.4), channel_id=1, source_target_pairs={{8,16},{12,20},{16,8},{20,12},{9,17},{13,21},{17,9},{21,13},{10,18... | collective-permute-start | bytes 786440 | tf_op jit(solution)/shard_map/ppermute | solution.py:708
  48.9 26.1 %collective-permute-start.15 = (bf16[2,144,1024]{2,1,0:T(8,128)(2,1)S(1)}, bf16[2,144,1024]{2,1,0:T(8,128)(2,1)S(1)}, u32[]{:S(2)}, u32[]{:S(2)}) collective-permute-start(bf16[2,144,1024]{2,1,0:T(8,128)(2,1)S(1)} %relay.1), channel_id=1, source_target_pairs={{0,1},{1,0},{2,3},{3,2},{4,5},{5,4},{6,7},{7,6},{8,9},{9,8},{10,11... | collective-permute-start | bytes 1769480 | tf_op jit(solution)/shard_map/ppermute | solution.py:551
  54.0 12.3 %collective-permute-start.12 = (bf16[128,1024]{1,0:T(8,128)(2,1)S(1)}, bf16[128,1024]{1,0:T(8,128)(2,1)S(1)}, u32[]{:S(2)}, u32[]{:S(2)}) collective-permute-start(bf16[128,1024]{1,0:T(8,128)(2,1)S(1)} %hop.6), channel_id=1, source_target_pairs={{16,24},{20,28},{8,0},{12,4},{17,25},{21,29},{9,1},{13,5},{18,26},... | collective-permute-start | bytes 786440 | tf_op jit(solution)/shard_map/ppermute | solution.py:708
  57.7 13.1 %collective-permute-start.17 = (bf16[128,1024]{1,0:T(8,128)(2,1)S(1)}, bf16[128,1024]{1,0:T(8,128)(2,1)S(1)}, u32[]{:S(2)}, u32[]{:S(2)}) collective-permute-start(bf16[128,1024]{1,0:T(8,128)(2,1)S(1)} %hop.7), channel_id=1, source_target_pairs={{16,24},{20,28},{8,0},{12,4},{17,25},{21,29},{9,1},{13,5},{18,26},... | collective-permute-start | bytes 786440 | tf_op jit(solution)/shard_map/ppermute | solution.py:708
  71.6 6.6 %collective-permute-start.18 = (bf16[128,256]{1,0:T(8,128)(2,1)S(1)}, bf16[128,256]{1,0:T(8,128)(2,1)S(1)}, u32[]{:S(2)}, u32[]{:S(2)}) collective-permute-start(bf16[128,256]{1,0:T(8,128)(2,1)S(1)} %get-tuple-element.219), channel_id=1, source_target_pairs={{0,4},{4,0},{8,12},{12,8},{16,20},{20,16},{24,28},{28,24},{1,5},{5... | collective-permute-start | bytes 196616 | tf_op jit(solution)/shard_map/ppermute | solution.py:551
  78.2 7.8 %collective-permute-start.19 = (bf16[128,1536]{1,0:T(8,128)(2,1)S(1)}, bf16[128,1536]{1,0:T(8,128)(2,1)S(1)}, u32[]{:S(2)}, u32[]{:S(2)}) collective-permute-start(bf16[128,1536]{1,0:T(8,128)(2,1)S(1)} %get-tuple-element.243), channel_id=1, source_target_pairs={{0,4},{4,0},{8,12},{12,8},{16,20},{20,16},{24,28},{28,24},{1,5},{5... | collective-permute-start | bytes 1179656 | tf_op jit(solution)/shard_map/ppermute | solution.py:551
  79.1 6.9 %collective-permute-start.20 = (bf16[160,256]{1,0:T(8,128)(2,1)S(1)}, bf16[160,256]{1,0:T(8,128)(2,1)S(1)}, u32[]{:S(2)}, u32[]{:S(2)}) collective-permute-start(bf16[160,256]{1,0:T(8,128)(2,1)S(1)} %get-tuple-element.244.refs_0_), channel_id=1, source_target_pairs={{0,1},{1,0},{2,3},{3,2},{4,5},{5,4},{6,7},{7,6},{8,9},{9,8},{10,11... | collective-permute-start | bytes 245768 | tf_op jit(solution)/shard_map/ppermute | solution.py:551
  79.2 6.9 %collective-permute-start.21 = (bf16[160,256]{1,0:T(8,128)(2,1)S(1)}, bf16[160,256]{1,0:T(8,128)(2,1)S(1)}, u32[]{:S(2)}, u32[]{:S(2)}) collective-permute-start(bf16[160,256]{1,0:T(8,128)(2,1)S(1)} %get-tuple-element.244.refs_0_), channel_id=1, source_target_pairs={{0,2},{1,3},{2,0},{3,1},{4,6},{5,7},{6,4},{7,5},{8,10},{9,11},{10,... | collective-permute-start | bytes 245768 | tf_op jit(solution)/shard_map/ppermute | solution.py:551
  79.8 6.3 %collective-permute-start.22 = (bf16[160,256]{1,0:T(8,128)(2,1)S(1)}, bf16[160,256]{1,0:T(8,128)(2,1)S(1)}, u32[]{:S(2)}, u32[]{:S(2)}) collective-permute-start(bf16[160,256]{1,0:T(8,128)(2,1)S(1)} %get-tuple-element.244.refs_0_), channel_id=1, source_target_pairs={{0,3},{1,2},{2,1},{3,0},{4,7},{5,6},{6,5},{7,4},{8,11},{9,10},{10,... | collective-permute-start | bytes 245768 | tf_op jit(solution)/shard_map/ppermute | solution.py:551
  87.5 19.7 %all-to-all-start = ((bf16[8,144,256]{2,1,0:T(8,128)(2,1)}), bf16[8,144,256]{2,1,0:T(8,128)(2,1)S(1)}, u32[]{:S(2)}, u32[]{:S(2)}) async-start(bf16[8,144,256]{2,1,0:T(8,128)(2,1)} %weight.1), calls=%async_computation | async-start | bytes 1179648 | tf_op jit(solution)/shard_map/all_to_all | solution.py:555
  91.1 14.8 %collective-permute-start.25 = (bf16[128,1024]{1,0:T(8,128)(2,1)}, bf16[128,1024]{1,0:T(8,128)(2,1)S(1)}, u32[]{:S(2)}, u32[]{:S(2)}) collective-permute-start(bf16[128,1024]{1,0:T(8,128)(2,1)} %copy-done.11), channel_id=1, source_target_pairs={{0,4},{4,0},{8,12},{12,8},{16,20},{20,16},{24,28},{28,24},{1,5},{5... | collective-permute-start | bytes 786440 | tf_op jit(solution)/shard_map/ppermute | solution.py:551
  93.0 12.8 %collective-permute-start.24 = (f32[16,128]{1,0:T(8,128)S(1)}, f32[16,128]{1,0:T(8,128)S(1)}, u32[]{:S(2)}, u32[]{:S(2)}) collective-permute-start(f32[16,128]{1,0:T(8,128)S(1)} %get-tuple-element.246), channel_id=1, source_target_pairs={{0,4},{4,0},{8,12},{12,8},{16,20},{20,16},{24,28},{28,24},{1,5},{5... | collective-permute-start | bytes 24584 | tf_op jit(solution)/shard_map/ppermute | solution.py:551
  93.2 12.7 %collective-permute-start.23 = (f32[8,256]{1,0:T(8,128)S(1)}, f32[8,256]{1,0:T(8,128)S(1)}, u32[]{:S(2)}, u32[]{:S(2)}) collective-permute-start(f32[8,256]{1,0:T(8,128)S(1)} %get-tuple-element.245), channel_id=1, source_target_pairs={{4,0},{8,4},{12,8},{16,12},{20,16},{24,20},{28,24},{5,1},{9,5},{13... | collective-permute-start | bytes 24584 | tf_op jit(solution)/shard_map/ppermute | solution.py:797
  108.2 18.2 %all-to-all-start.1 = ((bf16[8,128,256]{2,1,0:T(8,128)(2,1)}), bf16[8,128,256]{2,1,0:T(8,128)(2,1)S(1)}, u32[]{:S(2)}, u32[]{:S(2)}) async-start(bf16[8,128,256]{2,1,0:T(8,128)(2,1)} %get-tuple-element.250), calls=%async_computation.1 | async-start | bytes 1048576 | tf_op jit(solution)/shard_map/all_to_all | solution.py:555
  111.8 13.8 %collective-permute-start.26 = (bf16[128,1024]{1,0:T(8,128)(2,1)}, bf16[128,1024]{1,0:T(8,128)(2,1)S(1)}, u32[]{:S(2)}, u32[]{:S(2)}) collective-permute-start(bf16[128,1024]{1,0:T(8,128)(2,1)} %copy-done.10), channel_id=1, source_target_pairs={{0,4},{4,0},{8,12},{12,8},{16,20},{20,16},{24,28},{28,24},{1,5},{5... | collective-permute-start | bytes 786440 | tf_op jit(solution)/shard_map/ppermute | solution.py:551
  (17 other events, 106.6 us)
